TPU v7x, 32 devices: a whole 2x2x4 slice. The times are simulated.
32 devices in a mesh: seq: 8 (over z, x), head: 4 (over y, core).
Axes of the slice: x: 2, y: 2, z: 4, core: 2. Of those that a mesh axis runs over, the one named last changes fastest.
Arguments:
- qkv_pre: bfloat16 [4096, 3, 16, 128], P(('seq', 'head')), may hold values from -10 to 10
- grad_out: bfloat16 [4096, 2048], P(('seq', 'head')), may hold values from -48 to 48
- out_values: bfloat16 [2048, 2048], P('head'), may hold values from -4 to 4
- out_scales: float32 [16, 16], replicated, may hold values from 0.01 to 0.04
- conv_kernel: float32 [31, 3, 16, 128], P(None, None, 'head'), may hold values from -1 to 1
- window: int32 [16], replicated, may hold values from 64 to 96, as said below
- offsets: int32 [8], replicated, may hold values from 0 to 32, as said below
Outputs:
- grad_pre: bfloat16 [4096, 3, 16, 128], P(('seq', 'head'))
Inputs may be any that keep to these rules, and one draw needn't show every extreme that they name: window[h] + offsets[b] <= 128 for every head h and block b; some head has window exactly 96. offsets[b] <= 32 for every block b, with equality in at least one block.
All inputs are finite; a program needn't handle non-finite values.
Results may differ from a plain program's by a relative error of at most 0.005.
The roundings to bfloat16 on the way count: a program that leaves them out, or rounds other values in their place, can miss the bound.
Values may be sent and summed in bfloat16 or wider, within the bound.
No kernel may reach another device: no remote copies, remote signals or barrier semaphores. Data moves between devices by JAX's collectives and lax.ppermute only.
A program may use at most 64 MiB of HBM per device.

v0:
```python
import math

import jax
import jax.numpy as jnp
from jax import lax
from jax.sharding import PartitionSpec as P

KW = 31
MASKB = 512


def shifted(value, axis, by):
    length = lax.axis_size(axis)
    pairs = [(i, i + by) for i in range(length) if 0 <= i + by < length]
    return lax.ppermute(value, axis, pairs)


def causal_conv(series, kernel):
    length = series.shape[0]
    padded = jnp.concatenate(
        [jnp.zeros((KW - 1,) + series.shape[1:], series.dtype), series], axis=0
    )
    summed = jnp.zeros(series.shape, jnp.float32)
    for kernel_tap in range(KW):
        first_row = KW - 1 - kernel_tap
        summed = summed + kernel[kernel_tap] * padded[first_row : first_row + length].astype(
            jnp.float32
        )
    return summed


def transposed_conv(grads, kernel):
    length = grads.shape[0]
    padded = jnp.concatenate([grads, jnp.zeros((KW - 1,) + grads.shape[1:], jnp.float32)], axis=0)
    summed = jnp.zeros(grads.shape, jnp.float32)
    for kernel_tap in range(KW):
        summed = summed + kernel[kernel_tap] * padded[kernel_tap : kernel_tap + length]
    return summed


def dequantize(values, start, out_scales):
    row_count = values.shape[0]
    full_width = values.shape[1]
    block_count = out_scales.shape[0]
    block_size = full_width // out_scales.shape[1]
    column_scales = jnp.repeat(out_scales, block_size, axis=1)
    row_block = (start + lax.iota(jnp.int32, row_count)) // block_size
    picker = (row_block[:, None] == lax.iota(jnp.int32, block_count)[None, :]).astype(jnp.float32)
    scales = jnp.dot(picker, column_scales, precision=lax.Precision.HIGHEST)
    return (values.astype(jnp.float32) * scales).astype(jnp.bfloat16)


def per_device(qkv_pre, grad_out, out_values, out_scales, conv_kernel, window, offsets):
    tok_rows = qkv_pre.shape[0]
    head_count = qkv_pre.shape[2]
    head_dim = qkv_pre.shape[3]
    n_head = lax.axis_size("head")
    local_heads = head_count // n_head
    seq_rows = tok_rows * n_head
    span = seq_rows // 4
    margin = MASKB // 4
    prior = span + margin
    ext_rows = prior + seq_rows
    seq_index = lax.axis_index("seq")
    head_index = lax.axis_index("head")
    inv_scale = 1.0 / math.sqrt(head_dim)
    local_window = lax.dynamic_slice_in_dim(window, head_index * local_heads, local_heads, 0)
    weight = dequantize(out_values, head_index * out_values.shape[0], out_scales)
    grad_heads = lax.dot_general(
        lax.all_gather(grad_out, "head", axis=0, tiled=True),
        weight,
        (((1,), (1,)), ((), ())),
        preferred_element_type=jnp.float32,
    ).astype(jnp.bfloat16)
    grad_heads = grad_heads.reshape(seq_rows, local_heads, head_dim)
    mixed_in = lax.all_to_all(qkv_pre, "head", split_axis=2, concat_axis=0, tiled=True)
    tail_rows = mixed_in[seq_rows - prior :]
    before = shifted(tail_rows, "seq", 1)
    extended = jnp.concatenate([before, mixed_in], axis=0)
    mixed_rows = causal_conv(extended, conv_kernel).astype(jnp.bfloat16)
    query_rows = mixed_rows[prior:, 0]
    key_rows = mixed_rows[:, 1]
    value_rows = mixed_rows[:, 2]
    n_blocks = seq_rows // MASKB
    key_len = span + MASKB
    reach_base = seq_index * n_blocks

    def attend(block_index, totals):
        grad_q, grad_k, grad_v = totals
        q_start = block_index * MASKB
        k_start = margin + q_start
        q_block = lax.dynamic_slice_in_dim(query_rows, q_start, MASKB, 0)
        o_block = lax.dynamic_slice_in_dim(grad_heads, q_start, MASKB, 0)
        k_block = lax.dynamic_slice_in_dim(key_rows, k_start, key_len, 0)
        v_block = lax.dynamic_slice_in_dim(value_rows, k_start, key_len, 0)
        scores = (
            jnp.einsum("qhe,khe->hqk", q_block, k_block, preferred_element_type=jnp.float32)
            * inv_scale
        )
        query_pos = seq_index * seq_rows + q_start + lax.iota(jnp.int32, MASKB)
        key_pos = seq_index * seq_rows - prior + k_start + lax.iota(jnp.int32, key_len)
        distance = query_pos[:, None] - key_pos[None, :]
        reach_now = local_window + lax.dynamic_index_in_dim(
            offsets, reach_base + block_index, 0, keepdims=False
        )
        allowed = ((distance >= 0) & (key_pos[None, :] >= 0))[None] & (
            distance[None] <= reach_now[:, None, None]
        )
        row_top = jnp.max(jnp.where(allowed, scores, -1e30), axis=2, keepdims=True)
        exp_scores = jnp.where(allowed, jnp.exp(scores - row_top), 0.0)
        probs = exp_scores / jnp.sum(exp_scores, axis=2, keepdims=True)
        probs_b = probs.astype(jnp.bfloat16)
        d_prob = jnp.einsum("qhe,khe->hqk", o_block, v_block, preferred_element_type=jnp.float32)
        row_delta = jnp.sum(probs * d_prob, axis=2, keepdims=True)
        d_score = (probs * (d_prob - row_delta) * inv_scale).astype(jnp.bfloat16)
        grad_q_block = jnp.einsum(
            "hqk,khe->qhe", d_score, k_block, preferred_element_type=jnp.float32
        )
        grad_k_block = jnp.einsum(
            "hqk,qhe->khe", d_score, q_block, preferred_element_type=jnp.float32
        )
        grad_v_block = jnp.einsum(
            "hqk,qhe->khe", probs_b, o_block, preferred_element_type=jnp.float32
        )
        grad_q = lax.dynamic_update_slice_in_dim(grad_q, grad_q_block, q_start, 0)
        grad_k = lax.dynamic_update_slice_in_dim(
            grad_k, lax.dynamic_slice_in_dim(grad_k, k_start, key_len, 0) + grad_k_block, k_start, 0
        )
        grad_v = lax.dynamic_update_slice_in_dim(
            grad_v, lax.dynamic_slice_in_dim(grad_v, k_start, key_len, 0) + grad_v_block, k_start, 0
        )
        return (grad_q, grad_k, grad_v)

    start_totals = (
        jnp.zeros((seq_rows, local_heads, head_dim), jnp.float32),
        jnp.zeros((ext_rows, local_heads, head_dim), jnp.float32),
        jnp.zeros((ext_rows, local_heads, head_dim), jnp.float32),
    )
    grad_q, grad_k, grad_v = lax.fori_loop(0, n_blocks, attend, start_totals)
    grad_q_ext = jnp.concatenate(
        [jnp.zeros((prior, local_heads, head_dim), jnp.float32), grad_q], axis=0
    )
    grads = jnp.stack([grad_q_ext, grad_k, grad_v], axis=1)
    spread = transposed_conv(grads, conv_kernel)
    returned = shifted(spread[:prior].astype(jnp.bfloat16), "seq", -1)
    own_rows = spread[prior:]
    tail_sum = own_rows[seq_rows - prior :] + returned.astype(jnp.float32)
    result = jnp.concatenate([own_rows[: seq_rows - prior], tail_sum], axis=0).astype(jnp.bfloat16)
    return lax.all_to_all(result, "head", split_axis=0, concat_axis=2, tiled=True)


def solution(mesh):
    return jax.shard_map(
        per_device,
        mesh=mesh,
        in_specs=(
            P(("seq", "head"), None, None, None),
            P(("seq", "head"), None),
            P("head", None),
            P(),
            P(None, None, "head", None),
            P(),
            P(),
        ),
        out_specs=P(("seq", "head"), None, None, None),
        check_vma=False,
    )
```

profile of v0, /device:TPU:0, one launch (start us, length us, event | category | flops | bytes accessed | tf_op | source)
XLA Modules:
  0.0 214.1 jit_solution(17763769929687273269)
XLA Ops:
  6.5 3.0 %copy.26 = bf16[128,3,16,128]{3,0,1,2:T(8,128)(2,1)} copy(bf16[128,3,16,128]{3,2,1,0:T(8,128)(2,1)} %param.7) | data formatting | bytes 3145728 | tf_op args[0]
  9.5 4.4 %all-to-all-start = ((bf16[128,3,16,128]{3,0,1,2:T(8,128)(2,1)}), bf16[128,3,16,128]{3,0,1,2:T(8,128)(2,1)S(1)}, u32[]{:S(2)}, u32[]{:S(2)}) async-start(bf16[128,3,16,128]{3,0,1,2:T(8,128)(2,1)} %copy.26), calls=%async_computation | async-start | bytes 3145728 | tf_op jit(solution)/shard_map/all_to_all | solution.py:76
  13.9 0.7 all-gather.2.cloned.1.call-update
  14.7 0.7 dynamic_slice.31
  15.3 0.7 dynamic-slice_add_fusion
  16.3 1.1 compare_and_fusion.2
  17.4 22.6 %all-to-all-done = bf16[128,3,16,128]{3,0,1,2:T(8,128)(2,1)S(1)} async-done(((bf16[128,3,16,128]{3,0,1,2:T(8,128)(2,1)}), bf16[128,3,16,128]{3,0,1,2:T(8,128)(2,1)S(1)}, u32[]{:S(2)}, u32[]{:S(2)}) %all-to-all-start) | async-done | bytes 1572896 | tf_op jit(solution)/shard_map/all_to_all | solution.py:76
  40.0 0.2 copy.49
  40.2 4.9 %collective-permute-start = (bf16[256,3,4,128]{3,0,2,1:T(8,128)(2,1)S(1)}, bf16[256,3,4,128]{3,0,2,1:T(8,128)(2,1)S(1)}, u32[]{:S(2)}, u32[]{:S(2)}) collective-permute-start(bf16[256,3,4,128]{3,0,2,1:T(8,128)(2,1)S(1)} %bitcast.129), channel_id=1, source_target_pairs={{0,4},{4,8},{8,12},{12,16},{16,20},{20,24},{24,28},{1,5},{5,9},{9,... | collective-permute-start | bytes 2359304 | tf_op jit(solution)/shard_map/ppermute | solution.py:15
  45.2 1.3 broadcast_subtract_fusion
  46.6 3.3 %multiply_convert_fusion.1 = bf16[512,2048]{1,0:T(8,128)(2,1)} fusion(bf16[512,2048]{1,0:T(8,128)(2,1)S(1)} %copy-done.2, f32[2,8,16,128]{3,2,1,0:T(8,128)S(1)} %bitcast.132, s32[512]{0:T(512)S(1)} %add_select_fusion), kind=kOutput, calls=%fused_computation.16 | convolution fusion | flops 204480512 | bytes 4327424 | tf_op jit(solution)/shard_map/dot_general | solution.py:49
  49.9 11.0 %collective-permute-done = bf16[256,3,4,128]{3,0,2,1:T(8,128)(2,1)S(1)} collective-permute-done((bf16[256,3,4,128]{3,0,2,1:T(8,128)(2,1)S(1)}, bf16[256,3,4,128]{3,0,2,1:T(8,128)(2,1)S(1)}, u32[]{:S(2)}, u32[]{:S(2)}) %collective-permute-start) | collective-permute-done | bytes 786464 | tf_op jit(solution)/shard_map/ppermute | solution.py:15
  60.9 0.9 pad_maximum_fusion.1
  61.9 20.5 %add_convert_fusion = bf16[768,3,4,128]{3,0,2,1:T(8,128)(2,1)} fusion(bf16[798,3,4,128]{3,0,2,1:T(8,128)(2,1)S(1)} %pad_maximum_fusion.1, bf16[512,3,4,128]{3,0,2,1:T(8,128)(2,1)} %bitcast.126, bf16[256,3,4,128]{3,0,2,1:T(8,128)(2,1)S(1)} %collective-permute-done, f32[3,4,128]{2,1,0:T(4,128)S(1)} %get-tuple-element.76, ...), kind=kLoop, calls=%fused_computation.15 | loop fusion | flops 113246208 | bytes 75687936 | tf_op jit(solution)/shard_map/convert_element_type | solution.py:80
  82.4 9.2 %fusion.54 = (f32[4,512]{1,0:T(4,128)}, f32[4,512,640]{2,1,0:T(8,128)}) fusion(s32[512,640]{1,0:T(8,128)} %broadcast_subtract_fusion, s32[4]{0:T(128)S(1)} %dynamic-slice_add_fusion, pred[512,640]{1,0:T(8,128)(4,1)} %compare_and_fusion.2, bf16[768,3,4,128]{3,0,2,1:T(8,128)(2,1)} %add_convert_fusion), kind=kOutput, calls=%fused_computation.105 | convolution fusion | flops 684196480 | bytes 10888192 | tf_op jit(solution)/shard_map/while/body/eval_jaxpr/sub | solution.py:110
  91.6 3.6 %convolution_convert_fusion = bf16[512,512]{1,0:T(8,128)(2,1)S(1)} fusion(bf16[512,2048]{1,0:T(8,128)(2,1)} %multiply_convert_fusion.1, bf16[512,2048]{1,0:T(8,128)(2,1)} %all-gather.2.cloned.1.call-done), kind=kOutput, calls=%fused_computation.40 | convolution fusion | flops 1074003968 | bytes 4718592 | tf_op jit(solution)/shard_map/dot_general | solution.py:69
  95.3 3.3 %fusion.38 = f32[4,512,640]{2,1,0:T(8,128)} fusion(bf16[512,4,128]{0,2,1:T(8,128)(2,1)S(1)} %bitcast.130, bf16[768,3,4,128]{3,0,2,1:T(8,128)(2,1)S(1)} %copy-done.1), kind=kOutput, calls=%fused_computation.43 | convolution fusion | flops 335544320 | bytes 6422528 | tf_op jit(solution)/shard_map/while/body/eval_jaxpr/qhe,khe->hqk/dot_general | solution.py:113
  98.6 17.9 %fusion.33 = f32[512,4,128]{2,0,1:T(8,128)S(1)} fusion(f32[4,512,640]{2,1,0:T(8,128)} %fusion.38, bf16[768,3,4,128]{3,0,2,1:T(8,128)(2,1)S(1)} %copy-done.1, f32[4,512,640]{2,1,0:T(8,128)} %get-tuple-element.79, f32[4,512]{1,0:T(4,128)} %get-tuple-element.78), kind=kOutput, calls=%fused_computation.38 | convolution fusion | flops 344722048 | bytes 22691840 | tf_op jit(solution)/shard_map/while/body/eval_jaxpr/hqk,khe->qhe/dot_general | solution.py:116
  116.5 20.8 %fusion.30 = f32[640,4,128]{2,0,1:T(8,128)} fusion(f32[4,512,640]{2,1,0:T(8,128)} %fusion.38, bf16[768,3,4,128]{3,0,2,1:T(8,128)(2,1)S(1)} %copy-done.1, f32[4,512,640]{2,1,0:T(8,128)} %get-tuple-element.79, f32[4,512]{1,0:T(4,128)} %get-tuple-element.78), kind=kOutput, calls=%fused_computation.37 | convolution fusion | flops 344722048 | bytes 22822912 | tf_op jit(solution)/shard_map/while/body/eval_jaxpr/hqk,qhe->khe/dot_general | solution.py:119
  137.2 4.1 %fusion.27 = f32[640,4,128]{2,0,1:T(8,128)S(1)} fusion(bf16[512,4,128]{0,2,1:T(8,128)(2,1)} %bitcast.131, f32[4,512,640]{2,1,0:T(8,128)} %get-tuple-element.79, f32[4,512]{1,0:T(4,128)} %get-tuple-element.78), kind=kOutput, calls=%fused_computation.36 | convolution fusion | flops 338165760 | bytes 7086080 | tf_op jit(solution)/shard_map/while/body/eval_jaxpr/hqk,qhe->khe/dot_general | solution.py:122
  141.5 0.2 pad_bitcast_fusion
  141.8 0.3 pad_maximum_fusion
  142.2 0.2 copy-done.7
  142.6 18.6 %fusion.52 = (bf16[768,3,4,128]{3,0,2,1:T(8,128)(2,1)S(1)}, f32[768,3,4,128]{3,0,2,1:T(8,128)S(1)}) fusion(f32[3,4,128]{2,1,0:T(4,128)S(1)} %get-tuple-element.76, f32[3,4,128]{2,1,0:T(4,128)S(1)} %get-tuple-element.77, f32[3,4,128]{2,1,0:T(4,128)S(1)} %get-tuple-element.34, f32[3,4,128]{2,1,0:T(4,128)S(1)} %get-tuple-element.35, ...), kind=kLoop, calls=%fused_computation.103 | loop fusion | flops 73138176 | bytes 11986944 | tf_op jit(solution)/shard_map/convert.2
  161.2 0.1 fusion.53
  161.4 1.3 collective-permute-start.1
  162.7 18.7 %collective-permute-done.1 = bf16[256,3,4,128]{3,0,2,1:T(8,128)(2,1)S(1)} collective-permute-done((bf16[256,3,4,128]{3,0,2,1:T(8,128)(2,1)S(1)}, bf16[256,3,4,128]{3,0,2,1:T(8,128)(2,1)S(1)}, u32[]{:S(2)}, u32[]{:S(2)}) %collective-permute-start.1) | collective-permute-done | bytes 786464 | tf_op jit(solution)/shard_map/ppermute | solution.py:15
  181.4 0.2 fusion.26
  181.6 0.1 pad_maximum_fusion.2
  181.7 1.2 copy.34
  182.9 22.7 %all_to_all.36 = bf16[512,3,4,128]{3,2,1,0:T(4,128)(2,1)S(1)} all-to-all(bf16[512,3,4,128]{3,2,1,0:T(4,128)(2,1)S(1)} %copy.34), channel_id=1, replica_groups=mesh['seq'=8,'head'=4] {'head'}, dimensions={0} | all-to-all | bytes 3145728 | tf_op jit(solution)/shard_map/all_to_all | solution.py:149
  205.6 1.7 copy.35
  (82 shorter events, 0.6 us)
Async XLA Ops:
  6.5 8.1 %copy-start.34 = (s32[8]{0:T(128)S(1)}, s32[8]{0:T(128)}, u32[]{:S(2)}) copy-start(s32[8]{0:T(128)} %param.13) | copy-start | bytes 100
  6.5 8.8 %copy-start.33 = (s32[16]{0:T(128)S(1)}, s32[16]{0:T(128)}, u32[]{:S(2)}) copy-start(s32[16]{0:T(128)} %param.12) | copy-start | bytes 196
  6.5 9.6 %copy-start.5 = (f32[31,3,4,128]{3,2,1,0:T(4,128)S(1)}, f32[31,3,4,128]{3,2,1,0:T(4,128)}, u32[]{:S(2)}) copy-start(f32[31,3,4,128]{3,2,1,0:T(4,128)} %param.11) | copy-start | bytes 571396
  9.5 36.9 %copy-start.32 = (f32[16,16]{1,0:T(8,128)S(1)}, f32[16,16]{1,0:T(8,128)}, u32[]{:S(2)}) copy-start(f32[16,16]{1,0:T(8,128)} %param.10) | copy-start | bytes 3076
  9.5 30.4 %all-to-all-start = ((bf16[128,3,16,128]{3,0,1,2:T(8,128)(2,1)}), bf16[128,3,16,128]{3,0,1,2:T(8,128)(2,1)S(1)}, u32[]{:S(2)}, u32[]{:S(2)}) async-start(bf16[128,3,16,128]{3,0,1,2:T(8,128)(2,1)} %copy.26), calls=%async_computation | async-start | bytes 3145728 | tf_op jit(solution)/shard_map/all_to_all | solution.py:76
  13.9 77.7 %all-gather.2.cloned.1.call-start = ((), (), s32[]{:S(2)}) async-start(), calls=%async_computation.2 | async-start | bytes 2621440 | tf_op jit(solution)/shard_map/all_gather | solution.py:70
  16.2 45.6 %copy-start.6 = (f32[3,4,128]{2,1,0:T(4,128)}, f32[3,4,128]{2,1,0:T(4,128)S(1)}, u32[]{:S(2)}) copy-start(f32[3,4,128]{2,1,0:T(4,128)S(1)} %get-tuple-element.53) | copy-start | bytes 18436
  16.2 45.6 %copy-start.8 = (f32[3,4,128]{2,1,0:T(4,128)}, f32[3,4,128]{2,1,0:T(4,128)S(1)}, u32[]{:S(2)}) copy-start(f32[3,4,128]{2,1,0:T(4,128)S(1)} %get-tuple-element.54) | copy-start | bytes 18436
  16.2 45.6 %copy-start.10 = (f32[3,4,128]{2,1,0:T(4,128)}, f32[3,4,128]{2,1,0:T(4,128)S(1)}, u32[]{:S(2)}) copy-start(f32[3,4,128]{2,1,0:T(4,128)S(1)} %get-tuple-element.55) | copy-start | bytes 18436
  16.2 45.6 %copy-start.12 = (f32[3,4,128]{2,1,0:T(4,128)}, f32[3,4,128]{2,1,0:T(4,128)S(1)}, u32[]{:S(2)}) copy-start(f32[3,4,128]{2,1,0:T(4,128)S(1)} %get-tuple-element.56) | copy-start | bytes 18436
  16.2 45.6 %copy-start.14 = (f32[3,4,128]{2,1,0:T(4,128)}, f32[3,4,128]{2,1,0:T(4,128)S(1)}, u32[]{:S(2)}) copy-start(f32[3,4,128]{2,1,0:T(4,128)S(1)} %get-tuple-element.57) | copy-start | bytes 18436
  16.2 45.6 %copy-start.16 = (f32[3,4,128]{2,1,0:T(4,128)}, f32[3,4,128]{2,1,0:T(4,128)S(1)}, u32[]{:S(2)}) copy-start(f32[3,4,128]{2,1,0:T(4,128)S(1)} %get-tuple-element.58) | copy-start | bytes 18436
  16.2 45.6 %copy-start.18 = (f32[3,4,128]{2,1,0:T(4,128)}, f32[3,4,128]{2,1,0:T(4,128)S(1)}, u32[]{:S(2)}) copy-start(f32[3,4,128]{2,1,0:T(4,128)S(1)} %get-tuple-element.59) | copy-start | bytes 18436
  16.2 45.6 %copy-start.20 = (f32[3,4,128]{2,1,0:T(4,128)}, f32[3,4,128]{2,1,0:T(4,128)S(1)}, u32[]{:S(2)}) copy-start(f32[3,4,128]{2,1,0:T(4,128)S(1)} %get-tuple-element.60) | copy-start | bytes 18436
  16.2 45.6 %copy-start.22 = (f32[3,4,128]{2,1,0:T(4,128)}, f32[3,4,128]{2,1,0:T(4,128)S(1)}, u32[]{:S(2)}) copy-start(f32[3,4,128]{2,1,0:T(4,128)S(1)} %get-tuple-element.61) | copy-start | bytes 18436
  16.2 45.6 %copy-start.24 = (f32[3,4,128]{2,1,0:T(4,128)}, f32[3,4,128]{2,1,0:T(4,128)S(1)}, u32[]{:S(2)}) copy-start(f32[3,4,128]{2,1,0:T(4,128)S(1)} %get-tuple-element.62) | copy-start | bytes 18436
  16.3 45.6 %copy-start.26 = (f32[3,4,128]{2,1,0:T(4,128)}, f32[3,4,128]{2,1,0:T(4,128)S(1)}, u32[]{:S(2)}) copy-start(f32[3,4,128]{2,1,0:T(4,128)S(1)} %get-tuple-element.63) | copy-start | bytes 18436
  16.3 45.6 %copy-start.28 = (f32[3,4,128]{2,1,0:T(4,128)}, f32[3,4,128]{2,1,0:T(4,128)S(1)}, u32[]{:S(2)}) copy-start(f32[3,4,128]{2,1,0:T(4,128)S(1)} %get-tuple-element.64) | copy-start | bytes 18436
  16.3 45.6 %copy-start.30 = (f32[3,4,128]{2,1,0:T(4,128)}, f32[3,4,128]{2,1,0:T(4,128)S(1)}, u32[]{:S(2)}) copy-start(f32[3,4,128]{2,1,0:T(4,128)S(1)} %get-tuple-element.65) | copy-start | bytes 18436
  40.0 6.6 %copy-start.2 = (bf16[512,2048]{1,0:T(8,128)(2,1)S(1)}, bf16[512,2048]{1,0:T(8,128)(2,1)}, u32[]{:S(2)}) copy-start(bf16[512,2048]{1,0:T(8,128)(2,1)} %param.9) | copy-start | bytes 6291460
  40.1 21.6 %copy-start = (bf16[128,3,4,4,128]{4,0,2,3,1:T(8,128)(2,1)}, bf16[128,3,4,4,128]{4,0,2,3,1:T(8,128)(2,1)S(1)}, u32[]{:S(2)}) copy-start(bf16[128,3,4,4,128]{4,0,2,3,1:T(8,128)(2,1)S(1)} %copy.49) | copy-start | bytes 4718596
  40.2 20.6 %collective-permute-start = (bf16[256,3,4,128]{3,0,2,1:T(8,128)(2,1)S(1)}, bf16[256,3,4,128]{3,0,2,1:T(8,128)(2,1)S(1)}, u32[]{:S(2)}, u32[]{:S(2)}) collective-permute-start(bf16[256,3,4,128]{3,0,2,1:T(8,128)(2,1)S(1)} %bitcast.129), channel_id=1, source_target_pairs={{0,4},{4,8},{8,12},{12,16},{16,20},{20,24},{24,28},{1,5},{5,9},{9,... | collective-permute-start | bytes 2359304 | tf_op jit(solution)/shard_map/ppermute | solution.py:15
  91.6 3.7 %copy-start.1 = (bf16[768,3,4,128]{3,0,2,1:T(8,128)(2,1)S(1)}, bf16[768,3,4,128]{3,0,2,1:T(8,128)(2,1)}, u32[]{:S(2)}) copy-start(bf16[768,3,4,128]{3,0,2,1:T(8,128)(2,1)} %add_convert_fusion) | copy-start | bytes 7077892
  95.3 3.3 %copy-start.4 = (bf16[512,512]{1,0:T(8,128)(2,1)}, bf16[512,512]{1,0:T(8,128)(2,1)S(1)}, u32[]{:S(2)}) copy-start(bf16[512,512]{1,0:T(8,128)(2,1)S(1)} %convolution_convert_fusion) | copy-start | bytes 1572868
  137.2 4.2 %copy-start.3 = (f32[640,4,128]{2,0,1:T(8,128)S(1)}, f32[640,4,128]{2,0,1:T(8,128)}, u32[]{:S(2)}) copy-start(f32[640,4,128]{2,0,1:T(8,128)} %fusion.30) | copy-start | bytes 3932164
  141.8 0.7 copy-start.21
  141.8 0.7 copy-start.23
  141.8 0.7 copy-start.25
  141.8 0.8 copy-start.27
  141.8 0.8 copy-start.29
  141.8 0.8 copy-start.31
  161.4 20.0 %collective-permute-start.1 = (bf16[256,3,4,128]{3,0,2,1:T(8,128)(2,1)S(1)}, bf16[256,3,4,128]{3,0,2,1:T(8,128)(2,1)S(1)}, u32[]{:S(2)}, u32[]{:S(2)}) collective-permute-start(bf16[256,3,4,128]{3,0,2,1:T(8,128)(2,1)S(1)} %get-tuple-element.30), channel_id=1, source_target_pairs={{4,0},{8,4},{12,8},{16,12},{20,16},{24,20},{28,24},{5,1},{9,5},{13... | collective-permute-start | bytes 2359304 | tf_op jit(solution)/shard_map/ppermute | solution.py:15
  (7 other events, 5.0 us)
Sparse Core Ops, SparseCore 0:
  16.3 30.4 all-gather.1
where the time goes:
time: 215 us; the launch traced here: 214 us
  matrix products  62.2 us (29%)
  waiting for transfers between devices  52.9 us (25%)
  other arithmetic  43.8 us (20%)
  blocking collectives  22.7 us (11%)
  between operations  14 us (7%)
  starting transfers between devices  10.6 us (5%)
  local copies, waits for them, and re-layouts  7.9 us (4%)
    ppermute x2, waiting for transfers between devices, shifted(): return lax.ppermute(value, axis, pairs)  29.6 us
    all_to_all x1, blocking collectives, per_device(): lax.all_to_all(result, 'head', split_axis=0, concat_axis=2, tiled=True)  22.7 us
    all_to_all x1, waiting for transfers between devices, per_device(): lax.all_to_all(qkv_pre, 'head', split_axis=2, concat_axis=0, tiled=True)  22.6 us
    dot_general x1, matrix products, attend(): jnp.einsum('hqk,qhe->khe', d_score, q_block, preferred_element_type=jnp.f...  20.8 us
    convert_element_type x1, other arithmetic, per_device(): mixed_rows = causal_conv(extended, conv_kernel).astype(jnp.bfloat16)  20.5 us
    another operation x2, other arithmetic  18.9 us
    dot_general x1, matrix products, attend(): jnp.einsum('hqk,khe->qhe', d_score, k_block, preferred_element_type=jnp.f...  17.9 us
    sub x1, matrix products, attend(): exp_scores = jnp.where(allowed, jnp.exp(scores - row_top), 0.0)  9.22 us
  transfers between devices with their start and end apart: 4, of which 3 were waited for; matrix products, arithmetic and copies ran while one was open for 18% of the time, Pallas kernels for 0%

commit v1 on v0

v1 whole, which is shorter than its diff:
```python
import functools
import math

import jax
import jax.numpy as jnp
from jax import lax
from jax.experimental import pallas as pl
from jax.experimental.pallas import tpu as pltpu
from jax.sharding import PartitionSpec as P

KW = 31
MASKB = 512
TILE = 128
PAD = 32
NEG = -1e30
F32 = jnp.float32
BF16 = jnp.bfloat16
VMEM_LIMIT = 56 * 1024 * 1024


def params():
    return pltpu.CompilerParams(vmem_limit_bytes=VMEM_LIMIT)


def loop(count, body):
    if count <= 4:
        for i in range(count):
            body(i)
    else:
        lax.fori_loop(0, count, lambda i, c: (body(i), c)[1], 0)


def pack_kernel(n_head, n_chunks, src, *refs):
    outs, stage = refs[:-1], refs[-1]
    tokens, _, heads, dim = src.shape
    local = heads // n_head
    per_chunk = local // n_chunks
    me = lax.axis_index("head")
    stage[...] = src[:, 0].astype(F32).reshape(tokens * heads, dim)
    for j in range(n_head):
        first = jnp.bitwise_xor(me, j) * local
        for c in range(n_chunks):
            for h in range(per_chunk):
                rows = stage[pl.ds(first + c * per_chunk + h, tokens, stride=heads), :]
                outs[j * n_chunks + c][0, h] = rows.astype(BF16)


def pack(qkv, n_head, n_chunks):
    tokens, parts, heads, dim = qkv.shape
    per_chunk = heads // n_head // n_chunks
    count = n_head * n_chunks
    outs = pl.pallas_call(
        functools.partial(pack_kernel, n_head, n_chunks),
        grid=(parts,),
        in_specs=[pl.BlockSpec((tokens, 1, heads, dim), lambda p: (0, p, 0, 0))],
        out_specs=[pl.BlockSpec((1, per_chunk, tokens, dim), lambda p: (p, 0, 0, 0))] * count,
        out_shape=[jax.ShapeDtypeStruct((parts, per_chunk, tokens, dim), BF16)] * count,
        scratch_shapes=[pltpu.VMEM((tokens * heads, dim), F32)],
        compiler_params=params(),
        name="pack",
    )(qkv)
    return [[outs[j * n_chunks + c] for j in range(n_head)] for c in range(n_chunks)]


def unpack_kernel(n_head, n_chunks, *refs):
    srcs, out, stage = refs[:-2], refs[-2], refs[-1]
    tokens, _, heads, dim = out.shape
    local = heads // n_head
    per_chunk = local // n_chunks
    me = lax.axis_index("head")
    for j in range(n_head):
        first = jnp.bitwise_xor(me, j) * local
        for c in range(n_chunks):
            for h in range(per_chunk):
                rows = srcs[c * n_head + j][0, h].astype(F32)
                stage[pl.ds(first + c * per_chunk + h, tokens, stride=heads), :] = rows
    out[:, 0] = stage[...].reshape(tokens, heads, dim).astype(BF16)


def unpack(pieces, n_head, n_chunks):
    parts, per_chunk, tokens, dim = pieces[0][0].shape
    heads = per_chunk * n_chunks * n_head
    flat = [piece for chunk in pieces for piece in chunk]
    return pl.pallas_call(
        functools.partial(unpack_kernel, n_head, n_chunks),
        grid=(parts,),
        in_specs=[pl.BlockSpec((1, per_chunk, tokens, dim), lambda p: (p, 0, 0, 0))] * len(flat),
        out_specs=pl.BlockSpec((tokens, 1, heads, dim), lambda p: (0, p, 0, 0)),
        out_shape=jax.ShapeDtypeStruct((tokens, parts, heads, dim), BF16),
        scratch_shapes=[pltpu.VMEM((tokens * heads, dim), F32)],
        compiler_params=params(),
        name="unpack",
    )(*flat)


def dequant_kernel(values, scales, weight):
    rows, width = values.shape
    side = width // scales.shape[1]
    first = lax.axis_index("head") * (rows // side)
    for r in range(rows // side):
        for c in range(width // side):
            at = (slice(r * side, (r + 1) * side), slice(c * side, (c + 1) * side))
            weight[at] = (values[at].astype(F32) * scales[first + r, c]).astype(BF16)


def dequantize(values, scales):
    return pl.pallas_call(
        dequant_kernel,
        in_specs=[
            pl.BlockSpec(memory_space=pltpu.VMEM),
            pl.BlockSpec(memory_space=pltpu.SMEM),
        ],
        out_specs=pl.BlockSpec(memory_space=pltpu.VMEM),
        out_shape=jax.ShapeDtypeStruct(values.shape, BF16),
        compiler_params=params(),
        name="dequant",
    )(values, scales)


def dattn_kernel(grads, weight, out):
    heads, _, dim = out.shape
    full = lax.dot_general(
        grads[...], weight[...], (((1,), (1,)), ((), ())), preferred_element_type=F32
    )
    for h in range(heads):
        out[h] = full[:, h * dim : (h + 1) * dim].astype(BF16)


def d_attn(grads, weight, dim):
    tokens = grads.shape[0]
    heads = weight.shape[0] // dim
    return pl.pallas_call(
        dattn_kernel,
        out_shape=jax.ShapeDtypeStruct((heads, tokens, dim), BF16),
        compiler_params=params(),
        name="dattn",
    )(grads, weight)


def core_kernel(n_head, head0, span, window, offsets, *refs):
    pieces = refs[:n_head]
    grads = refs[n_head : 2 * n_head]
    halo, taps, own_out, carry_out, ext, mixed, d_out, totals = refs[2 * n_head :]
    tokens = pieces[0].shape[2]
    seq_rows = tokens * n_head
    margin = span + PAD
    keys = span + TILE
    dim = pieces[0].shape[3]
    inv_scale = 1.0 / math.sqrt(dim)
    me = lax.axis_index("head")
    seq_index = lax.axis_index("seq")
    head = head0 + pl.program_id(0)
    local = taps.shape[2]

    ext[1, :margin] = halo[0, :margin].astype(F32)
    ext[2, :margin] = halo[0, margin : 2 * margin].astype(F32)
    ext[0, span:margin] = halo[0, 2 * margin :].astype(F32)
    for j in range(n_head):
        start = pl.multiple_of(jnp.bitwise_xor(me, j) * tokens, tokens)
        for p in range(3):
            ext[p, pl.ds(margin + start, tokens), :] = pieces[j][p, 0].astype(F32)
        d_out[pl.ds(start, tokens), :] = grads[j][0]

    def tap(p, tau):
        return taps[tau, p, pl.ds(head, 1), :]

    def conv_block(p, first, rows):
        acc = jnp.zeros((rows, dim), F32)
        for b in range(8):
            window_rows = ext[p, pl.ds(first + 8 - b, rows + 24), :]
            for a in range(4):
                tau = 8 * a + b
                if tau < KW:
                    acc = acc + tap(p, tau) * window_rows[24 - 8 * a : 24 - 8 * a + rows]
        mixed[p, pl.ds(first, rows), :] = acc.astype(BF16)

    def conv_part(p):
        lax.fori_loop(
            0,
            (span + seq_rows) // TILE,
            lambda i, c: (conv_block(p, pl.multiple_of(i * TILE, TILE), TILE), c)[1],
            0,
        )

    lax.fori_loop(1, 3, lambda p, c: (conv_part(p), c)[1], 0)
    lax.fori_loop(
        0,
        seq_rows // TILE,
        lambda i, c: (conv_block(0, pl.multiple_of(span + i * TILE, TILE), TILE), c)[1],
        0,
    )

    totals[1] = jnp.zeros(totals.shape[1:], F32)
    totals[2] = jnp.zeros(totals.shape[1:], F32)
    totals[0, span:margin] = jnp.zeros((PAD, dim), F32)
    totals[0, margin + seq_rows :] = jnp.zeros((PAD, dim), F32)
    row = lax.broadcasted_iota(jnp.int32, (TILE, keys), 0)
    col = lax.broadcasted_iota(jnp.int32, (TILE, keys), 1)
    distance = row + span - col
    base = window[me * local + head]
    blocks = seq_rows // MASKB

    def attend(t):
        first = t * TILE
        reach = base + offsets[seq_index * blocks + first // MASKB]
        limit = jnp.minimum(reach, seq_index * seq_rows + first + row)
        allowed = (distance >= 0) & (distance <= limit)
        q = mixed[0, pl.ds(span + first, TILE), :]
        k = mixed[1, pl.ds(first, keys), :]
        v = mixed[2, pl.ds(first, keys), :]
        o = d_out[pl.ds(first, TILE), :]
        nt = (((1,), (1,)), ((), ()))
        tn = (((0,), (0,)), ((), ()))
        scores = lax.dot_general(q, k, nt, preferred_element_type=F32) * inv_scale
        scores = jnp.where(allowed, scores, NEG)
        top = jnp.max(scores, axis=1, keepdims=True)
        exps = jnp.where(allowed, jnp.exp(scores - top), 0.0)
        probs = exps / jnp.sum(exps, axis=1, keepdims=True)
        d_prob = lax.dot_general(o, v, nt, preferred_element_type=F32)
        delta = jnp.sum(probs * d_prob, axis=1, keepdims=True)
        d_score = (probs * (d_prob - delta) * inv_scale).astype(BF16)
        probs_b = probs.astype(BF16)
        totals[0, pl.ds(margin + first, TILE), :] = jnp.dot(d_score, k, preferred_element_type=F32)
        at = pl.ds(PAD + first, keys)
        totals[1, at, :] += lax.dot_general(d_score, q, tn, preferred_element_type=F32)
        totals[2, at, :] += lax.dot_general(probs_b, o, tn, preferred_element_type=F32)

    loop(seq_rows // TILE, attend)

    def spread_block(p, first, rows):
        acc = jnp.zeros((rows, dim), F32)
        for b in range(8):
            window_rows = totals[p, pl.ds(first + b, rows + 24), :]
            for a in range(4):
                tau = 8 * a + b
                if tau < KW:
                    acc = acc + tap(p, tau) * window_rows[8 * a : 8 * a + rows]
        return acc

    def own_block(p, i):
        first = pl.multiple_of(i * TILE, TILE)
        own_out[p, 0, pl.ds(first, TILE), :] = spread_block(p, margin + first, TILE)

    carry_out[0, 2 * margin :] = spread_block(0, span, PAD).astype(BF16)
    for p in (1, 2):
        for first in range(0, margin, PAD):
            at = (p - 1) * margin + first
            carry_out[0, at : at + PAD] = spread_block(p, first, PAD).astype(BF16)
    lax.fori_loop(
        0,
        3,
        lambda p, c: lax.fori_loop(
            0, seq_rows // TILE, lambda i, d: (own_block(p, i), d)[1], c
        ),
        0,
    )


def core(pieces, grads, halo, taps, window, offsets, head0, span):
    n_head = len(pieces)
    parts, heads, tokens, dim = pieces[0].shape
    seq_rows = tokens * n_head
    margin = span + PAD
    return pl.pallas_call(
        functools.partial(core_kernel, n_head, head0, span),
        grid=(heads,),
        in_specs=[pl.BlockSpec(memory_space=pltpu.SMEM)] * 2
        + [pl.BlockSpec((parts, 1, tokens, dim), lambda h: (0, h, 0, 0))] * n_head
        + [pl.BlockSpec((1, tokens, dim), lambda h: (head0 + h, 0, 0))] * n_head
        + [
            pl.BlockSpec((1, 2 * margin + PAD, dim), lambda h: (h, 0, 0)),
            pl.BlockSpec(taps.shape, lambda h: (0, 0, 0, 0)),
        ],
        out_specs=[
            pl.BlockSpec((parts, 1, seq_rows, dim), lambda h: (0, h, 0, 0)),
            pl.BlockSpec((1, 2 * margin + PAD, dim), lambda h: (h, 0, 0)),
        ],
        out_shape=[
            jax.ShapeDtypeStruct((parts, heads, seq_rows, dim), F32),
            jax.ShapeDtypeStruct((heads, 2 * margin + PAD, dim), BF16),
        ],
        scratch_shapes=[
            pltpu.VMEM((parts, margin + seq_rows, dim), F32),
            pltpu.VMEM((parts, span + seq_rows, dim), BF16),
            pltpu.VMEM((seq_rows, dim), BF16),
            pltpu.VMEM((parts, margin + seq_rows + PAD, dim), F32),
        ],
        compiler_params=params(),
        name="core",
    )(window, offsets, *pieces, *grads, halo, taps)


def finish_kernel(n_head, span, own, carry, *refs):
    outs, whole = refs[:-1], refs[-1]
    tokens = outs[0].shape[2]
    seq_rows = own.shape[2]
    margin = span + PAD
    me = lax.axis_index("head")
    for p, size, start in ((0, PAD, 2 * margin), (1, margin, 0), (2, margin, margin)):
        edge = seq_rows - size
        whole[p, :edge] = own[p, 0, :edge].astype(BF16)
        back = carry[0, start : start + size].astype(F32)
        whole[p, edge:] = (own[p, 0, edge:] + back).astype(BF16)
    for j in range(n_head):
        start = pl.multiple_of(jnp.bitwise_xor(me, j) * tokens, tokens)
        for p in range(3):
            outs[j][p, 0] = whole[p, pl.ds(start, tokens), :]


def finish(own, carry, n_head, span):
    parts, heads, seq_rows, dim = own.shape
    tokens = seq_rows // n_head
    return pl.pallas_call(
        functools.partial(finish_kernel, n_head, span),
        grid=(heads,),
        in_specs=[
            pl.BlockSpec((parts, 1, seq_rows, dim), lambda h: (0, h, 0, 0)),
            pl.BlockSpec((1, carry.shape[1], dim), lambda h: (h, 0, 0)),
        ],
        out_specs=[pl.BlockSpec((parts, 1, tokens, dim), lambda h: (0, h, 0, 0))] * n_head,
        out_shape=[jax.ShapeDtypeStruct((parts, heads, tokens, dim), BF16)] * n_head,
        scratch_shapes=[pltpu.VMEM((parts, seq_rows, dim), BF16)],
        compiler_params=params(),
        name="finish",
    )(own, carry)


def partner(value, j):
    if j == 0:
        return value
    size = lax.axis_size("head")
    return lax.ppermute(value, "head", [(i, i ^ j) for i in range(size)])


def shifted(value, by):
    length = lax.axis_size("seq")
    pairs = [(i, i + by) for i in range(length) if 0 <= i + by < length]
    return lax.ppermute(value, "seq", pairs)


def tail_of(pieces, p, rows):
    me = lax.axis_index("head")
    n_head = len(pieces)
    tokens = pieces[0].shape[2]
    found = []
    source = n_head - 1
    while rows > 0:
        take = min(rows, tokens)
        parts = [piece[p, :, tokens - take :] for piece in pieces]
        found.insert(0, lax.select_n(jnp.bitwise_xor(me, source), *parts))
        rows -= take
        source -= 1
    return found


def per_device(qkv_pre, grad_out, out_values, out_scales, conv_kernel, window, offsets):
    n_head = lax.axis_size("head")
    tokens, _, heads, dim = qkv_pre.shape
    local = heads // n_head
    n_chunks = 2 if local % 2 == 0 else 1
    per_chunk = local // n_chunks
    seq_rows = tokens * n_head
    span = seq_rows // 4
    margin = span + PAD

    packed = pack(qkv_pre, n_head, n_chunks)
    g_pieces = [grad_out]
    for j in range(1, n_head):
        if j > 1 and j % 2 == 1:
            g_pieces.append(partner(g_pieces[j - 1], 1))
        else:
            g_pieces.append(partner(grad_out, j))
    weight = dequantize(out_values, out_scales)
    grads = [d_attn(g, weight, dim) for g in g_pieces]

    results = []
    for c in range(n_chunks):
        pieces = [partner(packed[c][j], j) for j in range(n_head)]
        tail = jnp.concatenate(
            tail_of(pieces, 1, margin) + tail_of(pieces, 2, margin) + tail_of(pieces, 0, PAD), axis=1
        )
        halo = shifted(tail, 1)
        own, carry = core(
            pieces, grads, halo, conv_kernel, window, offsets, c * per_chunk, span
        )
        outs = finish(own, shifted(carry, -1), n_head, span)
        results.append([partner(outs[j], j) for j in range(n_head)])
    return unpack(results, n_head, n_chunks)


def solution(mesh):
    return jax.shard_map(
        per_device,
        mesh=mesh,
        in_specs=(
            P(("seq", "head"), None, None, None),
            P(("seq", "head"), None),
            P("head", None),
            P(),
            P(None, None, "head", None),
            P(),
            P(),
        ),
        out_specs=P(("seq", "head"), None, None, None),
        check_vma=False,
    )
```

time: 215 us -> 123 us (0.57)
  matrix products: 62.2 us -> 0 us
  Pallas kernels: 0 us -> 58.5 us
  other arithmetic: 43.8 us -> 0.34 us
  blocking collectives: 22.7 us -> 0 us
  waiting for transfers between devices: 52.9 us -> 33.9 us
  between operations: 14 us -> 0.24 us
  starting transfers between devices: 10.6 us -> 22.2 us
  local copies, waits for them, and re-layouts: 7.9 us -> 5.49 us
    pallas_call x0 -> x11, Pallas kernels: none -> 58.5 us  [the longest x2 29.3 us: core(): pl.pallas_call(functools.partial(core_kernel, n_head, head0, span), grid=...]
    dot_general x6 -> x0, matrix products: 53 us -> none  [the longest x1 20.8 us: attend(): jnp.einsum('hqk,qhe->khe', d_score, q_block, preferred_element_type=jnp.f...]
    all_to_all x1 -> x0, blocking collectives: 22.7 us -> none  [per_device(): lax.all_to_all(result, 'head', split_axis=0, concat_axis=2, tiled=True)]
    all_to_all x1 -> x0, waiting for transfers between devices: 22.6 us -> none  [per_device(): lax.all_to_all(qkv_pre, 'head', split_axis=2, concat_axis=0, tiled=True)]
    convert_element_type x1 -> x0, other arithmetic: 20.5 us -> none  [per_device(): mixed_rows = causal_conv(extended, conv_kernel).astype(jnp.bfloat16)]
    another operation x3 -> x0, other arithmetic: 19.2 us -> none
    ppermute x2 -> x19, starting transfers between devices: 6.23 us -> 22.2 us  [the longest x15 11.6 us: partner(): return lax.ppermute(value, 'head', [(i, i ^ j) for i in range(size)])]
    sub x1 -> x0, matrix products: 9.22 us -> none  [attend(): exp_scores = jnp.where(allowed, jnp.exp(scores - row_top), 0.0)]
  transfers between devices with their start and end apart: 4 -> 19, of which waited for: 3 -> 8; matrix products, arithmetic and copies ran while one was open for 18% -> 0% of each run, Pallas kernels for 0% -> 30%
where the time goes in v1:
time: 123 us; the launch traced here: 121 us
  Pallas kernels  58.5 us (48%)
  waiting for transfers between devices  33.9 us (28%)
  starting transfers between devices  22.2 us (18%)
  local copies, waits for them, and re-layouts  5.49 us (4%)
    pallas_call x2, Pallas kernels, core(): pl.pallas_call(functools.partial(core_kernel, n_head, head0, span), grid=...  29.3 us
    ppermute x15, waiting for transfers between devices, partner(): return lax.ppermute(value, 'head', [(i, i ^ j) for i in range(size)])  23.8 us
    pallas_call x4, Pallas kernels, d_attn(): pl.pallas_call(dattn_kernel, out_shape=jax.ShapeDtypeStruct((heads, token...  13.1 us
    ppermute x15, starting transfers between devices, partner(): return lax.ppermute(value, 'head', [(i, i ^ j) for i in range(size)])  11.6 us
    ppermute x4, starting transfers between devices, shifted(): return lax.ppermute(value, 'seq', pairs)  10.5 us
    ppermute x4, waiting for transfers between devices, shifted(): return lax.ppermute(value, 'seq', pairs)  10.1 us
    unnamed x54, local copies, waits for them, and re-layouts  5.49 us
    pallas_call x2, Pallas kernels, finish(): pl.pallas_call(functools.partial(finish_kernel, n_head, span), grid=(head...  4.49 us
  transfers between devices with their start and end apart: 19, of which 8 were waited for; matrix products, arithmetic and copies ran while one was open for 0% of the time, Pallas kernels for 30%

profile of v1, /device:TPU:0, one launch (start us, length us, event | category | flops | bytes accessed | tf_op | source)
XLA Modules:
  0.0 120.7 jit_solution(7348227002149386397)
XLA Ops:
  0.0 3.9 %pack.1 = (bf16[3,2,128,128]{3,2,1,0:T(8,128)(2,1)}, bf16[3,2,128,128]{3,2,1,0:T(8,128)(2,1)}, bf16[3,2,128,128]{3,2,1,0:T(8,128)(2,1)}, bf16[3,2,128,128]{3,2,1...) custom-call(bf16[128,3,16,128]{3,2,1,0:T(8,128)(2,1)} %src.1), custom_call_target="tpu_custom_call" | custom-call | tf_op jit(solution)/shard_map/pack/pallas_call | solution.py:52
  4.4 2.6 %collective-permute-start.12 = (bf16[3,2,128,128]{3,2,1,0:T(8,128)(2,1)}, bf16[3,2,128,128]{3,2,1,0:T(8,128)(2,1)S(1)}, u32[]{:S(2)}, u32[]{:S(2)}) collective-permute-start(bf16[3,2,128,128]{3,2,1,0:T(8,128)(2,1)} %get-tuple-element.37), channel_id=1, source_target_pairs={{0,2},{1,3},{2,0},{3,1},{4,6},{5,7},{6,4},{7,5},{8,10},{9,11},{10,... | collective-permute-start | bytes 589832 | tf_op jit(solution)/shard_map/ppermute | solution.py:332
  7.1 1.7 %collective-permute-start.4 = (bf16[128,2048]{1,0:T(8,128)(2,1)S(1)}, bf16[128,2048]{1,0:T(8,128)(2,1)S(1)}, u32[]{:S(2)}, u32[]{:S(2)}) collective-permute-start(bf16[128,2048]{1,0:T(8,128)(2,1)S(1)} %copy-done.8), channel_id=1, source_target_pairs={{0,2},{1,3},{2,0},{3,1},{4,6},{5,7},{6,4},{7,5},{8,10},{9,11},{10,... | collective-permute-start | bytes 1572872 | tf_op jit(solution)/shard_map/ppermute | solution.py:332
  8.9 3.5 %dequant.1.weight = bf16[512,2048]{1,0:T(8,128)(2,1)} custom-call(bf16[512,2048]{1,0:T(8,128)(2,1)} %values.1, f32[16,16]{1,0:T(8,128)} %scales.1), custom_call_target="tpu_custom_call" | custom-call | tf_op jit(solution)/shard_map/dequant/pallas_call | solution.py:107
  12.4 3.3 %dattn.4.refs_4_ = bf16[4,128,128]{2,1,0:T(8,128)(2,1)} custom-call(bf16[128,2048]{1,0:T(8,128)(2,1)} %grads.1, bf16[512,2048]{1,0:T(8,128)(2,1)} %dequant.1.weight), custom_call_target="tpu_custom_call" | custom-call | tf_op jit(solution)/shard_map/dattn/pallas_call | solution.py:132
  16.8 1.8 %collective-permute-start.2 = (bf16[3,2,128,128]{3,2,1,0:T(8,128)(2,1)S(1)}, bf16[3,2,128,128]{3,2,1,0:T(8,128)(2,1)S(1)}, u32[]{:S(2)}, u32[]{:S(2)}) collective-permute-start(bf16[3,2,128,128]{3,2,1,0:T(8,128)(2,1)S(1)} %copy-done.22), channel_id=1, source_target_pairs={{0,3},{1,2},{2,1},{3,0},{4,7},{5,6},{6,5},{7,4},{8,11},{9,10},{10,... | collective-permute-start | bytes 589832 | tf_op jit(solution)/shard_map/ppermute | solution.py:332
  18.8 3.4 %collective-permute-start.14 = (bf16[2,352,128]{2,1,0:T(8,128)(2,1)S(1)}, bf16[2,352,128]{2,1,0:T(8,128)(2,1)S(1)}, u32[]{:S(2)}, u32[]{:S(2)}) collective-permute-start(bf16[2,352,128]{2,1,0:T(8,128)(2,1)S(1)} %constant_dynamic-update-slice_fusion.3), channel_id=1, source_target_pairs={{0,4},{4,8},{8,12},{12,16},{16,20},{20,24},{24,28},{1,5},{5,9},{9,... | collective-permute-start | bytes 540680 | tf_op jit(solution)/shard_map/ppermute | solution.py:338
  22.2 10.4 %collective-permute-done.1.refs_2_ = bf16[3,2,128,128]{3,2,1,0:T(8,128)(2,1)S(1)} collective-permute-done((bf16[3,2,128,128]{3,2,1,0:T(8,128)(2,1)S(1)}, bf16[3,2,128,128]{3,2,1,0:T(8,128)(2,1)S(1)}, u32[]{:S(2)}, u32[]{:S(2)}) %collective-permute-start.1) | collective-permute-done | bytes 196640 | tf_op jit(solution)/shard_map/ppermute | solution.py:332
  32.6 3.7 %collective-permute-done.2.refs_3_ = bf16[3,2,128,128]{3,2,1,0:T(8,128)(2,1)S(1)} collective-permute-done((bf16[3,2,128,128]{3,2,1,0:T(8,128)(2,1)S(1)}, bf16[3,2,128,128]{3,2,1,0:T(8,128)(2,1)S(1)}, u32[]{:S(2)}, u32[]{:S(2)}) %collective-permute-start.2) | collective-permute-done | bytes 196640 | tf_op jit(solution)/shard_map/ppermute | solution.py:332
  37.2 3.3 %dattn.6.refs_6_ = bf16[4,128,128]{2,1,0:T(8,128)(2,1)} custom-call(bf16[128,2048]{1,0:T(8,128)(2,1)} %copy-done.9, bf16[512,2048]{1,0:T(8,128)(2,1)} %dequant.1.weight), custom_call_target="tpu_custom_call" | custom-call | tf_op jit(solution)/shard_map/dattn/pallas_call | solution.py:132
  40.5 0.8 copy-done.10
  41.2 3.3 %dattn.5.refs_5_ = bf16[4,128,128]{2,1,0:T(8,128)(2,1)} custom-call(bf16[128,2048]{1,0:T(8,128)(2,1)} %copy-done.10, bf16[512,2048]{1,0:T(8,128)(2,1)} %dequant.1.weight), custom_call_target="tpu_custom_call" | custom-call | tf_op jit(solution)/shard_map/dattn/pallas_call | solution.py:132
  44.5 0.8 copy-done.11
  45.3 3.2 %dattn.7.refs_7_ = bf16[4,128,128]{2,1,0:T(8,128)(2,1)} custom-call(bf16[128,2048]{1,0:T(8,128)(2,1)} %copy-done.11, bf16[512,2048]{1,0:T(8,128)(2,1)} %dequant.1.weight), custom_call_target="tpu_custom_call" | custom-call | tf_op jit(solution)/shard_map/dattn/pallas_call | solution.py:132
  48.5 0.7 copy-done.18
  49.2 14.7 %core.3 = (f32[3,2,512,128]{3,2,1,0:T(8,128)}, bf16[2,352,128]{2,1,0:T(8,128)(2,1)}) custom-call(s32[16]{0:T(128)} %window.3, s32[8]{0:T(128)} %offsets.3, bf16[3,2,128,128]{3,2,1,0:T(8,128)(2,1)} %get-tuple-element.35.refs_0_, bf16[3,2,128,128]{3,2,1,0:T(8,128)(2,1)} %copy-done.2, bf16[3,2,128,128]{3,2,1,0:T(8,128)(2,1)} %copy-done.3, ...), custom_call_target="tpu_custom_call" | custom-call | tf_op jit(solution)/shard_map/core/pallas_call | solution.py:264
  63.9 1.3 %collective-permute-start.15 = (bf16[2,352,128]{2,1,0:T(8,128)(2,1)}, bf16[2,352,128]{2,1,0:T(8,128)(2,1)S(1)}, u32[]{:S(2)}, u32[]{:S(2)}) collective-permute-start(bf16[2,352,128]{2,1,0:T(8,128)(2,1)} %get-tuple-element.40), channel_id=1, source_target_pairs={{4,0},{8,4},{12,8},{16,12},{20,16},{24,20},{28,24},{5,1},{9,5},{13... | collective-permute-start | bytes 540680 | tf_op jit(solution)/shard_map/ppermute | solution.py:338
  65.3 4.6 %collective-permute-start.6 = (bf16[2,352,128]{2,1,0:T(8,128)(2,1)S(1)}, bf16[2,352,128]{2,1,0:T(8,128)(2,1)S(1)}, u32[]{:S(2)}, u32[]{:S(2)}) collective-permute-start(bf16[2,352,128]{2,1,0:T(8,128)(2,1)S(1)} %constant_dynamic-update-slice_fusion), channel_id=1, source_target_pairs={{0,4},{4,8},{8,12},{12,16},{16,20},{20,24},{24,28},{1,5},{5,9},{9,... | collective-permute-start | bytes 540680 | tf_op jit(solution)/shard_map/ppermute | solution.py:338
  69.8 2.8 %collective-permute-done.15.carry = bf16[2,352,128]{2,1,0:T(8,128)(2,1)S(1)} collective-permute-done((bf16[2,352,128]{2,1,0:T(8,128)(2,1)}, bf16[2,352,128]{2,1,0:T(8,128)(2,1)S(1)}, u32[]{:S(2)}, u32[]{:S(2)}) %collective-permute-start.15) | collective-permute-done | bytes 180256 | tf_op jit(solution)/shard_map/ppermute | solution.py:338
  72.6 0.7 copy-done.20
  73.3 2.3 %finish.3 = (bf16[3,2,128,128]{3,2,1,0:T(8,128)(2,1)}, bf16[3,2,128,128]{3,2,1,0:T(8,128)(2,1)}, bf16[3,2,128,128]{3,2,1,0:T(8,128)(2,1)}, bf16[3,2,128,128]{3,2,1,0:T(8,128)(2,1)}) custom-call(f32[3,2,512,128]{3,2,1,0:T(8,128)} %get-tuple-element.39.own, bf16[2,352,128]{2,1,0:T(8,128)(2,1)} %copy-done.20), custom_call_target="tpu_custom_call" | custom-call | tf_op jit(solution)/shard_map/finish/pallas_call | solution.py:313
  75.6 1.0 collective-permute-done.6.refs_8_
  77.2 14.7 %core.2 = (f32[3,2,512,128]{3,2,1,0:T(8,128)}, bf16[2,352,128]{2,1,0:T(8,128)(2,1)}) custom-call(s32[16]{0:T(128)} %window.3, s32[8]{0:T(128)} %offsets.3, bf16[3,2,128,128]{3,2,1,0:T(8,128)(2,1)} %get-tuple-element.25.refs_0_, bf16[3,2,128,128]{3,2,1,0:T(8,128)(2,1)} %copy-done.4, bf16[3,2,128,128]{3,2,1,0:T(8,128)(2,1)} %copy-done.6, ...), custom_call_target="tpu_custom_call" | custom-call | tf_op jit(solution)/shard_map/core/pallas_call | solution.py:264
  91.9 1.3 %collective-permute-start.7 = (bf16[2,352,128]{2,1,0:T(8,128)(2,1)}, bf16[2,352,128]{2,1,0:T(8,128)(2,1)S(1)}, u32[]{:S(2)}, u32[]{:S(2)}) collective-permute-start(bf16[2,352,128]{2,1,0:T(8,128)(2,1)} %get-tuple-element.30), channel_id=1, source_target_pairs={{4,0},{8,4},{12,8},{16,12},{20,16},{24,20},{28,24},{5,1},{9,5},{13... | collective-permute-start | bytes 540680 | tf_op jit(solution)/shard_map/ppermute | solution.py:338
  93.2 1.6 %collective-permute-start.17 = (bf16[3,2,128,128]{3,2,1,0:T(8,128)(2,1)S(1)}, bf16[3,2,128,128]{3,2,1,0:T(8,128)(2,1)S(1)}, u32[]{:S(2)}, u32[]{:S(2)}) collective-permute-start(bf16[3,2,128,128]{3,2,1,0:T(8,128)(2,1)S(1)} %copy-done.26), channel_id=1, source_target_pairs={{0,2},{1,3},{2,0},{3,1},{4,6},{5,7},{6,4},{7,5},{8,10},{9,11},{10,... | collective-permute-start | bytes 589832 | tf_op jit(solution)/shard_map/ppermute | solution.py:332
  94.8 6.4 %collective-permute-done.7.carry = bf16[2,352,128]{2,1,0:T(8,128)(2,1)S(1)} collective-permute-done((bf16[2,352,128]{2,1,0:T(8,128)(2,1)}, bf16[2,352,128]{2,1,0:T(8,128)(2,1)S(1)}, u32[]{:S(2)}, u32[]{:S(2)}) %collective-permute-start.7) | collective-permute-done | bytes 180256 | tf_op jit(solution)/shard_map/ppermute | solution.py:338
  101.2 0.7 copy-done.21
  101.9 2.2 %finish.2 = (bf16[3,2,128,128]{3,2,1,0:T(8,128)(2,1)}, bf16[3,2,128,128]{3,2,1,0:T(8,128)(2,1)}, bf16[3,2,128,128]{3,2,1,0:T(8,128)(2,1)}, bf16[3,2,128,128]{3,2,1,0:T(8,128)(2,1)}) custom-call(f32[3,2,512,128]{3,2,1,0:T(8,128)} %get-tuple-element.29.own, bf16[2,352,128]{2,1,0:T(8,128)(2,1)} %copy-done.21), custom_call_target="tpu_custom_call" | custom-call | tf_op jit(solution)/shard_map/finish/pallas_call | solution.py:313
  104.7 1.0 collective-permute-start.8
  106.3 5.2 %collective-permute-done.10.refs_3_ = bf16[3,2,128,128]{3,2,1,0:T(8,128)(2,1)S(1)} collective-permute-done((bf16[3,2,128,128]{3,2,1,0:T(8,128)(2,1)}, bf16[3,2,128,128]{3,2,1,0:T(8,128)(2,1)S(1)}, u32[]{:S(2)}, u32[]{:S(2)}) %collective-permute-start.10) | collective-permute-done | bytes 196640 | tf_op jit(solution)/shard_map/ppermute | solution.py:332
  111.5 4.3 %collective-permute-done.9.refs_2_ = bf16[3,2,128,128]{3,2,1,0:T(8,128)(2,1)S(1)} collective-permute-done((bf16[3,2,128,128]{3,2,1,0:T(8,128)(2,1)}, bf16[3,2,128,128]{3,2,1,0:T(8,128)(2,1)S(1)}, u32[]{:S(2)}, u32[]{:S(2)}) %collective-permute-start.9) | collective-permute-done | bytes 196640 | tf_op jit(solution)/shard_map/ppermute | solution.py:332
  116.4 4.2 %unpack.1 = bf16[128,3,16,128]{3,2,1,0:T(8,128)(2,1)} custom-call(bf16[3,2,128,128]{3,2,1,0:T(8,128)(2,1)} %get-tuple-element.31.refs_0_, bf16[3,2,128,128]{3,2,1,0:T(8,128)(2,1)} %copy-done.16, bf16[3,2,128,128]{3,2,1,0:T(8,128)(2,1)} %copy-done.17, bf16[3,2,128,128]{3,2,1,0:T(8,128)(2,1)} %copy-done.15, ...), custom_call_target="tpu_custom_call" | custom-call | tf_op jit(solution)/shard_map/unpack/pallas_call | solution.py:84
  (81 shorter events, 5.3 us)
Async XLA Ops:
  0.0 7.1 %copy-start.8 = (bf16[128,2048]{1,0:T(8,128)(2,1)S(1)}, bf16[128,2048]{1,0:T(8,128)(2,1)}, u32[]{:S(2)}) copy-start(bf16[128,2048]{1,0:T(8,128)(2,1)} %grads.1) | copy-start | bytes 1572868
  3.9 11.8 %collective-permute-start.11 = (bf16[3,2,128,128]{3,2,1,0:T(8,128)(2,1)}, bf16[3,2,128,128]{3,2,1,0:T(8,128)(2,1)S(1)}, u32[]{:S(2)}, u32[]{:S(2)}) collective-permute-start(bf16[3,2,128,128]{3,2,1,0:T(8,128)(2,1)} %get-tuple-element.36), channel_id=1, source_target_pairs={{0,1},{1,0},{2,3},{3,2},{4,5},{5,4},{6,7},{7,6},{8,9},{9,8},{10,11... | collective-permute-start | bytes 589832 | tf_op jit(solution)/shard_map/ppermute | solution.py:332
  4.4 11.8 %collective-permute-start.12 = (bf16[3,2,128,128]{3,2,1,0:T(8,128)(2,1)}, bf16[3,2,128,128]{3,2,1,0:T(8,128)(2,1)S(1)}, u32[]{:S(2)}, u32[]{:S(2)}) collective-permute-start(bf16[3,2,128,128]{3,2,1,0:T(8,128)(2,1)} %get-tuple-element.37), channel_id=1, source_target_pairs={{0,2},{1,3},{2,0},{3,1},{4,6},{5,7},{6,4},{7,5},{8,10},{9,11},{10,... | collective-permute-start | bytes 589832 | tf_op jit(solution)/shard_map/ppermute | solution.py:332
  7.0 9.8 %collective-permute-start.13 = (bf16[3,2,128,128]{3,2,1,0:T(8,128)(2,1)}, bf16[3,2,128,128]{3,2,1,0:T(8,128)(2,1)S(1)}, u32[]{:S(2)}, u32[]{:S(2)}) collective-permute-start(bf16[3,2,128,128]{3,2,1,0:T(8,128)(2,1)} %get-tuple-element.38), channel_id=1, source_target_pairs={{0,3},{1,2},{2,1},{3,0},{4,7},{5,6},{6,5},{7,4},{8,11},{9,10},{10,... | collective-permute-start | bytes 589832 | tf_op jit(solution)/shard_map/ppermute | solution.py:332
  7.1 29.3 %collective-permute-start.4 = (bf16[128,2048]{1,0:T(8,128)(2,1)S(1)}, bf16[128,2048]{1,0:T(8,128)(2,1)S(1)}, u32[]{:S(2)}, u32[]{:S(2)}) collective-permute-start(bf16[128,2048]{1,0:T(8,128)(2,1)S(1)} %copy-done.8), channel_id=1, source_target_pairs={{0,2},{1,3},{2,0},{3,1},{4,6},{5,7},{6,4},{7,5},{8,10},{9,11},{10,... | collective-permute-start | bytes 1572872 | tf_op jit(solution)/shard_map/ppermute | solution.py:332
  8.8 31.6 %collective-permute-start.3 = (bf16[128,2048]{1,0:T(8,128)(2,1)S(1)}, bf16[128,2048]{1,0:T(8,128)(2,1)S(1)}, u32[]{:S(2)}, u32[]{:S(2)}) collective-permute-start(bf16[128,2048]{1,0:T(8,128)(2,1)S(1)} %copy-done.8), channel_id=1, source_target_pairs={{0,1},{1,0},{2,3},{3,2},{4,5},{5,4},{6,7},{7,6},{8,9},{9,8},{10,11... | collective-permute-start | bytes 1572872 | tf_op jit(solution)/shard_map/ppermute | solution.py:332
  12.4 23.9 %copy-start = (bf16[3,2,128,128]{3,2,1,0:T(8,128)(2,1)S(1)}, bf16[3,2,128,128]{3,2,1,0:T(8,128)(2,1)}, u32[]{:S(2)}) copy-start(bf16[3,2,128,128]{3,2,1,0:T(8,128)(2,1)} %get-tuple-element.25.refs_0_) | copy-start | bytes 589828
  15.7 24.7 %copy-start.2 = (bf16[3,2,128,128]{3,2,1,0:T(8,128)(2,1)}, bf16[3,2,128,128]{3,2,1,0:T(8,128)(2,1)S(1)}, u32[]{:S(2)}) copy-start(bf16[3,2,128,128]{3,2,1,0:T(8,128)(2,1)S(1)} %collective-permute-done.11.refs_1_) | copy-start | bytes 589828
  15.7 3.0 %collective-permute-start = (bf16[3,2,128,128]{3,2,1,0:T(8,128)(2,1)S(1)}, bf16[3,2,128,128]{3,2,1,0:T(8,128)(2,1)S(1)}, u32[]{:S(2)}, u32[]{:S(2)}) collective-permute-start(bf16[3,2,128,128]{3,2,1,0:T(8,128)(2,1)S(1)} %copy-done.24), channel_id=1, source_target_pairs={{0,1},{1,0},{2,3},{3,2},{4,5},{5,4},{6,7},{7,6},{8,9},{9,8},{10,11... | collective-permute-start | bytes 589832 | tf_op jit(solution)/shard_map/ppermute | solution.py:332
  16.2 24.2 %copy-start.3 = (bf16[3,2,128,128]{3,2,1,0:T(8,128)(2,1)}, bf16[3,2,128,128]{3,2,1,0:T(8,128)(2,1)S(1)}, u32[]{:S(2)}) copy-start(bf16[3,2,128,128]{3,2,1,0:T(8,128)(2,1)S(1)} %collective-permute-done.12.refs_2_) | copy-start | bytes 589828
  16.2 16.4 %collective-permute-start.1 = (bf16[3,2,128,128]{3,2,1,0:T(8,128)(2,1)S(1)}, bf16[3,2,128,128]{3,2,1,0:T(8,128)(2,1)S(1)}, u32[]{:S(2)}, u32[]{:S(2)}) collective-permute-start(bf16[3,2,128,128]{3,2,1,0:T(8,128)(2,1)S(1)} %copy-done.23), channel_id=1, source_target_pairs={{0,2},{1,3},{2,0},{3,1},{4,6},{5,7},{6,4},{7,5},{8,10},{9,11},{10,... | collective-permute-start | bytes 589832 | tf_op jit(solution)/shard_map/ppermute | solution.py:332
  16.8 23.7 %copy-start.5 = (bf16[3,2,128,128]{3,2,1,0:T(8,128)(2,1)}, bf16[3,2,128,128]{3,2,1,0:T(8,128)(2,1)S(1)}, u32[]{:S(2)}) copy-start(bf16[3,2,128,128]{3,2,1,0:T(8,128)(2,1)S(1)} %collective-permute-done.13.refs_3_) | copy-start | bytes 589828
  16.8 19.6 %collective-permute-start.2 = (bf16[3,2,128,128]{3,2,1,0:T(8,128)(2,1)S(1)}, bf16[3,2,128,128]{3,2,1,0:T(8,128)(2,1)S(1)}, u32[]{:S(2)}, u32[]{:S(2)}) collective-permute-start(bf16[3,2,128,128]{3,2,1,0:T(8,128)(2,1)S(1)} %copy-done.22), channel_id=1, source_target_pairs={{0,3},{1,2},{2,1},{3,0},{4,7},{5,6},{6,5},{7,4},{8,11},{9,10},{10,... | collective-permute-start | bytes 589832 | tf_op jit(solution)/shard_map/ppermute | solution.py:332
  18.8 46.4 %copy-start.4 = (bf16[3,2,128,128]{3,2,1,0:T(8,128)(2,1)}, bf16[3,2,128,128]{3,2,1,0:T(8,128)(2,1)S(1)}, u32[]{:S(2)}) copy-start(bf16[3,2,128,128]{3,2,1,0:T(8,128)(2,1)S(1)} %collective-permute-done.refs_1_) | copy-start | bytes 589828
  18.8 29.8 %collective-permute-start.14 = (bf16[2,352,128]{2,1,0:T(8,128)(2,1)S(1)}, bf16[2,352,128]{2,1,0:T(8,128)(2,1)S(1)}, u32[]{:S(2)}, u32[]{:S(2)}) collective-permute-start(bf16[2,352,128]{2,1,0:T(8,128)(2,1)S(1)} %constant_dynamic-update-slice_fusion.3), channel_id=1, source_target_pairs={{0,4},{4,8},{8,12},{12,16},{16,20},{20,24},{24,28},{1,5},{5,9},{9,... | collective-permute-start | bytes 540680 | tf_op jit(solution)/shard_map/ppermute | solution.py:338
  32.6 32.6 %copy-start.6 = (bf16[3,2,128,128]{3,2,1,0:T(8,128)(2,1)}, bf16[3,2,128,128]{3,2,1,0:T(8,128)(2,1)S(1)}, u32[]{:S(2)}) copy-start(bf16[3,2,128,128]{3,2,1,0:T(8,128)(2,1)S(1)} %collective-permute-done.1.refs_2_) | copy-start | bytes 589828
  36.3 28.9 %copy-start.7 = (bf16[3,2,128,128]{3,2,1,0:T(8,128)(2,1)}, bf16[3,2,128,128]{3,2,1,0:T(8,128)(2,1)S(1)}, u32[]{:S(2)}) copy-start(bf16[3,2,128,128]{3,2,1,0:T(8,128)(2,1)S(1)} %collective-permute-done.2.refs_3_) | copy-start | bytes 589828
  36.4 8.1 %collective-permute-start.5 = (bf16[128,2048]{1,0:T(8,128)(2,1)S(1)}, bf16[128,2048]{1,0:T(8,128)(2,1)S(1)}, u32[]{:S(2)}, u32[]{:S(2)}) collective-permute-start(bf16[128,2048]{1,0:T(8,128)(2,1)S(1)} %collective-permute-done.4.grads), channel_id=1, source_target_pairs={{0,1},{1,0},{2,3},{3,2},{4,5},{5,4},{6,7},{7,6},{8,9},{9,8},{10,11... | collective-permute-start | bytes 1572872 | tf_op jit(solution)/shard_map/ppermute | solution.py:332
  63.9 8.7 %collective-permute-start.15 = (bf16[2,352,128]{2,1,0:T(8,128)(2,1)}, bf16[2,352,128]{2,1,0:T(8,128)(2,1)S(1)}, u32[]{:S(2)}, u32[]{:S(2)}) collective-permute-start(bf16[2,352,128]{2,1,0:T(8,128)(2,1)} %get-tuple-element.40), channel_id=1, source_target_pairs={{4,0},{8,4},{12,8},{16,12},{20,16},{24,20},{28,24},{5,1},{9,5},{13... | collective-permute-start | bytes 540680 | tf_op jit(solution)/shard_map/ppermute | solution.py:338
  65.3 11.3 %collective-permute-start.6 = (bf16[2,352,128]{2,1,0:T(8,128)(2,1)S(1)}, bf16[2,352,128]{2,1,0:T(8,128)(2,1)S(1)}, u32[]{:S(2)}, u32[]{:S(2)}) collective-permute-start(bf16[2,352,128]{2,1,0:T(8,128)(2,1)S(1)} %constant_dynamic-update-slice_fusion), channel_id=1, source_target_pairs={{0,4},{4,8},{8,12},{12,16},{16,20},{20,24},{24,28},{1,5},{5,9},{9,... | collective-permute-start | bytes 540680 | tf_op jit(solution)/shard_map/ppermute | solution.py:338
  75.5 17.7 %copy-start.26 = (bf16[3,2,128,128]{3,2,1,0:T(8,128)(2,1)S(1)}, bf16[3,2,128,128]{3,2,1,0:T(8,128)(2,1)}, u32[]{:S(2)}) copy-start(bf16[3,2,128,128]{3,2,1,0:T(8,128)(2,1)} %get-tuple-element.43) | copy-start | bytes 589828
  75.5 19.3 %copy-start.25 = (bf16[3,2,128,128]{3,2,1,0:T(8,128)(2,1)S(1)}, bf16[3,2,128,128]{3,2,1,0:T(8,128)(2,1)}, u32[]{:S(2)}) copy-start(bf16[3,2,128,128]{3,2,1,0:T(8,128)(2,1)} %get-tuple-element.44) | copy-start | bytes 589828
  75.5 30.2 %collective-permute-start.16 = (bf16[3,2,128,128]{3,2,1,0:T(8,128)(2,1)}, bf16[3,2,128,128]{3,2,1,0:T(8,128)(2,1)S(1)}, u32[]{:S(2)}, u32[]{:S(2)}) collective-permute-start(bf16[3,2,128,128]{3,2,1,0:T(8,128)(2,1)} %get-tuple-element.42), channel_id=1, source_target_pairs={{0,1},{1,0},{2,3},{3,2},{4,5},{5,4},{6,7},{7,6},{8,9},{9,8},{10,11... | collective-permute-start | bytes 589832 | tf_op jit(solution)/shard_map/ppermute | solution.py:332
  91.9 9.3 %collective-permute-start.7 = (bf16[2,352,128]{2,1,0:T(8,128)(2,1)}, bf16[2,352,128]{2,1,0:T(8,128)(2,1)S(1)}, u32[]{:S(2)}, u32[]{:S(2)}) collective-permute-start(bf16[2,352,128]{2,1,0:T(8,128)(2,1)} %get-tuple-element.30), channel_id=1, source_target_pairs={{4,0},{8,4},{12,8},{16,12},{20,16},{24,20},{28,24},{5,1},{9,5},{13... | collective-permute-start | bytes 540680 | tf_op jit(solution)/shard_map/ppermute | solution.py:338
  93.2 13.1 %collective-permute-start.17 = (bf16[3,2,128,128]{3,2,1,0:T(8,128)(2,1)S(1)}, bf16[3,2,128,128]{3,2,1,0:T(8,128)(2,1)S(1)}, u32[]{:S(2)}, u32[]{:S(2)}) collective-permute-start(bf16[3,2,128,128]{3,2,1,0:T(8,128)(2,1)S(1)} %copy-done.26), channel_id=1, source_target_pairs={{0,2},{1,3},{2,0},{3,1},{4,6},{5,7},{6,4},{7,5},{8,10},{9,11},{10,... | collective-permute-start | bytes 589832 | tf_op jit(solution)/shard_map/ppermute | solution.py:332
  94.8 11.5 %collective-permute-start.18 = (bf16[3,2,128,128]{3,2,1,0:T(8,128)(2,1)S(1)}, bf16[3,2,128,128]{3,2,1,0:T(8,128)(2,1)S(1)}, u32[]{:S(2)}, u32[]{:S(2)}) collective-permute-start(bf16[3,2,128,128]{3,2,1,0:T(8,128)(2,1)S(1)} %copy-done.25), channel_id=1, source_target_pairs={{0,3},{1,2},{2,1},{3,0},{4,7},{5,6},{6,5},{7,4},{8,11},{9,10},{10,... | collective-permute-start | bytes 589832 | tf_op jit(solution)/shard_map/ppermute | solution.py:332
  104.1 7.3 %collective-permute-start.10 = (bf16[3,2,128,128]{3,2,1,0:T(8,128)(2,1)}, bf16[3,2,128,128]{3,2,1,0:T(8,128)(2,1)S(1)}, u32[]{:S(2)}, u32[]{:S(2)}) collective-permute-start(bf16[3,2,128,128]{3,2,1,0:T(8,128)(2,1)} %get-tuple-element.34), channel_id=1, source_target_pairs={{0,3},{1,2},{2,1},{3,0},{4,7},{5,6},{6,5},{7,4},{8,11},{9,10},{10,... | collective-permute-start | bytes 589832 | tf_op jit(solution)/shard_map/ppermute | solution.py:332
  104.7 6.7 %collective-permute-start.8 = (bf16[3,2,128,128]{3,2,1,0:T(8,128)(2,1)}, bf16[3,2,128,128]{3,2,1,0:T(8,128)(2,1)S(1)}, u32[]{:S(2)}, u32[]{:S(2)}) collective-permute-start(bf16[3,2,128,128]{3,2,1,0:T(8,128)(2,1)} %get-tuple-element.32), channel_id=1, source_target_pairs={{0,1},{1,0},{2,3},{3,2},{4,5},{5,4},{6,7},{7,6},{8,9},{9,8},{10,11... | collective-permute-start | bytes 589832 | tf_op jit(solution)/shard_map/ppermute | solution.py:332
  105.8 10.0 %copy-start.12 = (bf16[3,2,128,128]{3,2,1,0:T(8,128)(2,1)}, bf16[3,2,128,128]{3,2,1,0:T(8,128)(2,1)S(1)}, u32[]{:S(2)}) copy-start(bf16[3,2,128,128]{3,2,1,0:T(8,128)(2,1)S(1)} %collective-permute-done.16.refs_5_) | copy-start | bytes 589828
  105.8 10.0 %collective-permute-start.9 = (bf16[3,2,128,128]{3,2,1,0:T(8,128)(2,1)}, bf16[3,2,128,128]{3,2,1,0:T(8,128)(2,1)S(1)}, u32[]{:S(2)}, u32[]{:S(2)}) collective-permute-start(bf16[3,2,128,128]{3,2,1,0:T(8,128)(2,1)} %get-tuple-element.33), channel_id=1, source_target_pairs={{0,2},{1,3},{2,0},{3,1},{4,6},{5,7},{6,4},{7,5},{8,10},{9,11},{10,... | collective-permute-start | bytes 589832 | tf_op jit(solution)/shard_map/ppermute | solution.py:332
  106.3 9.5 %copy-start.13 = (bf16[3,2,128,128]{3,2,1,0:T(8,128)(2,1)}, bf16[3,2,128,128]{3,2,1,0:T(8,128)(2,1)S(1)}, u32[]{:S(2)}) copy-start(bf16[3,2,128,128]{3,2,1,0:T(8,128)(2,1)S(1)} %collective-permute-done.17.refs_6_) | copy-start | bytes 589828
  106.3 9.5 %copy-start.14 = (bf16[3,2,128,128]{3,2,1,0:T(8,128)(2,1)}, bf16[3,2,128,128]{3,2,1,0:T(8,128)(2,1)S(1)}, u32[]{:S(2)}) copy-start(bf16[3,2,128,128]{3,2,1,0:T(8,128)(2,1)S(1)} %collective-permute-done.18.refs_7_) | copy-start | bytes 589828
  (14 other events, 32.2 us)

commit v2 on v1

v2 whole, which is shorter than its diff:
```python
import functools
import math

import jax
import jax.numpy as jnp
from jax import lax
from jax.experimental import pallas as pl
from jax.experimental.pallas import tpu as pltpu
from jax.sharding import PartitionSpec as P

KW = 31
MASKB = 512
TILE = 128
PAD = 32
NEG = -1e30
F32 = jnp.float32
BF16 = jnp.bfloat16
MIB = 1024 * 1024
NT = (((1,), (1,)), ((), ()))
TN = (((0,), (0,)), ((), ()))


def call(kernel, mib, **kw):
    return pl.pallas_call(
        kernel,
        compiler_params=pltpu.CompilerParams(vmem_limit_bytes=mib * MIB),
        cost_estimate=pl.CostEstimate(flops=1000, bytes_accessed=1000, transcendentals=0),
        **kw,
    )


def loop(count, body):
    if count <= 4:
        for i in range(count):
            body(i)
    else:
        lax.fori_loop(0, count, lambda i, c: (body(i), c)[1], 0)


def pack_kernel(n_head, n_chunks, src, *refs):
    outs, stage = refs[:-1], refs[-1]
    heads = src.shape[2]
    local = heads // n_head
    per_chunk = local // n_chunks
    me = lax.axis_index("head")
    stage[...] = jnp.swapaxes(src[:, 0], 0, 1)
    for j in range(n_head):
        first = jnp.bitwise_xor(me, j) * local
        for c in range(n_chunks):
            for h in range(per_chunk):
                outs[j * n_chunks + c][0, h] = stage[first + c * per_chunk + h]


def pack(qkv, n_head, n_chunks):
    tokens, parts, heads, dim = qkv.shape
    per_chunk = heads // n_head // n_chunks
    count = n_head * n_chunks
    outs = call(
        functools.partial(pack_kernel, n_head, n_chunks),
        8,
        grid=(parts,),
        in_specs=[pl.BlockSpec((tokens, 1, heads, dim), lambda p: (0, p, 0, 0))],
        out_specs=[pl.BlockSpec((1, per_chunk, tokens, dim), lambda p: (p, 0, 0, 0))] * count,
        out_shape=[jax.ShapeDtypeStruct((parts, per_chunk, tokens, dim), BF16)] * count,
        scratch_shapes=[pltpu.VMEM((heads, tokens, dim), BF16)],
        name="pack",
    )(qkv)
    return [[outs[j * n_chunks + c] for j in range(n_head)] for c in range(n_chunks)]


def unpack_kernel(n_head, n_chunks, *refs):
    srcs, out, stage = refs[:-2], refs[-2], refs[-1]
    heads = out.shape[2]
    local = heads // n_head
    per_chunk = local // n_chunks
    me = lax.axis_index("head")
    for j in range(n_head):
        first = jnp.bitwise_xor(me, j) * local
        for c in range(n_chunks):
            for h in range(per_chunk):
                stage[first + c * per_chunk + h] = srcs[c * n_head + j][0, h]
    out[:, 0] = jnp.swapaxes(stage[...], 0, 1)


def unpack(pieces, n_head, n_chunks):
    parts, per_chunk, tokens, dim = pieces[0][0].shape
    heads = per_chunk * n_chunks * n_head
    flat = [piece for chunk in pieces for piece in chunk]
    return call(
        functools.partial(unpack_kernel, n_head, n_chunks),
        8,
        grid=(parts,),
        in_specs=[pl.BlockSpec((1, per_chunk, tokens, dim), lambda p: (p, 0, 0, 0))] * len(flat),
        out_specs=pl.BlockSpec((tokens, 1, heads, dim), lambda p: (0, p, 0, 0)),
        out_shape=jax.ShapeDtypeStruct((tokens, parts, heads, dim), BF16),
        scratch_shapes=[pltpu.VMEM((heads, tokens, dim), BF16)],
        name="unpack",
    )(*flat)


def dequant_kernel(side, values, scales, weight):
    rows, width = values.shape
    first = lax.axis_index("head") * (rows // side)
    for r in range(rows // side):
        for c in range(width // side):
            block = values[r * side : (r + 1) * side, c * side : (c + 1) * side].astype(F32)
            block = block * scales[first + r, pl.program_id(0) * (width // side) + c]
            weight[c * side : (c + 1) * side, r * side : (r + 1) * side] = block.T.astype(BF16)


def dequantize(values, scales):
    rows, width = values.shape
    side = width // scales.shape[1]
    step = 4 * side
    return call(
        functools.partial(dequant_kernel, side),
        8,
        grid=(width // step,),
        in_specs=[
            pl.BlockSpec((rows, step), lambda i: (0, i)),
            pl.BlockSpec(memory_space=pltpu.SMEM),
        ],
        out_specs=pl.BlockSpec((step, rows), lambda i: (i, 0)),
        out_shape=jax.ShapeDtypeStruct((width, rows), BF16),
        name="dequant",
    )(values, scales)


def dattn_kernel(count, *refs):
    weight = refs[count]
    for grads, out in zip(refs[:count], refs[count + 1 :]):
        out[...] = jnp.dot(grads[...], weight[...], preferred_element_type=F32).astype(BF16)


def d_attn(pieces, weight):
    out = jax.ShapeDtypeStruct((pieces[0].shape[0], weight.shape[1]), BF16)
    return call(
        functools.partial(dattn_kernel, len(pieces)),
        12,
        out_shape=[out] * len(pieces),
        name="dattn",
    )(*pieces, weight)


def spread(totals, taps, head, p, first, rows):
    acc = jnp.zeros((rows, totals.shape[-1]), F32)
    for b in range(8):
        window_rows = totals[p, pl.ds(first + b, rows + 24), :]
        for a in range(4):
            tau = 8 * a + b
            if tau < KW:
                acc = acc + taps[tau, p, pl.ds(head, 1), :] * window_rows[8 * a : 8 * a + rows]
    return acc


def core_kernel(n_head, head0, span, window, offsets, *refs):
    pieces = refs[:n_head]
    grads = refs[n_head : 2 * n_head]
    halo, taps, totals_out, carry_out, ext, mixed, d_out = refs[2 * n_head :]
    totals = totals_out.at[:, 0]
    tokens = pieces[0].shape[2]
    seq_rows = tokens * n_head
    margin = span + PAD
    keys = span + TILE
    dim = pieces[0].shape[3]
    inv_scale = 1.0 / math.sqrt(dim)
    me = lax.axis_index("head")
    seq_index = lax.axis_index("seq")
    head = head0 + pl.program_id(0)
    local = taps.shape[2]

    ext[1, :margin] = halo[0, :margin].astype(F32)
    ext[2, :margin] = halo[0, margin : 2 * margin].astype(F32)
    ext[0, span:margin] = halo[0, 2 * margin :].astype(F32)
    for j in range(n_head):
        start = pl.multiple_of(jnp.bitwise_xor(me, j) * tokens, tokens)
        for p in range(3):
            ext[p, pl.ds(margin + start, tokens), :] = pieces[j][p, 0].astype(F32)
        d_out[pl.ds(start, tokens), :] = grads[j][...]

    def tap(p, tau):
        return taps[tau, p, pl.ds(head, 1), :]

    def conv_block(p, first, rows):
        acc = jnp.zeros((rows, dim), F32)
        for b in range(8):
            window_rows = ext[p, pl.ds(first + 8 - b, rows + 24), :]
            for a in range(4):
                tau = 8 * a + b
                if tau < KW:
                    acc = acc + tap(p, tau) * window_rows[24 - 8 * a : 24 - 8 * a + rows]
        mixed[p, pl.ds(first, rows), :] = acc.astype(BF16)

    def conv_part(p):
        lax.fori_loop(
            0,
            (span + seq_rows) // TILE,
            lambda i, c: (conv_block(p, pl.multiple_of(i * TILE, TILE), TILE), c)[1],
            0,
        )

    lax.fori_loop(1, 3, lambda p, c: (conv_part(p), c)[1], 0)
    lax.fori_loop(
        0,
        seq_rows // TILE,
        lambda i, c: (conv_block(0, pl.multiple_of(span + i * TILE, TILE), TILE), c)[1],
        0,
    )

    totals[1] = jnp.zeros(totals.shape[1:], F32)
    totals[2] = jnp.zeros(totals.shape[1:], F32)
    totals[0, span:margin] = jnp.zeros((PAD, dim), F32)
    totals[0, margin + seq_rows :] = jnp.zeros((PAD, dim), F32)
    row = lax.broadcasted_iota(jnp.int32, (TILE, keys), 0)
    col = lax.broadcasted_iota(jnp.int32, (TILE, keys), 1)
    distance = row + span - col
    base = window[me * local + head]
    blocks = seq_rows // MASKB

    def attend(t):
        first = t * TILE
        reach = base + offsets[seq_index * blocks + first // MASKB]
        limit = jnp.minimum(reach, seq_index * seq_rows + first + row)
        allowed = (distance >= 0) & (distance <= limit)
        q = mixed[0, pl.ds(span + first, TILE), :]
        k = mixed[1, pl.ds(first, keys), :]
        v = mixed[2, pl.ds(first, keys), :]
        o = d_out[pl.ds(first, TILE), :]
        scores = lax.dot_general(q, k, NT, preferred_element_type=F32) * inv_scale
        scores = jnp.where(allowed, scores, NEG)
        top = jnp.max(scores, axis=1, keepdims=True)
        exps = jnp.where(allowed, jnp.exp(scores - top), 0.0)
        probs = exps / jnp.sum(exps, axis=1, keepdims=True)
        d_prob = lax.dot_general(o, v, NT, preferred_element_type=F32)
        delta = jnp.sum(probs * d_prob, axis=1, keepdims=True)
        d_score = (probs * (d_prob - delta) * inv_scale).astype(BF16)
        probs_b = probs.astype(BF16)
        totals[0, pl.ds(margin + first, TILE), :] = jnp.dot(d_score, k, preferred_element_type=F32)
        at = pl.ds(PAD + first, keys)
        totals[1, at, :] += lax.dot_general(d_score, q, TN, preferred_element_type=F32)
        totals[2, at, :] += lax.dot_general(probs_b, o, TN, preferred_element_type=F32)

    loop(seq_rows // TILE, attend)

    carry_out[0, 2 * margin :] = spread(totals, taps, head, 0, span, PAD).astype(BF16)
    for p in (1, 2):
        for first in range(0, margin, PAD):
            at = (p - 1) * margin + first
            carry_out[0, at : at + PAD] = spread(totals, taps, head, p, first, PAD).astype(BF16)


def core(pieces, grads, halo, taps, window, offsets, head0, span):
    n_head = len(pieces)
    parts, heads, tokens, dim = pieces[0].shape
    seq_rows = tokens * n_head
    margin = span + PAD
    return call(
        functools.partial(core_kernel, n_head, head0, span),
        16,
        grid=(heads,),
        in_specs=[pl.BlockSpec(memory_space=pltpu.SMEM)] * 2
        + [pl.BlockSpec((parts, 1, tokens, dim), lambda h: (0, h, 0, 0))] * n_head
        + [pl.BlockSpec((tokens, dim), lambda h: (0, head0 + h))] * n_head
        + [
            pl.BlockSpec((1, 2 * margin + PAD, dim), lambda h: (h, 0, 0)),
            pl.BlockSpec(taps.shape, lambda h: (0, 0, 0, 0)),
        ],
        out_specs=[
            pl.BlockSpec((parts, 1, margin + seq_rows + PAD, dim), lambda h: (0, h, 0, 0)),
            pl.BlockSpec((1, 2 * margin + PAD, dim), lambda h: (h, 0, 0)),
        ],
        out_shape=[
            jax.ShapeDtypeStruct((parts, heads, margin + seq_rows + PAD, dim), F32),
            jax.ShapeDtypeStruct((heads, 2 * margin + PAD, dim), BF16),
        ],
        scratch_shapes=[
            pltpu.VMEM((parts, margin + seq_rows, dim), F32),
            pltpu.VMEM((parts, span + seq_rows, dim), BF16),
            pltpu.VMEM((seq_rows, dim), BF16),
        ],
        name="core",
    )(window, offsets, *pieces, *grads, halo, taps)


def finish_kernel(n_head, head0, span, totals, carry, taps, *refs):
    outs, edge = refs[:-1], refs[-1]
    tokens = outs[0].shape[2]
    seq_rows = tokens * n_head
    margin = span + PAD
    me = lax.axis_index("head")
    head = head0 + pl.program_id(0)
    rows = totals.at[:, 0]

    @pl.when(pl.program_id(0) == 0)
    def _():
        edge[...] = jnp.zeros(edge.shape, F32)

    for p, size, start in ((0, PAD, 2 * margin), (1, margin, 0), (2, margin, margin)):
        edge[p, seq_rows - size :] = carry[0, start : start + size].astype(F32)
    for j in range(n_head):
        start = pl.multiple_of(jnp.bitwise_xor(me, j) * tokens, tokens)

        def part(p, c, j=j, start=start):
            own = spread(rows, taps, head, p, margin + start, tokens)
            outs[j][p, 0] = (own + edge[p, pl.ds(start, tokens), :]).astype(BF16)
            return c

        lax.fori_loop(0, 3, part, 0)


def finish(totals, carry, taps, head0, n_head, span):
    parts, heads, rows, dim = totals.shape
    seq_rows = rows - span - 2 * PAD
    tokens = seq_rows // n_head
    return call(
        functools.partial(finish_kernel, n_head, head0, span),
        16,
        grid=(heads,),
        in_specs=[
            pl.BlockSpec((parts, 1, rows, dim), lambda h: (0, h, 0, 0)),
            pl.BlockSpec((1, carry.shape[1], dim), lambda h: (h, 0, 0)),
            pl.BlockSpec(taps.shape, lambda h: (0, 0, 0, 0)),
        ],
        out_specs=[pl.BlockSpec((parts, 1, tokens, dim), lambda h: (0, h, 0, 0))] * n_head,
        out_shape=[jax.ShapeDtypeStruct((parts, heads, tokens, dim), BF16)] * n_head,
        scratch_shapes=[pltpu.VMEM((parts, seq_rows, dim), F32)],
        name="finish",
    )(totals, carry, taps)


def partner(value, j):
    if j == 0:
        return value
    size = lax.axis_size("head")
    return lax.ppermute(value, "head", [(i, i ^ j) for i in range(size)])


def shifted(value, by):
    length = lax.axis_size("seq")
    pairs = [(i, i + by) for i in range(length) if 0 <= i + by < length]
    return lax.ppermute(value, "seq", pairs)


def tail_of(pieces, p, rows):
    me = lax.axis_index("head")
    n_head = len(pieces)
    tokens = pieces[0].shape[2]
    found = []
    source = n_head - 1
    while rows > 0:
        take = min(rows, tokens)
        parts = [piece[p, :, tokens - take :] for piece in pieces]
        found.insert(0, lax.select_n(jnp.bitwise_xor(me, source), *parts))
        rows -= take
        source -= 1
    return found


def per_device(qkv_pre, grad_out, out_values, out_scales, conv_kernel, window, offsets):
    n_head = lax.axis_size("head")
    tokens, _, heads, dim = qkv_pre.shape
    local = heads // n_head
    n_chunks = 2 if local % 2 == 0 else 1
    per_chunk = local // n_chunks
    seq_rows = tokens * n_head
    span = seq_rows // 4
    margin = span + PAD

    packed = pack(qkv_pre, n_head, n_chunks)
    g_pieces = [grad_out]
    for j in range(1, n_head):
        if j > 1 and j % 2 == 1:
            g_pieces.append(partner(g_pieces[j - 1], 1))
        else:
            g_pieces.append(partner(grad_out, j))
    weight = dequantize(out_values, out_scales)
    grads = []
    for j in range(0, n_head, 2):
        grads += d_attn(g_pieces[j : j + 2], weight)

    carried = []
    for c in range(n_chunks):
        pieces = [partner(packed[c][j], j) for j in range(n_head)]
        tail = jnp.concatenate(
            tail_of(pieces, 1, margin) + tail_of(pieces, 2, margin) + tail_of(pieces, 0, PAD), axis=1
        )
        totals, carry = core(
            pieces, grads, shifted(tail, 1), conv_kernel, window, offsets, c * per_chunk, span
        )
        carried.append((totals, shifted(carry, -1)))
    results = []
    for c, (totals, carry) in enumerate(carried):
        outs = finish(totals, carry, conv_kernel, c * per_chunk, n_head, span)
        results.append([partner(outs[j], j) for j in range(n_head)])
    return unpack(results, n_head, n_chunks)


def solution(mesh):
    return jax.shard_map(
        per_device,
        mesh=mesh,
        in_specs=(
            P(("seq", "head"), None, None, None),
            P(("seq", "head"), None),
            P("head", None),
            P(),
            P(None, None, "head", None),
            P(),
            P(),
        ),
        out_specs=P(("seq", "head"), None, None, None),
        check_vma=False,
    )
```

time: 123 us -> 99.9 us (0.81); the launches traced: 121 us -> 99.5 us
  Pallas kernels: 58.5 us -> 36.3 us
    pallas_call x11 -> x9, Pallas kernels: 58.5 us -> 36.3 us  [the longest x2 19 us: core(): call(functools.partial(core_kernel, n_head, head0, span), 16, grid=(heads...]
    ppermute x15, waiting for transfers between devices: 23.8 us -> 25.5 us  [partner(): return lax.ppermute(value, 'head', [(i, i ^ j) for i in range(size)])]
    ppermute x15, starting transfers between devices: 11.6 us -> 12.9 us  [partner(): return lax.ppermute(value, 'head', [(i, i ^ j) for i in range(size)])]
    unnamed x54 -> x16, local copies, waits for them, and re-layouts: 5.49 us -> 4.39 us
  transfers between devices with their start and end apart: 19 -> 19, of which waited for: 8 -> 7; matrix products, arithmetic and copies ran while one was open for 0% -> 0% of each run, Pallas kernels for 30% -> 23%
where the time goes in v2:
time: 99.9 us; the launch traced here: 99.5 us
  Pallas kernels  36.3 us (36%)
  waiting for transfers between devices  34.8 us (35%)
  starting transfers between devices  23.4 us (23%)
  local copies, waits for them, and re-layouts  4.39 us (4%)
    ppermute x15, waiting for transfers between devices, partner(): return lax.ppermute(value, 'head', [(i, i ^ j) for i in range(size)])  25.5 us
    pallas_call x2, Pallas kernels, core(): call(functools.partial(core_kernel, n_head, head0, span), 16, grid=(heads...  19 us
    ppermute x15, starting transfers between devices, partner(): return lax.ppermute(value, 'head', [(i, i ^ j) for i in range(size)])  12.9 us
    ppermute x4, starting transfers between devices, shifted(): return lax.ppermute(value, 'seq', pairs)  10.6 us
    ppermute x4, waiting for transfers between devices, shifted(): return lax.ppermute(value, 'seq', pairs)  9.23 us
    pallas_call x2, Pallas kernels, finish(): call(functools.partial(finish_kernel, n_head, head0, span), 16, grid=(hea...  8.02 us
    unnamed x16, local copies, waits for them, and re-layouts  4.39 us
    pallas_call x2, Pallas kernels, d_attn(): call(functools.partial(dattn_kernel, len(pieces)), 12, out_shape=[out] *...  3.56 us
  transfers between devices with their start and end apart: 19, of which 7 were waited for; matrix products, arithmetic and copies ran while one was open for 0% of the time, Pallas kernels for 23%

profile of v2, /device:TPU:0, one launch (start us, length us, event | category | flops | bytes accessed | tf_op | source)
XLA Modules:
  0.0 99.5 jit_solution(10590371299563811821)
XLA Ops:
  0.0 1.4 %copy-done.2 = bf16[128,3,16,128]{3,2,1,0:T(8,128)(2,1)S(1)} copy-done((bf16[128,3,16,128]{3,2,1,0:T(8,128)(2,1)S(1)}, bf16[128,3,16,128]{3,2,1,0:T(8,128)(2,1)}, u32[]{:S(2)}) %copy-start.2) | copy-done | bytes 1572888
  1.4 1.9 %pack.1 = (bf16[3,2,128,128]{3,2,1,0:T(8,128)(2,1)S(1)}, bf16[3,2,128,128]{3,2,1,0:T(8,128)(2,1)S(1)}, bf16[3,2,128,128]{3,2,1,0:T(8,128)(2,1)S(1)}, bf16[3,2,12...) custom-call(bf16[128,3,16,128]{3,2,1,0:T(8,128)(2,1)S(1)} %copy-done.2), custom_call_target="tpu_custom_call" | custom-call | flops 1000 | bytes 1000 | tf_op jit(solution)/shard_map/pack/pallas_call | solution.py:58
  3.3 0.7 copy-done.7
  4.5 2.5 %collective-permute-start.12 = (bf16[3,2,128,128]{3,2,1,0:T(8,128)(2,1)}, bf16[3,2,128,128]{3,2,1,0:T(8,128)(2,1)S(1)}, u32[]{:S(2)}, u32[]{:S(2)}) collective-permute-start(bf16[3,2,128,128]{3,2,1,0:T(8,128)(2,1)} %get-tuple-element.45), channel_id=1, source_target_pairs={{0,2},{1,3},{2,0},{3,1},{4,6},{5,7},{6,4},{7,5},{8,10},{9,11},{10,... | collective-permute-start | bytes 589832 | tf_op jit(solution)/shard_map/ppermute | solution.py:335
  7.1 1.7 %collective-permute-start.4 = (bf16[128,2048]{1,0:T(8,128)(2,1)}, bf16[128,2048]{1,0:T(8,128)(2,1)}, u32[]{:S(2)}, u32[]{:S(2)}) collective-permute-start(bf16[128,2048]{1,0:T(8,128)(2,1)} %refs_0_.1), channel_id=1, source_target_pairs={{0,2},{1,3},{2,0},{3,1},{4,6},{5,7},{6,4},{7,5},{8,10},{9,11},{10,... | collective-permute-start | bytes 1572872 | tf_op jit(solution)/shard_map/ppermute | solution.py:335
  8.8 1.6 %copy-done.1 = bf16[512,2048]{1,0:T(8,128)(2,1)S(1)} copy-done((bf16[512,2048]{1,0:T(8,128)(2,1)S(1)}, bf16[512,2048]{1,0:T(8,128)(2,1)}, u32[]{:S(2)}) %copy-start.1) | copy-done | bytes 2097176
  10.4 0.7 copy-done.4
  11.1 1.8 %dequant.1.refs_2_ = bf16[2048,512]{1,0:T(8,128)(2,1)S(1)} custom-call(bf16[512,2048]{1,0:T(8,128)(2,1)S(1)} %copy-done.1, f32[16,16]{1,0:T(8,128)S(1)} %copy-done.4), custom_call_target="tpu_custom_call" | custom-call | flops 1000 | bytes 1000 | tf_op jit(solution)/shard_map/dequant/pallas_call | solution.py:115
  12.9 0.6 collective-permute-start
  13.5 1.4 %collective-permute-start.1 = (bf16[3,2,128,128]{3,2,1,0:T(8,128)(2,1)S(1)}, bf16[3,2,128,128]{3,2,1,0:T(8,128)(2,1)S(1)}, u32[]{:S(2)}, u32[]{:S(2)}) collective-permute-start(bf16[3,2,128,128]{3,2,1,0:T(8,128)(2,1)S(1)} %get-tuple-element.31), channel_id=1, source_target_pairs={{0,2},{1,3},{2,0},{3,1},{4,6},{5,7},{6,4},{7,5},{8,10},{9,11},{10,... | collective-permute-start | bytes 589832 | tf_op jit(solution)/shard_map/ppermute | solution.py:335
  14.9 1.9 %collective-permute-done.13.refs_3_ = bf16[3,2,128,128]{3,2,1,0:T(8,128)(2,1)S(1)} collective-permute-done((bf16[3,2,128,128]{3,2,1,0:T(8,128)(2,1)}, bf16[3,2,128,128]{3,2,1,0:T(8,128)(2,1)S(1)}, u32[]{:S(2)}, u32[]{:S(2)}) %collective-permute-start.13) | collective-permute-done | bytes 196640 | tf_op jit(solution)/shard_map/ppermute | solution.py:335
  16.8 1.7 %collective-permute-start.2 = (bf16[3,2,128,128]{3,2,1,0:T(8,128)(2,1)S(1)}, bf16[3,2,128,128]{3,2,1,0:T(8,128)(2,1)S(1)}, u32[]{:S(2)}, u32[]{:S(2)}) collective-permute-start(bf16[3,2,128,128]{3,2,1,0:T(8,128)(2,1)S(1)} %get-tuple-element.32), channel_id=1, source_target_pairs={{0,3},{1,2},{2,1},{3,0},{4,7},{5,6},{6,5},{7,4},{8,11},{9,10},{10,... | collective-permute-start | bytes 589832 | tf_op jit(solution)/shard_map/ppermute | solution.py:335
  18.7 3.4 %collective-permute-start.14 = (bf16[2,352,128]{2,1,0:T(8,128)(2,1)S(1)}, bf16[2,352,128]{2,1,0:T(8,128)(2,1)S(1)}, u32[]{:S(2)}, u32[]{:S(2)}) collective-permute-start(bf16[2,352,128]{2,1,0:T(8,128)(2,1)S(1)} %constant_dynamic-update-slice_fusion.3), channel_id=1, source_target_pairs={{0,4},{4,8},{8,12},{12,16},{16,20},{20,24},{24,28},{1,5},{5,9},{9,... | collective-permute-start | bytes 540680 | tf_op jit(solution)/shard_map/ppermute | solution.py:341
  22.1 10.5 %collective-permute-done.1.refs_2_ = bf16[3,2,128,128]{3,2,1,0:T(8,128)(2,1)S(1)} collective-permute-done((bf16[3,2,128,128]{3,2,1,0:T(8,128)(2,1)S(1)}, bf16[3,2,128,128]{3,2,1,0:T(8,128)(2,1)S(1)}, u32[]{:S(2)}, u32[]{:S(2)}) %collective-permute-start.1) | collective-permute-done | bytes 196640 | tf_op jit(solution)/shard_map/ppermute | solution.py:335
  32.6 3.8 %collective-permute-done.2.refs_3_ = bf16[3,2,128,128]{3,2,1,0:T(8,128)(2,1)S(1)} collective-permute-done((bf16[3,2,128,128]{3,2,1,0:T(8,128)(2,1)S(1)}, bf16[3,2,128,128]{3,2,1,0:T(8,128)(2,1)S(1)}, u32[]{:S(2)}, u32[]{:S(2)}) %collective-permute-start.2) | collective-permute-done | bytes 196640 | tf_op jit(solution)/shard_map/ppermute | solution.py:335
  36.8 1.8 %dattn.2 = (bf16[128,512]{1,0:T(8,128)(2,1)S(1)}, bf16[128,512]{1,0:T(8,128)(2,1)S(1)}) custom-call(bf16[128,2048]{1,0:T(8,128)(2,1)S(1)} %copy-done.3, bf16[128,2048]{1,0:T(8,128)(2,1)} %collective-permute-done.3.refs_1_, bf16[2048,512]{1,0:T(8,128)(2,1)S(1)} %dequant.1.refs_2_), custom_call_target="tpu_custom_call" | custom-call | flops 1000 | bytes 1000 | tf_op jit(solution)/shard_map/dattn/pallas_call | solution.py:137
  38.7 1.8 %dattn.3 = (bf16[128,512]{1,0:T(8,128)(2,1)S(1)}, bf16[128,512]{1,0:T(8,128)(2,1)S(1)}) custom-call(bf16[128,2048]{1,0:T(8,128)(2,1)} %collective-permute-done.4.refs_0_, bf16[128,2048]{1,0:T(8,128)(2,1)S(1)} %collective-permute-done.5.refs_1_, bf16[2048,512]{1,0:T(8,128)(2,1)S(1)} %dequant.1.refs_2_), custom_call_target="tpu_custom_call" | custom-call | flops 1000 | bytes 1000 | tf_op jit(solution)/shard_map/dattn/pallas_call | solution.py:137
  40.5 9.5 %core.3 = (f32[3,2,704,128]{3,2,1,0:T(8,128)S(1)}, bf16[2,352,128]{2,1,0:T(8,128)(2,1)S(1)}) custom-call(s32[16]{0:T(128)S(1)} %copy-done.5, s32[8]{0:T(128)S(1)} %copy-done.6, bf16[3,2,128,128]{3,2,1,0:T(8,128)(2,1)S(1)} %get-tuple-element.43.refs_0_, bf16[3,2,128,128]{3,2,1,0:T(8,128)(2,1)S(1)} %collective-permute-done.11.refs_1_, ...), custom_call_target="tpu_custom_call" | custom-call | flops 1000 | bytes 1000 | tf_op jit(solution)/shard_map/core/pallas_call | solution.py:257
  50.0 1.3 %collective-permute-start.15 = (bf16[2,352,128]{2,1,0:T(8,128)(2,1)S(1)}, bf16[2,352,128]{2,1,0:T(8,128)(2,1)S(1)}, u32[]{:S(2)}, u32[]{:S(2)}) collective-permute-start(bf16[2,352,128]{2,1,0:T(8,128)(2,1)S(1)} %get-tuple-element.48), channel_id=1, source_target_pairs={{4,0},{8,4},{12,8},{16,12},{20,16},{24,20},{28,24},{5,1},{9,5},{13... | collective-permute-start | bytes 540680 | tf_op jit(solution)/shard_map/ppermute | solution.py:341
  51.4 4.6 %collective-permute-start.6 = (bf16[2,352,128]{2,1,0:T(8,128)(2,1)S(1)}, bf16[2,352,128]{2,1,0:T(8,128)(2,1)S(1)}, u32[]{:S(2)}, u32[]{:S(2)}) collective-permute-start(bf16[2,352,128]{2,1,0:T(8,128)(2,1)S(1)} %constant_dynamic-update-slice_fusion), channel_id=1, source_target_pairs={{0,4},{4,8},{8,12},{12,16},{16,20},{20,24},{24,28},{1,5},{5,9},{9,... | collective-permute-start | bytes 540680 | tf_op jit(solution)/shard_map/ppermute | solution.py:341
  55.9 2.8 %collective-permute-done.15.carry = bf16[2,352,128]{2,1,0:T(8,128)(2,1)S(1)} collective-permute-done((bf16[2,352,128]{2,1,0:T(8,128)(2,1)S(1)}, bf16[2,352,128]{2,1,0:T(8,128)(2,1)S(1)}, u32[]{:S(2)}, u32[]{:S(2)}) %collective-permute-start.15) | collective-permute-done | bytes 180256 | tf_op jit(solution)/shard_map/ppermute | solution.py:341
  58.8 4.0 %finish.3 = (bf16[3,2,128,128]{3,2,1,0:T(8,128)(2,1)S(1)}, bf16[3,2,128,128]{3,2,1,0:T(8,128)(2,1)S(1)}, bf16[3,2,128,128]{3,2,1,0:T(8,128)(2,1)S(1)}, bf16[3,2,128,128]{3,2,1,0:T(8,128)(2,1)S(1)}) custom-call(f32[3,2,704,128]{3,2,1,0:T(8,128)S(1)} %get-tuple-element.47.totals, bf16[2,352,128]{2,1,0:T(8,128)(2,1)S(1)} %collective-permute-done.15.carry, ...), custom_call_target="tpu_custom_call" | custom-call | flops 1000 | bytes 1000 | tf_op jit(solution)/shard_map/finish/pallas_call | solution.py:315
  62.9 9.5 %core.2 = (f32[3,2,704,128]{3,2,1,0:T(8,128)S(1)}, bf16[2,352,128]{2,1,0:T(8,128)(2,1)S(1)}) custom-call(s32[16]{0:T(128)S(1)} %copy-done.5, s32[8]{0:T(128)S(1)} %copy-done.6, bf16[3,2,128,128]{3,2,1,0:T(8,128)(2,1)S(1)} %get-tuple-element.29.refs_0_, bf16[3,2,128,128]{3,2,1,0:T(8,128)(2,1)S(1)} %collective-permute-done.refs_1_, ...), custom_call_target="tpu_custom_call" | custom-call | flops 1000 | bytes 1000 | tf_op jit(solution)/shard_map/core/pallas_call | solution.py:257
  72.4 1.3 %collective-permute-start.7 = (bf16[2,352,128]{2,1,0:T(8,128)(2,1)S(1)}, bf16[2,352,128]{2,1,0:T(8,128)(2,1)S(1)}, u32[]{:S(2)}, u32[]{:S(2)}) collective-permute-start(bf16[2,352,128]{2,1,0:T(8,128)(2,1)S(1)} %get-tuple-element.38), channel_id=1, source_target_pairs={{4,0},{8,4},{12,8},{16,12},{20,16},{24,20},{28,24},{5,1},{9,5},{13... | collective-permute-start | bytes 540680 | tf_op jit(solution)/shard_map/ppermute | solution.py:341
  73.7 1.6 %collective-permute-start.17 = (bf16[3,2,128,128]{3,2,1,0:T(8,128)(2,1)S(1)}, bf16[3,2,128,128]{3,2,1,0:T(8,128)(2,1)S(1)}, u32[]{:S(2)}, u32[]{:S(2)}) collective-permute-start(bf16[3,2,128,128]{3,2,1,0:T(8,128)(2,1)S(1)} %get-tuple-element.51), channel_id=1, source_target_pairs={{0,2},{1,3},{2,0},{3,1},{4,6},{5,7},{6,4},{7,5},{8,10},{9,11},{10,... | collective-permute-start | bytes 589832 | tf_op jit(solution)/shard_map/ppermute | solution.py:335
  75.6 6.4 %collective-permute-done.7.carry = bf16[2,352,128]{2,1,0:T(8,128)(2,1)S(1)} collective-permute-done((bf16[2,352,128]{2,1,0:T(8,128)(2,1)S(1)}, bf16[2,352,128]{2,1,0:T(8,128)(2,1)S(1)}, u32[]{:S(2)}, u32[]{:S(2)}) %collective-permute-start.7) | collective-permute-done | bytes 180256 | tf_op jit(solution)/shard_map/ppermute | solution.py:341
  82.0 4.0 %finish.2 = (bf16[3,2,128,128]{3,2,1,0:T(8,128)(2,1)S(1)}, bf16[3,2,128,128]{3,2,1,0:T(8,128)(2,1)S(1)}, bf16[3,2,128,128]{3,2,1,0:T(8,128)(2,1)S(1)}, bf16[3,2,128,128]{3,2,1,0:T(8,128)(2,1)S(1)}) custom-call(f32[3,2,704,128]{3,2,1,0:T(8,128)S(1)} %get-tuple-element.37.totals, bf16[2,352,128]{2,1,0:T(8,128)(2,1)S(1)} %collective-permute-done.7.carry, ...), custom_call_target="tpu_custom_call" | custom-call | flops 1000 | bytes 1000 | tf_op jit(solution)/shard_map/finish/pallas_call | solution.py:315
  86.0 1.1 %collective-permute-start.10 = (bf16[3,2,128,128]{3,2,1,0:T(8,128)(2,1)S(1)}, bf16[3,2,128,128]{3,2,1,0:T(8,128)(2,1)S(1)}, u32[]{:S(2)}, u32[]{:S(2)}) collective-permute-start(bf16[3,2,128,128]{3,2,1,0:T(8,128)(2,1)S(1)} %get-tuple-element.42), channel_id=1, source_target_pairs={{0,3},{1,2},{2,1},{3,0},{4,7},{5,6},{6,5},{7,4},{8,11},{9,10},{10,... | collective-permute-start | bytes 589832 | tf_op jit(solution)/shard_map/ppermute | solution.py:335
  87.1 0.6 collective-permute-start.8
  88.2 5.0 %collective-permute-done.10.refs_3_ = bf16[3,2,128,128]{3,2,1,0:T(8,128)(2,1)S(1)} collective-permute-done((bf16[3,2,128,128]{3,2,1,0:T(8,128)(2,1)S(1)}, bf16[3,2,128,128]{3,2,1,0:T(8,128)(2,1)S(1)}, u32[]{:S(2)}, u32[]{:S(2)}) %collective-permute-start.10) | collective-permute-done | bytes 196640 | tf_op jit(solution)/shard_map/ppermute | solution.py:335
  93.2 4.3 %collective-permute-done.9.refs_2_ = bf16[3,2,128,128]{3,2,1,0:T(8,128)(2,1)S(1)} collective-permute-done((bf16[3,2,128,128]{3,2,1,0:T(8,128)(2,1)S(1)}, bf16[3,2,128,128]{3,2,1,0:T(8,128)(2,1)S(1)}, u32[]{:S(2)}, u32[]{:S(2)}) %collective-permute-start.9) | collective-permute-done | bytes 196640 | tf_op jit(solution)/shard_map/ppermute | solution.py:335
  97.5 2.0 %unpack.1 = bf16[128,3,16,128]{3,2,1,0:T(8,128)(2,1)} custom-call(bf16[3,2,128,128]{3,2,1,0:T(8,128)(2,1)S(1)} %get-tuple-element.39.refs_0_, bf16[3,2,128,128]{3,2,1,0:T(8,128)(2,1)S(1)} %collective-permute-done.8.refs_1_, bf16[3,2,128,128]{3,2,1,0:T(8,128)(2,1)S(1)} %collective-permute-done.9.refs_2_, ...), custom_call_target="tpu_custom_call" | custom-call | flops 1000 | bytes 1000 | tf_op jit(solution)/shard_map/unpack/pallas_call | solution.py:89
  (41 shorter events, 2.1 us)
Async XLA Ops:
  0.0 1.4 %copy-start.2 = (bf16[128,3,16,128]{3,2,1,0:T(8,128)(2,1)S(1)}, bf16[128,3,16,128]{3,2,1,0:T(8,128)(2,1)}, u32[]{:S(2)}) copy-start(bf16[128,3,16,128]{3,2,1,0:T(8,128)(2,1)} %src.1) | copy-start | bytes 4718596
  3.3 0.7 copy-start.7
  4.0 8.9 %collective-permute-start.11 = (bf16[3,2,128,128]{3,2,1,0:T(8,128)(2,1)}, bf16[3,2,128,128]{3,2,1,0:T(8,128)(2,1)S(1)}, u32[]{:S(2)}, u32[]{:S(2)}) collective-permute-start(bf16[3,2,128,128]{3,2,1,0:T(8,128)(2,1)} %get-tuple-element.44), channel_id=1, source_target_pairs={{0,1},{1,0},{2,3},{3,2},{4,5},{5,4},{6,7},{7,6},{8,9},{9,8},{10,11... | collective-permute-start | bytes 589832 | tf_op jit(solution)/shard_map/ppermute | solution.py:335
  4.5 9.0 %collective-permute-start.12 = (bf16[3,2,128,128]{3,2,1,0:T(8,128)(2,1)}, bf16[3,2,128,128]{3,2,1,0:T(8,128)(2,1)S(1)}, u32[]{:S(2)}, u32[]{:S(2)}) collective-permute-start(bf16[3,2,128,128]{3,2,1,0:T(8,128)(2,1)} %get-tuple-element.45), channel_id=1, source_target_pairs={{0,2},{1,3},{2,0},{3,1},{4,6},{5,7},{6,4},{7,5},{8,10},{9,11},{10,... | collective-permute-start | bytes 589832 | tf_op jit(solution)/shard_map/ppermute | solution.py:335
  7.0 9.8 %collective-permute-start.13 = (bf16[3,2,128,128]{3,2,1,0:T(8,128)(2,1)}, bf16[3,2,128,128]{3,2,1,0:T(8,128)(2,1)S(1)}, u32[]{:S(2)}, u32[]{:S(2)}) collective-permute-start(bf16[3,2,128,128]{3,2,1,0:T(8,128)(2,1)} %get-tuple-element.46), channel_id=1, source_target_pairs={{0,3},{1,2},{2,1},{3,0},{4,7},{5,6},{6,5},{7,4},{8,11},{9,10},{10,... | collective-permute-start | bytes 589832 | tf_op jit(solution)/shard_map/ppermute | solution.py:335
  7.1 29.3 %collective-permute-start.4 = (bf16[128,2048]{1,0:T(8,128)(2,1)}, bf16[128,2048]{1,0:T(8,128)(2,1)}, u32[]{:S(2)}, u32[]{:S(2)}) collective-permute-start(bf16[128,2048]{1,0:T(8,128)(2,1)} %refs_0_.1), channel_id=1, source_target_pairs={{0,2},{1,3},{2,0},{3,1},{4,6},{5,7},{6,4},{7,5},{8,10},{9,11},{10,... | collective-permute-start | bytes 1572872 | tf_op jit(solution)/shard_map/ppermute | solution.py:335
  8.8 28.0 %collective-permute-start.3 = (bf16[128,2048]{1,0:T(8,128)(2,1)}, bf16[128,2048]{1,0:T(8,128)(2,1)}, u32[]{:S(2)}, u32[]{:S(2)}) collective-permute-start(bf16[128,2048]{1,0:T(8,128)(2,1)} %refs_0_.1), channel_id=1, source_target_pairs={{0,1},{1,0},{2,3},{3,2},{4,5},{5,4},{6,7},{7,6},{8,9},{9,8},{10,11... | collective-permute-start | bytes 1572872 | tf_op jit(solution)/shard_map/ppermute | solution.py:335
  8.8 1.6 %copy-start.1 = (bf16[512,2048]{1,0:T(8,128)(2,1)S(1)}, bf16[512,2048]{1,0:T(8,128)(2,1)}, u32[]{:S(2)}) copy-start(bf16[512,2048]{1,0:T(8,128)(2,1)} %values.1) | copy-start | bytes 6291460
  10.4 0.7 copy-start.4
  12.9 23.9 %copy-start.3 = (bf16[128,2048]{1,0:T(8,128)(2,1)S(1)}, bf16[128,2048]{1,0:T(8,128)(2,1)}, u32[]{:S(2)}) copy-start(bf16[128,2048]{1,0:T(8,128)(2,1)} %refs_0_.1) | copy-start | bytes 1572868
  12.9 5.8 %collective-permute-start = (bf16[3,2,128,128]{3,2,1,0:T(8,128)(2,1)}, bf16[3,2,128,128]{3,2,1,0:T(8,128)(2,1)S(1)}, u32[]{:S(2)}, u32[]{:S(2)}) collective-permute-start(bf16[3,2,128,128]{3,2,1,0:T(8,128)(2,1)} %copy-done.7), channel_id=1, source_target_pairs={{0,1},{1,0},{2,3},{3,2},{4,5},{5,4},{6,7},{7,6},{8,9},{9,8},{10,11... | collective-permute-start | bytes 589832 | tf_op jit(solution)/shard_map/ppermute | solution.py:335
  13.5 19.1 %collective-permute-start.1 = (bf16[3,2,128,128]{3,2,1,0:T(8,128)(2,1)S(1)}, bf16[3,2,128,128]{3,2,1,0:T(8,128)(2,1)S(1)}, u32[]{:S(2)}, u32[]{:S(2)}) collective-permute-start(bf16[3,2,128,128]{3,2,1,0:T(8,128)(2,1)S(1)} %get-tuple-element.31), channel_id=1, source_target_pairs={{0,2},{1,3},{2,0},{3,1},{4,6},{5,7},{6,4},{7,5},{8,10},{9,11},{10,... | collective-permute-start | bytes 589832 | tf_op jit(solution)/shard_map/ppermute | solution.py:335
  16.8 19.7 %collective-permute-start.2 = (bf16[3,2,128,128]{3,2,1,0:T(8,128)(2,1)S(1)}, bf16[3,2,128,128]{3,2,1,0:T(8,128)(2,1)S(1)}, u32[]{:S(2)}, u32[]{:S(2)}) collective-permute-start(bf16[3,2,128,128]{3,2,1,0:T(8,128)(2,1)S(1)} %get-tuple-element.32), channel_id=1, source_target_pairs={{0,3},{1,2},{2,1},{3,0},{4,7},{5,6},{6,5},{7,4},{8,11},{9,10},{10,... | collective-permute-start | bytes 589832 | tf_op jit(solution)/shard_map/ppermute | solution.py:335
  18.7 21.8 %collective-permute-start.14 = (bf16[2,352,128]{2,1,0:T(8,128)(2,1)S(1)}, bf16[2,352,128]{2,1,0:T(8,128)(2,1)S(1)}, u32[]{:S(2)}, u32[]{:S(2)}) collective-permute-start(bf16[2,352,128]{2,1,0:T(8,128)(2,1)S(1)} %constant_dynamic-update-slice_fusion.3), channel_id=1, source_target_pairs={{0,4},{4,8},{8,12},{12,16},{16,20},{20,24},{24,28},{1,5},{5,9},{9,... | collective-permute-start | bytes 540680 | tf_op jit(solution)/shard_map/ppermute | solution.py:341
  36.5 2.2 %collective-permute-start.5 = (bf16[128,2048]{1,0:T(8,128)(2,1)}, bf16[128,2048]{1,0:T(8,128)(2,1)S(1)}, u32[]{:S(2)}, u32[]{:S(2)}) collective-permute-start(bf16[128,2048]{1,0:T(8,128)(2,1)} %collective-permute-done.4.refs_0_), channel_id=1, source_target_pairs={{0,1},{1,0},{2,3},{3,2},{4,5},{5,4},{6,7},{7,6},{8,9},{9,8},{10,11... | collective-permute-start | bytes 1572872 | tf_op jit(solution)/shard_map/ppermute | solution.py:335
  38.6 1.9 %copy-start = (f32[31,3,4,128]{3,2,1,0:T(4,128)S(1)}, f32[31,3,4,128]{3,2,1,0:T(4,128)}, u32[]{:S(2)}) copy-start(f32[31,3,4,128]{3,2,1,0:T(4,128)} %taps.3) | copy-start | bytes 571396
  38.6 1.9 %copy-start.5 = (s32[16]{0:T(128)S(1)}, s32[16]{0:T(128)}, u32[]{:S(2)}) copy-start(s32[16]{0:T(128)} %window.3) | copy-start | bytes 196
  38.6 1.9 %copy-start.6 = (s32[8]{0:T(128)S(1)}, s32[8]{0:T(128)}, u32[]{:S(2)}) copy-start(s32[8]{0:T(128)} %offsets.3) | copy-start | bytes 100
  50.0 8.7 %collective-permute-start.15 = (bf16[2,352,128]{2,1,0:T(8,128)(2,1)S(1)}, bf16[2,352,128]{2,1,0:T(8,128)(2,1)S(1)}, u32[]{:S(2)}, u32[]{:S(2)}) collective-permute-start(bf16[2,352,128]{2,1,0:T(8,128)(2,1)S(1)} %get-tuple-element.48), channel_id=1, source_target_pairs={{4,0},{8,4},{12,8},{16,12},{20,16},{24,20},{28,24},{5,1},{9,5},{13... | collective-permute-start | bytes 540680 | tf_op jit(solution)/shard_map/ppermute | solution.py:341
  51.4 11.5 %collective-permute-start.6 = (bf16[2,352,128]{2,1,0:T(8,128)(2,1)S(1)}, bf16[2,352,128]{2,1,0:T(8,128)(2,1)S(1)}, u32[]{:S(2)}, u32[]{:S(2)}) collective-permute-start(bf16[2,352,128]{2,1,0:T(8,128)(2,1)S(1)} %constant_dynamic-update-slice_fusion), channel_id=1, source_target_pairs={{0,4},{4,8},{8,12},{12,16},{16,20},{20,24},{24,28},{1,5},{5,9},{9,... | collective-permute-start | bytes 540680 | tf_op jit(solution)/shard_map/ppermute | solution.py:341
  62.8 24.9 %collective-permute-start.16 = (bf16[3,2,128,128]{3,2,1,0:T(8,128)(2,1)S(1)}, bf16[3,2,128,128]{3,2,1,0:T(8,128)(2,1)S(1)}, u32[]{:S(2)}, u32[]{:S(2)}) collective-permute-start(bf16[3,2,128,128]{3,2,1,0:T(8,128)(2,1)S(1)} %get-tuple-element.50), channel_id=1, source_target_pairs={{0,1},{1,0},{2,3},{3,2},{4,5},{5,4},{6,7},{7,6},{8,9},{9,8},{10,11... | collective-permute-start | bytes 589832 | tf_op jit(solution)/shard_map/ppermute | solution.py:335
  72.4 9.6 %collective-permute-start.7 = (bf16[2,352,128]{2,1,0:T(8,128)(2,1)S(1)}, bf16[2,352,128]{2,1,0:T(8,128)(2,1)S(1)}, u32[]{:S(2)}, u32[]{:S(2)}) collective-permute-start(bf16[2,352,128]{2,1,0:T(8,128)(2,1)S(1)} %get-tuple-element.38), channel_id=1, source_target_pairs={{4,0},{8,4},{12,8},{16,12},{20,16},{24,20},{28,24},{5,1},{9,5},{13... | collective-permute-start | bytes 540680 | tf_op jit(solution)/shard_map/ppermute | solution.py:341
  73.7 14.5 %collective-permute-start.17 = (bf16[3,2,128,128]{3,2,1,0:T(8,128)(2,1)S(1)}, bf16[3,2,128,128]{3,2,1,0:T(8,128)(2,1)S(1)}, u32[]{:S(2)}, u32[]{:S(2)}) collective-permute-start(bf16[3,2,128,128]{3,2,1,0:T(8,128)(2,1)S(1)} %get-tuple-element.51), channel_id=1, source_target_pairs={{0,2},{1,3},{2,0},{3,1},{4,6},{5,7},{6,4},{7,5},{8,10},{9,11},{10,... | collective-permute-start | bytes 589832 | tf_op jit(solution)/shard_map/ppermute | solution.py:335
  75.3 12.9 %collective-permute-start.18 = (bf16[3,2,128,128]{3,2,1,0:T(8,128)(2,1)S(1)}, bf16[3,2,128,128]{3,2,1,0:T(8,128)(2,1)S(1)}, u32[]{:S(2)}, u32[]{:S(2)}) collective-permute-start(bf16[3,2,128,128]{3,2,1,0:T(8,128)(2,1)S(1)} %get-tuple-element.52), channel_id=1, source_target_pairs={{0,3},{1,2},{2,1},{3,0},{4,7},{5,6},{6,5},{7,4},{8,11},{9,10},{10,... | collective-permute-start | bytes 589832 | tf_op jit(solution)/shard_map/ppermute | solution.py:335
  86.0 7.2 %collective-permute-start.10 = (bf16[3,2,128,128]{3,2,1,0:T(8,128)(2,1)S(1)}, bf16[3,2,128,128]{3,2,1,0:T(8,128)(2,1)S(1)}, u32[]{:S(2)}, u32[]{:S(2)}) collective-permute-start(bf16[3,2,128,128]{3,2,1,0:T(8,128)(2,1)S(1)} %get-tuple-element.42), channel_id=1, source_target_pairs={{0,3},{1,2},{2,1},{3,0},{4,7},{5,6},{6,5},{7,4},{8,11},{9,10},{10,... | collective-permute-start | bytes 589832 | tf_op jit(solution)/shard_map/ppermute | solution.py:335
  87.1 6.1 %collective-permute-start.8 = (bf16[3,2,128,128]{3,2,1,0:T(8,128)(2,1)S(1)}, bf16[3,2,128,128]{3,2,1,0:T(8,128)(2,1)S(1)}, u32[]{:S(2)}, u32[]{:S(2)}) collective-permute-start(bf16[3,2,128,128]{3,2,1,0:T(8,128)(2,1)S(1)} %get-tuple-element.40), channel_id=1, source_target_pairs={{0,1},{1,0},{2,3},{3,2},{4,5},{5,4},{6,7},{7,6},{8,9},{9,8},{10,11... | collective-permute-start | bytes 589832 | tf_op jit(solution)/shard_map/ppermute | solution.py:335
  87.7 9.8 %collective-permute-start.9 = (bf16[3,2,128,128]{3,2,1,0:T(8,128)(2,1)S(1)}, bf16[3,2,128,128]{3,2,1,0:T(8,128)(2,1)S(1)}, u32[]{:S(2)}, u32[]{:S(2)}) collective-permute-start(bf16[3,2,128,128]{3,2,1,0:T(8,128)(2,1)S(1)} %get-tuple-element.41), channel_id=1, source_target_pairs={{0,2},{1,3},{2,0},{3,1},{4,6},{5,7},{6,4},{7,5},{8,10},{9,11},{10,... | collective-permute-start | bytes 589832 | tf_op jit(solution)/shard_map/ppermute | solution.py:335

commit v3 on v2

v3 whole, which is shorter than its diff:
```python
import functools
import math

import jax
import jax.numpy as jnp
from jax import lax
from jax.experimental import pallas as pl
from jax.experimental.pallas import tpu as pltpu
from jax.sharding import PartitionSpec as P

KW = 31
MASKB = 512
TILE = 128
PAD = 32
NEG = -1e30
F32 = jnp.float32
BF16 = jnp.bfloat16
MIB = 1024 * 1024
NT = (((1,), (1,)), ((), ()))
TN = (((0,), (0,)), ((), ()))


def call(kernel, mib, cost, **kw):
    estimate = pl.CostEstimate(
        flops=int(cost * 1e9), bytes_accessed=int(cost * 3e6), transcendentals=0
    )
    return pl.pallas_call(
        kernel,
        compiler_params=pltpu.CompilerParams(vmem_limit_bytes=mib * MIB),
        cost_estimate=estimate,
        **kw,
    )


def loop(count, body):
    if count <= 4:
        for i in range(count):
            body(i)
    else:
        lax.fori_loop(0, count, lambda i, c: (body(i), c)[1], 0)


def pack_kernel(n_head, n_chunks, src, *refs):
    near, far, stage = refs[: n_head // 2], refs[n_head // 2 : -1], refs[-1]
    local = src.shape[2] // n_head
    per_chunk = local // n_chunks
    me = lax.axis_index("head")
    stage[...] = jnp.swapaxes(src[:, 0], 0, 1)
    for j in range(n_head):
        first = jnp.bitwise_xor(me, j) * local
        for h in range(local):
            block = stage[first + h]
            if j < n_head // 2:
                near[j][0, h] = block
            else:
                at = (h // per_chunk) * (n_head // 2) + j - n_head // 2
                far[at][0, h % per_chunk] = block


def pack(qkv, n_head, n_chunks):
    tokens, parts, heads, dim = qkv.shape
    half = n_head // 2
    sizes = [heads // n_head] * half + [heads // n_head // n_chunks] * (half * n_chunks)
    outs = call(
        functools.partial(pack_kernel, n_head, n_chunks),
        8,
        2,
        grid=(parts,),
        in_specs=[pl.BlockSpec((tokens, 1, heads, dim), lambda p: (0, p, 0, 0))],
        out_specs=[pl.BlockSpec((1, size, tokens, dim), lambda p: (p, 0, 0, 0)) for size in sizes],
        out_shape=[jax.ShapeDtypeStruct((parts, size, tokens, dim), BF16) for size in sizes],
        scratch_shapes=[pltpu.VMEM((heads, tokens, dim), BF16)],
        name="pack",
    )(qkv)
    outs = list(outs)
    return outs[:half], [outs[half * (c + 1) : half * (c + 2)] for c in range(n_chunks)]


def unpack_kernel(n_head, n_chunks, *refs):
    srcs, out, stage = refs[:-2], refs[-2], refs[-1]
    heads = out.shape[2]
    local = heads // n_head
    per_chunk = local // n_chunks
    me = lax.axis_index("head")
    for j in range(n_head):
        first = jnp.bitwise_xor(me, j) * local
        for c in range(n_chunks):
            for h in range(per_chunk):
                stage[first + c * per_chunk + h] = srcs[c * n_head + j][0, h]
    out[:, 0] = jnp.swapaxes(stage[...], 0, 1)


def unpack(pieces, n_head, n_chunks):
    parts, per_chunk, tokens, dim = pieces[0][0].shape
    heads = per_chunk * n_chunks * n_head
    flat = [piece for chunk in pieces for piece in chunk]
    return call(
        functools.partial(unpack_kernel, n_head, n_chunks),
        8,
        2,
        grid=(parts,),
        in_specs=[pl.BlockSpec((1, per_chunk, tokens, dim), lambda p: (p, 0, 0, 0))] * len(flat),
        out_specs=pl.BlockSpec((tokens, 1, heads, dim), lambda p: (0, p, 0, 0)),
        out_shape=jax.ShapeDtypeStruct((tokens, parts, heads, dim), BF16),
        scratch_shapes=[pltpu.VMEM((heads, tokens, dim), BF16)],
        name="unpack",
    )(*flat)


def dequant_kernel(side, values, scales, weight):
    rows, width = values.shape
    first = lax.axis_index("head") * (rows // side)
    for r in range(rows // side):
        for c in range(width // side):
            block = values[r * side : (r + 1) * side, c * side : (c + 1) * side].astype(F32)
            block = block * scales[first + r, pl.program_id(0) * (width // side) + c]
            weight[c * side : (c + 1) * side, r * side : (r + 1) * side] = block.T.astype(BF16)


def dequantize(values, scales):
    rows, width = values.shape
    side = width // scales.shape[1]
    step = 4 * side
    return call(
        functools.partial(dequant_kernel, side),
        8,
        2,
        grid=(width // step,),
        in_specs=[
            pl.BlockSpec((rows, step), lambda i: (0, i)),
            pl.BlockSpec(memory_space=pltpu.SMEM),
        ],
        out_specs=pl.BlockSpec((step, rows), lambda i: (i, 0)),
        out_shape=jax.ShapeDtypeStruct((width, rows), BF16),
        name="dequant",
    )(values, scales)


def dattn_kernel(count, *refs):
    weight = refs[count]
    for grads, out in zip(refs[:count], refs[count + 1 :]):
        out[...] = jnp.dot(grads[...], weight[...], preferred_element_type=F32).astype(BF16)


def d_attn(pieces, weight):
    out = jax.ShapeDtypeStruct((pieces[0].shape[0], weight.shape[1]), BF16)
    return call(
        functools.partial(dattn_kernel, len(pieces)),
        12,
        1.5,
        out_shape=[out] * len(pieces),
        name="dattn",
    )(*pieces, weight)


def spread(totals, taps, head, p, first, rows):
    acc = jnp.zeros((rows, totals.shape[-1]), F32)
    for b in range(8):
        window_rows = totals[p, pl.ds(first + b, rows + 24), :]
        for a in range(4):
            tau = 8 * a + b
            if tau < KW:
                acc = acc + taps[tau, p, pl.ds(head, 1), :] * window_rows[8 * a : 8 * a + rows]
    return acc


def convolve(ext, taps, head, p, first, rows):
    acc = jnp.zeros((rows, ext.shape[-1]), F32)
    for b in range(8):
        window_rows = ext[p, pl.ds(first + 8 - b, rows + 24), :]
        for a in range(4):
            tau = 8 * a + b
            if tau < KW:
                at = 24 - 8 * a
                acc = acc + taps[tau, p, pl.ds(head, 1), :] * window_rows[at : at + rows]
    return acc.astype(BF16)


def steps(rows):
    return 112 if rows % 112 == 0 else PAD


def near_kernel(n_head, taps, *refs):
    pieces, mixed, ext = refs[: n_head // 2], *refs[n_head // 2 :]
    tokens = pieces[0].shape[2]
    half = tokens * len(pieces)
    me = lax.axis_index("head")
    head = pl.program_id(0)
    for j, piece in enumerate(pieces):
        start = pl.multiple_of(jnp.bitwise_xor(me % len(pieces), j) * tokens, tokens)
        for p in range(3):
            ext[p, pl.ds(start, tokens), :] = piece[p, 0].astype(F32)
    size = steps(half - PAD)
    blocks = (half - PAD) // size

    def block(i, c):
        first = pl.multiple_of(lax.rem(i, blocks) * size, 16)
        p = i // blocks
        mixed[p, 0, pl.ds(first, size), :] = convolve(ext, taps, head, p, first, size)
        return c

    lax.fori_loop(0, 3 * blocks, block, 0)


def conv_near(pieces, taps):
    parts, heads, tokens, dim = pieces[0].shape
    half = tokens * len(pieces)
    return call(
        functools.partial(near_kernel, 2 * len(pieces)),
        16,
        heads,
        grid=(heads,),
        in_specs=[pl.BlockSpec(taps.shape, lambda h: (0, 0, 0, 0))]
        + [pl.BlockSpec((parts, 1, tokens, dim), lambda h: (0, h, 0, 0))] * len(pieces),
        out_specs=pl.BlockSpec((parts, 1, half - PAD, dim), lambda h: (0, h, 0, 0)),
        out_shape=jax.ShapeDtypeStruct((parts, heads, half - PAD, dim), BF16),
        scratch_shapes=[pltpu.VMEM((parts, half, dim), F32)],
        name="conv_near",
    )(taps, *pieces)


def far_kernel(n_head, head0, taps, *refs):
    pieces, mixed, middle, first_rows, ext = refs[:n_head], *refs[n_head:]
    tokens = pieces[0].shape[2]
    half = tokens * n_head // 2
    me = lax.axis_index("head")
    head = head0 + pl.program_id(0)
    for j in range(n_head):
        start = pl.multiple_of(jnp.bitwise_xor(me, j) * tokens, tokens)
        for p in range(3):
            ext[p, pl.ds(start, tokens), :] = pieces[j][p, 0].astype(F32)
    size = steps(half - PAD)
    blocks = (half - PAD) // size
    base = jnp.where(me < n_head // 2, half, 0)

    def block(i, c):
        first = pl.multiple_of(lax.rem(i, blocks) * size, 16)
        p = i // blocks
        at = pl.multiple_of(base + first, 16)
        mixed[p, 0, pl.ds(first, size), :] = convolve(ext, taps, head, p, at, size)
        return c

    lax.fori_loop(0, 3 * blocks, block, 0)
    for p in range(3):
        middle[p, 0] = convolve(ext, taps, head, p, half - PAD, PAD)
        first_rows[p, 0] = ext[p, :PAD].astype(BF16)


def conv_far(near, far, taps, head0):
    n_head = len(near) + len(far)
    parts, heads, tokens, dim = far[0].shape
    half = tokens * n_head // 2
    sizes = (half - PAD, PAD, PAD)
    return call(
        functools.partial(far_kernel, n_head, head0),
        16,
        heads,
        grid=(heads,),
        in_specs=[pl.BlockSpec(taps.shape, lambda h: (0, 0, 0, 0))]
        + [pl.BlockSpec((parts, 1, tokens, dim), lambda h: (0, head0 + h, 0, 0))] * len(near)
        + [pl.BlockSpec((parts, 1, tokens, dim), lambda h: (0, h, 0, 0))] * len(far),
        out_specs=[pl.BlockSpec((parts, 1, rows, dim), lambda h: (0, h, 0, 0)) for rows in sizes],
        out_shape=[jax.ShapeDtypeStruct((parts, heads, rows, dim), BF16) for rows in sizes],
        scratch_shapes=[pltpu.VMEM((parts, 2 * half, dim), F32)],
        name="conv_far",
    )(taps, *near, *far)


def attn_kernel(n_head, head0, span, window, offsets, near, far, middle, first_rows, halo, taps, *refs):
    grads = refs[:n_head]
    totals_out, carry_out, ext, mixed, d_out = refs[n_head:]
    totals = totals_out.at[:, 0]
    tokens, dim = grads[0].shape
    seq_rows = tokens * n_head
    half = seq_rows // 2
    margin = span + PAD
    keys = span + TILE
    scale = 1.0 / math.sqrt(dim)
    me = lax.axis_index("head")
    seq_index = lax.axis_index("seq")
    head = head0 + pl.program_id(0)
    local = taps.shape[2]

    keep = seq_index > 0
    ext[1, :margin] = jnp.where(keep, halo[0, :margin].astype(F32), 0.0)
    ext[2, :margin] = jnp.where(keep, halo[0, margin : 2 * margin].astype(F32), 0.0)
    ext[0, span:margin] = jnp.where(keep, halo[0, 2 * margin :].astype(F32), 0.0)
    here = jnp.where(me < n_head // 2, 0, half)
    for p in range(3):
        ext[p, margin:] = first_rows[p, 0].astype(F32)
        mixed[p, pl.ds(pl.multiple_of(margin + here, PAD), half - PAD), :] = near[p, 0]
        mixed[p, pl.ds(pl.multiple_of(margin + half - here, PAD), half - PAD), :] = far[p, 0]
        mixed[p, span + half : margin + half] = middle[p, 0]
    mixed[0, span:margin] = convolve(ext, taps, head, 0, span, PAD)
    size = 5 * PAD if margin % (5 * PAD) == 0 else PAD
    for p in (1, 2):
        for first in range(0, margin, size):
            mixed[p, first : first + size] = convolve(ext, taps, head, p, first, size)
    for j in range(n_head):
        start = pl.multiple_of(jnp.bitwise_xor(me, j) * tokens, tokens)
        d_out[pl.ds(start, tokens), :] = grads[j][...]

    totals[1] = jnp.zeros(totals.shape[1:], F32)
    totals[2] = jnp.zeros(totals.shape[1:], F32)
    row = lax.broadcasted_iota(jnp.int32, (TILE, keys), 0)
    col = lax.broadcasted_iota(jnp.int32, (TILE, keys), 1)
    distance = row + span - col
    base = window[me * local + head]
    blocks = seq_rows // MASKB

    def attend(t):
        first = t * TILE
        reach = base + offsets[seq_index * blocks + first // MASKB]
        limit = jnp.minimum(reach, seq_index * seq_rows + first + row)
        allowed = (distance >= 0) & (distance <= limit)
        q = mixed[0, pl.ds(span + first, TILE), :]
        k = mixed[1, pl.ds(first, keys), :]
        v = mixed[2, pl.ds(first, keys), :]
        o = d_out[pl.ds(first, TILE), :]
        scores = lax.dot_general(q, k, NT, preferred_element_type=F32)
        d_prob = lax.dot_general(o, v, NT, preferred_element_type=F32)
        scores = jnp.where(allowed, scores, NEG)
        top = jnp.max(scores, axis=1, keepdims=True)
        exps = jnp.exp((scores - top) * scale)
        probs = exps * (1.0 / jnp.sum(exps, axis=1, keepdims=True))
        delta = jnp.sum(probs * d_prob, axis=1, keepdims=True)
        d_score = (probs * ((d_prob - delta) * scale)).astype(BF16)
        probs_b = probs.astype(BF16)
        totals[0, pl.ds(span + first, TILE), :] = jnp.dot(d_score, k, preferred_element_type=F32)
        at = pl.ds(first, keys)
        totals[1, at, :] += lax.dot_general(d_score, q, TN, preferred_element_type=F32)
        totals[2, at, :] += lax.dot_general(probs_b, o, TN, preferred_element_type=F32)

    loop(seq_rows // TILE, attend)

    carry_out[0, :span] = totals[1, :span].astype(BF16)
    carry_out[0, span : 2 * span] = totals[2, :span].astype(BF16)
    for p in range(3):
        at = 2 * span + p * PAD
        carry_out[0, at : at + PAD] = totals[p, span:margin].astype(BF16)


def attention(near, far_parts, halo, grads, taps, window, offsets, head0, span):
    parts, heads, rows, dim = far_parts[0].shape
    seq_rows = 2 * (rows + PAD)
    n_head = len(grads)
    tokens = seq_rows // n_head
    margin = span + PAD
    edge = 2 * span + 3 * PAD
    mine = lambda h: (0, h, 0, 0)
    return call(
        functools.partial(attn_kernel, n_head, head0, span),
        16,
        2.5 * heads,
        grid=(heads,),
        in_specs=[pl.BlockSpec(memory_space=pltpu.SMEM)] * 2
        + [
            pl.BlockSpec((parts, 1, rows, dim), lambda h: (0, head0 + h, 0, 0)),
            pl.BlockSpec((parts, 1, rows, dim), mine),
            pl.BlockSpec((parts, 1, PAD, dim), mine),
            pl.BlockSpec((parts, 1, PAD, dim), mine),
            pl.BlockSpec((1, 2 * margin + PAD, dim), lambda h: (h, 0, 0)),
            pl.BlockSpec(taps.shape, lambda h: (0, 0, 0, 0)),
        ]
        + [pl.BlockSpec((tokens, dim), lambda h: (0, head0 + h))] * n_head,
        out_specs=[
            pl.BlockSpec((parts, 1, span + seq_rows, dim), mine),
            pl.BlockSpec((1, edge, dim), lambda h: (h, 0, 0)),
        ],
        out_shape=[
            jax.ShapeDtypeStruct((parts, heads, span + seq_rows, dim), F32),
            jax.ShapeDtypeStruct((heads, edge, dim), BF16),
        ],
        scratch_shapes=[
            pltpu.VMEM((parts, margin + PAD, dim), F32),
            pltpu.VMEM((parts, span + seq_rows, dim), BF16),
            pltpu.VMEM((seq_rows, dim), BF16),
        ],
        name="attention",
    )(window, offsets, near, *far_parts, halo, taps, *grads)


def finish_kernel(n_head, head0, span, totals, carry, taps, *refs):
    outs, rows = refs[:-1], refs[-1]
    tokens = outs[0].shape[2]
    seq_rows = tokens * n_head
    me = lax.axis_index("head")
    head = head0 + pl.program_id(0)
    inner = lax.axis_index("seq") < lax.axis_size("seq") - 1

    rows[0, :seq_rows] = totals[0, 0, span:]
    for p in (1, 2):
        edge = seq_rows - span
        back = carry[0, (p - 1) * span : p * span].astype(F32)
        rows[p, :edge] = totals[p, 0, span:seq_rows]
        rows[p, edge:seq_rows] = totals[p, 0, seq_rows:] + jnp.where(inner, back, 0.0)
    for p in range(3):
        at = 2 * span + p * PAD
        rows[p, seq_rows:] = jnp.where(inner, carry[0, at : at + PAD].astype(F32), 0.0)
    for j in range(n_head):
        start = pl.multiple_of(jnp.bitwise_xor(me, j) * tokens, tokens)

        def part(p, c, j=j, start=start):
            outs[j][p, 0] = spread(rows, taps, head, p, start, tokens).astype(BF16)
            return c

        lax.fori_loop(0, 3, part, 0)


def finish(totals, carry, taps, head0, n_head, span):
    parts, heads, rows, dim = totals.shape
    seq_rows = rows - span
    tokens = seq_rows // n_head
    return call(
        functools.partial(finish_kernel, n_head, head0, span),
        16,
        2 * heads,
        grid=(heads,),
        in_specs=[
            pl.BlockSpec((parts, 1, rows, dim), lambda h: (0, h, 0, 0)),
            pl.BlockSpec((1, carry.shape[1], dim), lambda h: (h, 0, 0)),
            pl.BlockSpec(taps.shape, lambda h: (0, 0, 0, 0)),
        ],
        out_specs=[pl.BlockSpec((parts, 1, tokens, dim), lambda h: (0, h, 0, 0))] * n_head,
        out_shape=[jax.ShapeDtypeStruct((parts, heads, tokens, dim), BF16)] * n_head,
        scratch_shapes=[pltpu.VMEM((parts, seq_rows + PAD, dim), F32)],
        name="finish",
    )(totals, carry, taps)


def partner(value, j):
    if j == 0:
        return value
    size = lax.axis_size("head")
    return lax.ppermute(value, "head", [(i, i ^ j) for i in range(size)])


def shifted(value, by):
    length = lax.axis_size("seq")
    pairs = [(i, (i + by) % length) for i in range(length)]
    return lax.ppermute(value, "seq", pairs)


def tail_kernel(n_head, head0, span, *refs):
    pieces, out, sems = refs[:n_head], refs[n_head], refs[n_head + 1]
    tokens = pieces[0].shape[2]
    heads = out.shape[0]
    margin = span + PAD
    me = lax.axis_index("head")
    moves = []
    for p, rows, at in ((1, margin, 0), (2, margin, margin), (0, PAD, 2 * margin)):
        source = n_head - 1
        while rows > 0:
            take = min(rows, tokens)
            rows -= take
            moves.append((p, source, take, at + rows))
            source -= 1

    def move(i, j):
        p, _, take, at = moves[i]
        first = head0 if j < n_head // 2 else 0
        return pltpu.make_async_copy(
            pieces[j].at[p, first : first + heads, tokens - take :],
            out.at[:, at : at + take],
            sems.at[i],
        )

    for i, (_, source, _, _) in enumerate(moves):
        for j in range(n_head):
            pl.when(me == source ^ j)(lambda i=i, j=j: move(i, j).start())
    for i in range(len(moves)):
        move(i, 0).wait()


def tail_of(near, far, head0, span):
    pieces = list(near) + list(far)
    _, heads, tokens, dim = far[0].shape
    margin = span + PAD
    count = 2 * -(-margin // tokens) + 1
    return call(
        functools.partial(tail_kernel, len(pieces), head0, span),
        8,
        0.5,
        in_specs=[pl.BlockSpec(memory_space=pl.ANY)] * len(pieces),
        out_specs=pl.BlockSpec(memory_space=pl.ANY),
        out_shape=jax.ShapeDtypeStruct((heads, 2 * margin + PAD, dim), BF16),
        scratch_shapes=[pltpu.SemaphoreType.DMA((count,))],
        name="tail",
    )(*pieces)


def tied(*values):
    return lax.optimization_barrier(values)


def per_device(qkv_pre, grad_out, out_values, out_scales, conv_kernel, window, offsets):
    n_head = lax.axis_size("head")
    tokens, _, heads, dim = qkv_pre.shape
    local = heads // n_head
    n_chunks = 2 if local % 2 == 0 else 1
    per_chunk = local // n_chunks
    half = n_head // 2
    span = tokens * n_head // 4

    g_near = [partner(grad_out, j) for j in range(half)]
    g_far = partner(grad_out, half)
    near, far = pack(qkv_pre, n_head, n_chunks)
    near = [partner(near[j], j) for j in range(half)]
    far = [[partner(far[c][j], half + j) for j in range(half)] for c in range(n_chunks)]
    near, values, g_near = tied(near, out_values, g_near)
    weight = dequantize(values, out_scales)
    grads = list(d_attn(g_near, weight))
    near, grads = tied(near, grads)
    mixed_near = conv_near(near, conv_kernel)
    far[0], g_far, mixed_near = tied(far[0], g_far, mixed_near)

    def halo_of(c):
        tail = tail_of(near, far[c], c * per_chunk, span)
        far[c], tail = tied(far[c], tail)
        return shifted(tail, 1)

    halo = halo_of(0)
    g_rest = [partner(g_far, j) for j in range(1, half)]
    parts = conv_far(near, far[0], conv_kernel, 0)
    g_rest, parts = tied(g_rest, parts)
    grads += list(d_attn([g_far] + g_rest, weight))
    parts, grads, halo = tied(parts, grads, halo)
    held = []
    for c in range(n_chunks):
        if c + 1 < n_chunks:
            far[c + 1], halo, parts = tied(far[c + 1], halo, parts)
            later = halo_of(c + 1)
        totals, carry = attention(
            mixed_near, parts, halo, grads, conv_kernel, window, offsets, c * per_chunk, span
        )
        if c + 1 < n_chunks:
            halo, totals, carry, near = tied(later, totals, carry, near)
            parts = conv_far(near, far[c + 1], conv_kernel, (c + 1) * per_chunk)
        held.append((totals, shifted(carry, -1)))
    results = []
    held[0], last = tied(held[0], held[-1][0])
    for c in range(n_chunks):
        outs = finish(*held[c], conv_kernel, c * per_chunk, n_head, span)
        if c > 0:
            sent, outs = tied(results[c - 1][: half + 1], outs)
            results[c - 1][: half + 1] = sent
        if c + 1 < n_chunks:
            outs, totals = tied(outs, held[c + 1][0])
            held[c + 1] = (totals, held[c + 1][1])
        results.append([partner(outs[j], j) for j in range(n_head)])
    return unpack(results, n_head, n_chunks)


def solution(mesh):
    return jax.shard_map(
        per_device,
        mesh=mesh,
        in_specs=(
            P(("seq", "head"), None, None, None),
            P(("seq", "head"), None),
            P("head", None),
            P(),
            P(None, None, "head", None),
            P(),
            P(),
        ),
        out_specs=P(("seq", "head"), None, None, None),
        check_vma=False,
    )
```

time: 99.9 us -> 83.9 us (0.84)
  starting transfers between devices: 23.4 us -> 14.7 us
  local copies, waits for them, and re-layouts: 4.39 us -> 1.77 us
  Pallas kernels: 36.3 us -> 34.2 us
  waiting for transfers between devices: 34.8 us -> 32.9 us
    ppermute x4, starting transfers between devices: 10.6 us -> 4.28 us  [shifted(): return lax.ppermute(value, 'seq', pairs)]
    unnamed x16 -> x14, local copies, waits for them, and re-layouts: 4.39 us -> 1.77 us
    ppermute x15 -> x14, starting transfers between devices: 12.9 us -> 10.4 us  [partner(): return lax.ppermute(value, 'head', [(i, i ^ j) for i in range(size)])]
    pallas_call x9 -> x14, Pallas kernels: 36.3 us -> 34.2 us  [the longest x2 11 us: attention(): call(functools.partial(attn_kernel, n_head, head0, span), 16, 2.5 * heads...]
    ppermute x15 -> x14, waiting for transfers between devices: 25.5 us -> 24.2 us  [partner(): return lax.ppermute(value, 'head', [(i, i ^ j) for i in range(size)])]
  transfers between devices with their start and end apart: 19 -> 18, of which waited for: 7 -> 8; matrix products, arithmetic and copies ran while one was open for 0% -> 0% of each run, Pallas kernels for 23% -> 38%
where the time goes in v3:
time: 83.9 us; the launch traced here: 83.7 us
  Pallas kernels  34.2 us (41%)
  waiting for transfers between devices  32.9 us (39%)
  starting transfers between devices  14.7 us (18%)
  local copies, waits for them, and re-layouts  1.77 us (2%)
    ppermute x14, waiting for transfers between devices, partner(): return lax.ppermute(value, 'head', [(i, i ^ j) for i in range(size)])  24.2 us
    pallas_call x2, Pallas kernels, attention(): call(functools.partial(attn_kernel, n_head, head0, span), 16, 2.5 * heads...  11 us
    ppermute x14, starting transfers between devices, partner(): return lax.ppermute(value, 'head', [(i, i ^ j) for i in range(size)])  10.4 us
    ppermute x4, waiting for transfers between devices, shifted(): return lax.ppermute(value, 'seq', pairs)  8.72 us
    pallas_call x2, Pallas kernels, finish(): call(functools.partial(finish_kernel, n_head, head0, span), 16, 2 * heads...  8.07 us
    pallas_call x2, Pallas kernels, conv_far(): call(functools.partial(far_kernel, n_head, head0), 16, heads, grid=(heads...  4.57 us
    ppermute x4, starting transfers between devices, shifted(): return lax.ppermute(value, 'seq', pairs)  4.28 us
    pallas_call x1, Pallas kernels, conv_near(): call(functools.partial(near_kernel, 2 * len(pieces)), 16, heads, grid=(he...  3.82 us
  transfers between devices with their start and end apart: 18, of which 8 were waited for; matrix products, arithmetic and copies ran while one was open for 0% of the time, Pallas kernels for 38%

profile of v3, /device:TPU:0, one launch (start us, length us, event | category | flops | bytes accessed | tf_op | source)
XLA Modules:
  0.0 83.7 jit_solution(14467508278366164731)
XLA Ops:
  0.0 0.5 collective-permute-start.6
  0.5 1.6 %copy-done.1 = bf16[128,3,16,128]{3,2,1,0:T(8,128)(2,1)S(1)} copy-done((bf16[128,3,16,128]{3,2,1,0:T(8,128)(2,1)S(1)}, bf16[128,3,16,128]{3,2,1,0:T(8,128)(2,1)}, u32[]{:S(2)}) %copy-start.1) | copy-done | bytes 1572888
  2.0 1.0 %pack.1 = (bf16[3,4,128,128]{3,2,1,0:T(8,128)(2,1)S(1)}, bf16[3,4,128,128]{3,2,1,0:T(8,128)(2,1)S(1)}, bf16[3,2,128,128]{3,2,1,0:T(8,128)(2,1)S(1)}, bf16[3,2,12...) custom-call(bf16[128,3,16,128]{3,2,1,0:T(8,128)(2,1)S(1)} %copy-done.1), custom_call_target="tpu_custom_call" | custom-call | flops 2000000000 | bytes 6000000 | tf_op jit(solution)/shard_map/pack/pallas_call | solution.py:64
  3.1 2.8 %collective-permute-start.4 = (bf16[128,2048]{1,0:T(8,128)(2,1)S(1)}, bf16[128,2048]{1,0:T(8,128)(2,1)S(1)}, u32[]{:S(2)}, u32[]{:S(2)}) collective-permute-start(bf16[128,2048]{1,0:T(8,128)(2,1)S(1)} %copy-done.2), channel_id=1, source_target_pairs={{0,2},{1,3},{2,0},{3,1},{4,6},{5,7},{6,4},{7,5},{8,10},{9,11},{10,... | collective-permute-start | bytes 1572872 | tf_op jit(solution)/shard_map/ppermute | solution.py:435
  6.0 1.2 %collective-permute-start.3 = (bf16[3,2,128,128]{3,2,1,0:T(8,128)(2,1)S(1)}, bf16[3,2,128,128]{3,2,1,0:T(8,128)(2,1)S(1)}, u32[]{:S(2)}, u32[]{:S(2)}) collective-permute-start(bf16[3,2,128,128]{3,2,1,0:T(8,128)(2,1)S(1)} %get-tuple-element.92), channel_id=1, source_target_pairs={{0,3},{1,2},{2,1},{3,0},{4,7},{5,6},{6,5},{7,4},{8,11},{9,10},{10,... | collective-permute-start | bytes 589832 | tf_op jit(solution)/shard_map/ppermute | solution.py:435
  7.2 1.8 %dequant.1.refs_2_ = bf16[2048,512]{1,0:T(8,128)(2,1)S(1)} custom-call(bf16[512,2048]{1,0:T(8,128)(2,1)S(1)} %copy-done, f32[16,16]{1,0:T(8,128)S(1)} %copy-done.4), custom_call_target="tpu_custom_call" | custom-call | flops 2000000000 | bytes 6000000 | tf_op jit(solution)/shard_map/dequant/pallas_call | solution.py:124
  9.0 0.7 dattn.2
  9.9 3.8 %conv_near.1.near = bf16[3,4,224,128]{3,2,1,0:T(8,128)(2,1)S(1)} custom-call(f32[31,3,4,128]{3,2,1,0:T(4,128)S(1)} %copy-done.3, bf16[3,4,128,128]{3,2,1,0:T(8,128)(2,1)S(1)} %get-tuple-element.141.refs_0_, bf16[3,4,128,128]{3,2,1,0:T(8,128)(2,1)S(1)} %collective-permute-done.5.refs_1_), custom_call_target="tpu_custom_call" | custom-call | flops 4000000000 | bytes 12000000 | tf_op jit(solution)/shard_map/conv_near/pallas_call | solution.py:208
  13.8 9.2 %collective-permute-done.2.refs_2_ = bf16[3,2,128,128]{3,2,1,0:T(8,128)(2,1)S(1)} collective-permute-done((bf16[3,2,128,128]{3,2,1,0:T(8,128)(2,1)S(1)}, bf16[3,2,128,128]{3,2,1,0:T(8,128)(2,1)S(1)}, u32[]{:S(2)}, u32[]{:S(2)}) %collective-permute-start.2) | collective-permute-done | bytes 196640 | tf_op jit(solution)/shard_map/ppermute | solution.py:435
  22.9 3.3 %collective-permute-done.3.refs_3_ = bf16[3,2,128,128]{3,2,1,0:T(8,128)(2,1)S(1)} collective-permute-done((bf16[3,2,128,128]{3,2,1,0:T(8,128)(2,1)S(1)}, bf16[3,2,128,128]{3,2,1,0:T(8,128)(2,1)S(1)}, u32[]{:S(2)}, u32[]{:S(2)}) %collective-permute-start.3) | collective-permute-done | bytes 196640 | tf_op jit(solution)/shard_map/ppermute | solution.py:435
  26.2 0.3 collective-permute-start.7
  26.5 1.7 %collective-permute-start = (bf16[3,2,128,128]{3,2,1,0:T(8,128)(2,1)S(1)}, bf16[3,2,128,128]{3,2,1,0:T(8,128)(2,1)S(1)}, u32[]{:S(2)}, u32[]{:S(2)}) collective-permute-start(bf16[3,2,128,128]{3,2,1,0:T(8,128)(2,1)S(1)} %get-tuple-element.89), channel_id=1, source_target_pairs={{0,2},{1,3},{2,0},{3,1},{4,6},{5,7},{6,4},{7,5},{8,10},{9,11},{10,... | collective-permute-start | bytes 589832 | tf_op jit(solution)/shard_map/ppermute | solution.py:435
  28.4 1.5 %collective-permute-start.8 = (bf16[2,352,128]{2,1,0:T(8,128)(2,1)S(1)}, bf16[2,352,128]{2,1,0:T(8,128)(2,1)S(1)}, u32[]{:S(2)}, u32[]{:S(2)}) collective-permute-start(bf16[2,352,128]{2,1,0:T(8,128)(2,1)S(1)} %tail.2), channel_id=1, source_target_pairs={{0,4},{4,8},{8,12},{12,16},{16,20},{20,24},{24,28},{28,0},{1,5},{5... | collective-permute-start | bytes 540680 | tf_op jit(solution)/shard_map/ppermute | solution.py:441
  30.0 2.3 %conv_far.2 = (bf16[3,2,224,128]{3,2,1,0:T(8,128)(2,1)S(1)}, bf16[3,2,32,128]{3,2,1,0:T(8,128)(2,1)S(1)}, bf16[3,2,32,128]{3,2,1,0:T(8,128)(2,1)S(1)}) custom-call(f32[31,3,4,128]{3,2,1,0:T(4,128)S(1)} %copy-done.3, bf16[3,4,128,128]{3,2,1,0:T(8,128)(2,1)S(1)} %get-tuple-element.141.refs_0_, bf16[3,4,128,128]{3,2,1,0:T(8,128)(2,1)S(1)} %collective-permute-done.5.refs_1_, ...), custom_call_target="tpu_custom_call" | custom-call | flops 2000000000 | bytes 6000000 | tf_op jit(solution)/shard_map/conv_far/pallas_call | solution.py:254
  32.3 0.8 dattn.3
  33.1 5.3 %collective-permute-done.8.halo = bf16[2,352,128]{2,1,0:T(8,128)(2,1)S(1)} collective-permute-done((bf16[2,352,128]{2,1,0:T(8,128)(2,1)S(1)}, bf16[2,352,128]{2,1,0:T(8,128)(2,1)S(1)}, u32[]{:S(2)}, u32[]{:S(2)}) %collective-permute-start.8) | collective-permute-done | bytes 180256 | tf_op jit(solution)/shard_map/ppermute | solution.py:441
  38.7 5.5 %attention.2 = (f32[3,2,640,128]{3,2,1,0:T(8,128)S(1)}, bf16[2,352,128]{2,1,0:T(8,128)(2,1)S(1)}) custom-call(s32[16]{0:T(128)S(1)} %copy-done.5, s32[8]{0:T(128)S(1)} %copy-done.6, bf16[3,4,224,128]{3,2,1,0:T(8,128)(2,1)S(1)} %conv_near.1.near, bf16[3,2,224,128]{3,2,1,0:T(8,128)(2,1)S(1)} %get-tuple-element.129.far, ...), custom_call_target="tpu_custom_call" | custom-call | flops 5000000000 | bytes 15000000 | tf_op jit(solution)/shard_map/attention/pallas_call | solution.py:351
  44.1 3.4 %collective-permute-done.9.halo = bf16[2,352,128]{2,1,0:T(8,128)(2,1)S(1)} collective-permute-done((bf16[2,352,128]{2,1,0:T(8,128)(2,1)S(1)}, bf16[2,352,128]{2,1,0:T(8,128)(2,1)S(1)}, u32[]{:S(2)}, u32[]{:S(2)}) %collective-permute-start.9) | collective-permute-done | bytes 180256 | tf_op jit(solution)/shard_map/ppermute | solution.py:441
  47.6 1.3 %collective-permute-start.10 = (bf16[2,352,128]{2,1,0:T(8,128)(2,1)S(1)}, bf16[2,352,128]{2,1,0:T(8,128)(2,1)S(1)}, u32[]{:S(2)}, u32[]{:S(2)}) collective-permute-start(bf16[2,352,128]{2,1,0:T(8,128)(2,1)S(1)} %get-tuple-element.140), channel_id=1, source_target_pairs={{0,28},{4,0},{8,4},{12,8},{16,12},{20,16},{24,20},{28,24},{1,29},{... | collective-permute-start | bytes 540680 | tf_op jit(solution)/shard_map/ppermute | solution.py:441
  48.9 2.3 %conv_far.3 = (bf16[3,2,224,128]{3,2,1,0:T(8,128)(2,1)S(1)}, bf16[3,2,32,128]{3,2,1,0:T(8,128)(2,1)S(1)}, bf16[3,2,32,128]{3,2,1,0:T(8,128)(2,1)S(1)}) custom-call(f32[31,3,4,128]{3,2,1,0:T(4,128)S(1)} %copy-done.3, bf16[3,4,128,128]{3,2,1,0:T(8,128)(2,1)S(1)} %get-tuple-element.141.refs_0_, bf16[3,4,128,128]{3,2,1,0:T(8,128)(2,1)S(1)} %collective-permute-done.5.refs_1_, ...), custom_call_target="tpu_custom_call" | custom-call | flops 2000000000 | bytes 6000000 | tf_op jit(solution)/shard_map/conv_far/pallas_call | solution.py:254
  51.2 5.5 %attention.3 = (f32[3,2,640,128]{3,2,1,0:T(8,128)S(1)}, bf16[2,352,128]{2,1,0:T(8,128)(2,1)S(1)}) custom-call(s32[16]{0:T(128)S(1)} %copy-done.5, s32[8]{0:T(128)S(1)} %copy-done.6, bf16[3,4,224,128]{3,2,1,0:T(8,128)(2,1)S(1)} %conv_near.1.near, bf16[3,2,224,128]{3,2,1,0:T(8,128)(2,1)S(1)} %get-tuple-element.145.far, ...), custom_call_target="tpu_custom_call" | custom-call | flops 5000000000 | bytes 15000000 | tf_op jit(solution)/shard_map/attention/pallas_call | solution.py:351
  56.7 1.4 %collective-permute-start.13 = (bf16[2,352,128]{2,1,0:T(8,128)(2,1)S(1)}, bf16[2,352,128]{2,1,0:T(8,128)(2,1)S(1)}, u32[]{:S(2)}, u32[]{:S(2)}) collective-permute-start(bf16[2,352,128]{2,1,0:T(8,128)(2,1)S(1)} %get-tuple-element.160), channel_id=1, source_target_pairs={{0,28},{4,0},{8,4},{12,8},{16,12},{20,16},{24,20},{28,24},{1,29},{... | collective-permute-start | bytes 540680 | tf_op jit(solution)/shard_map/ppermute | solution.py:441
  58.1 4.0 %finish.2 = (bf16[3,2,128,128]{3,2,1,0:T(8,128)(2,1)S(1)}, bf16[3,2,128,128]{3,2,1,0:T(8,128)(2,1)S(1)}, bf16[3,2,128,128]{3,2,1,0:T(8,128)(2,1)S(1)}, bf16[3,2,128,128]{3,2,1,0:T(8,128)(2,1)S(1)}) custom-call(f32[3,2,640,128]{3,2,1,0:T(8,128)S(1)} %get-tuple-element.150.totals, bf16[2,352,128]{2,1,0:T(8,128)(2,1)S(1)} %collective-permute-done.10.carry, ...), custom_call_target="tpu_custom_call" | custom-call | flops 4000000000 | bytes 12000000 | tf_op jit(solution)/shard_map/finish/pallas_call | solution.py:414
  62.2 1.6 %collective-permute-start.12 = (bf16[3,2,128,128]{3,2,1,0:T(8,128)(2,1)S(1)}, bf16[3,2,128,128]{3,2,1,0:T(8,128)(2,1)S(1)}, u32[]{:S(2)}, u32[]{:S(2)}) collective-permute-start(bf16[3,2,128,128]{3,2,1,0:T(8,128)(2,1)S(1)} %get-tuple-element.158), channel_id=1, source_target_pairs={{0,2},{1,3},{2,0},{3,1},{4,6},{5,7},{6,4},{7,5},{8,10},{9,11},{10,... | collective-permute-start | bytes 589832 | tf_op jit(solution)/shard_map/ppermute | solution.py:435
  64.0 4.0 %finish.3 = (bf16[3,2,128,128]{3,2,1,0:T(8,128)(2,1)S(1)}, bf16[3,2,128,128]{3,2,1,0:T(8,128)(2,1)S(1)}, bf16[3,2,128,128]{3,2,1,0:T(8,128)(2,1)S(1)}, bf16[3,2,128,128]{3,2,1,0:T(8,128)(2,1)S(1)}) custom-call(f32[3,2,640,128]{3,2,1,0:T(8,128)S(1)} %get-tuple-element.159.totals, bf16[2,352,128]{2,1,0:T(8,128)(2,1)S(1)} %collective-permute-done.13.carry, ...), custom_call_target="tpu_custom_call" | custom-call | flops 4000000000 | bytes 12000000 | tf_op jit(solution)/shard_map/finish/pallas_call | solution.py:414
  68.1 1.8 %collective-permute-done.12.refs_2_ = bf16[3,2,128,128]{3,2,1,0:T(8,128)(2,1)S(1)} collective-permute-done((bf16[3,2,128,128]{3,2,1,0:T(8,128)(2,1)S(1)}, bf16[3,2,128,128]{3,2,1,0:T(8,128)(2,1)S(1)}, u32[]{:S(2)}, u32[]{:S(2)}) %collective-permute-start.12) | collective-permute-done | bytes 196640 | tf_op jit(solution)/shard_map/ppermute | solution.py:435
  70.0 1.5 %collective-permute-start.16 = (bf16[3,2,128,128]{3,2,1,0:T(8,128)(2,1)S(1)}, bf16[3,2,128,128]{3,2,1,0:T(8,128)(2,1)S(1)}, u32[]{:S(2)}, u32[]{:S(2)}) collective-permute-start(bf16[3,2,128,128]{3,2,1,0:T(8,128)(2,1)S(1)} %get-tuple-element.171), channel_id=1, source_target_pairs={{0,2},{1,3},{2,0},{3,1},{4,6},{5,7},{6,4},{7,5},{8,10},{9,11},{10,... | collective-permute-start | bytes 589832 | tf_op jit(solution)/shard_map/ppermute | solution.py:435
  71.5 0.3 collective-permute-start.17
  71.8 1.4 %collective-permute-done.14.refs_3_ = bf16[3,2,128,128]{3,2,1,0:T(8,128)(2,1)S(1)} collective-permute-done((bf16[3,2,128,128]{3,2,1,0:T(8,128)(2,1)S(1)}, bf16[3,2,128,128]{3,2,1,0:T(8,128)(2,1)S(1)}, u32[]{:S(2)}, u32[]{:S(2)}) %collective-permute-start.14) | collective-permute-done | bytes 196640 | tf_op jit(solution)/shard_map/ppermute | solution.py:435
  73.3 5.1 %collective-permute-done.16.refs_6_ = bf16[3,2,128,128]{3,2,1,0:T(8,128)(2,1)S(1)} collective-permute-done((bf16[3,2,128,128]{3,2,1,0:T(8,128)(2,1)S(1)}, bf16[3,2,128,128]{3,2,1,0:T(8,128)(2,1)S(1)}, u32[]{:S(2)}, u32[]{:S(2)}) %collective-permute-start.16) | collective-permute-done | bytes 196640 | tf_op jit(solution)/shard_map/ppermute | solution.py:435
  78.4 3.3 %collective-permute-done.17.refs_7_ = bf16[3,2,128,128]{3,2,1,0:T(8,128)(2,1)S(1)} collective-permute-done((bf16[3,2,128,128]{3,2,1,0:T(8,128)(2,1)S(1)}, bf16[3,2,128,128]{3,2,1,0:T(8,128)(2,1)S(1)}, u32[]{:S(2)}, u32[]{:S(2)}) %collective-permute-start.17) | collective-permute-done | bytes 196640 | tf_op jit(solution)/shard_map/ppermute | solution.py:435
  81.7 2.0 %unpack.1 = bf16[128,3,16,128]{3,2,1,0:T(8,128)(2,1)} custom-call(bf16[3,2,128,128]{3,2,1,0:T(8,128)(2,1)S(1)} %get-tuple-element.165.refs_0_, bf16[3,2,128,128]{3,2,1,0:T(8,128)(2,1)S(1)} %collective-permute-done.11.refs_1_, bf16[3,2,128,128]{3,2,1,0:T(8,128)(2,1)S(1)} %collective-permute-done.12.refs_2_, ...), custom_call_target="tpu_custom_call" | custom-call | flops 2000000000 | bytes 6000000 | tf_op jit(solution)/shard_map/unpack/pallas_call | solution.py:97
  (32 shorter events, 1.2 us)
Async XLA Ops:
  0.0 7.2 %copy-start = (bf16[512,2048]{1,0:T(8,128)(2,1)S(1)}, bf16[512,2048]{1,0:T(8,128)(2,1)}, u32[]{:S(2)}) copy-start(bf16[512,2048]{1,0:T(8,128)(2,1)} %values) | copy-start | bytes 6291460
  0.0 7.2 %collective-permute-start.6 = (bf16[128,2048]{1,0:T(8,128)(2,1)}, bf16[128,2048]{1,0:T(8,128)(2,1)S(1)}, u32[]{:S(2)}, u32[]{:S(2)}) collective-permute-start(bf16[128,2048]{1,0:T(8,128)(2,1)} %refs_0_), channel_id=1, source_target_pairs={{0,1},{1,0},{2,3},{3,2},{4,5},{5,4},{6,7},{7,6},{8,9},{9,8},{10,11... | collective-permute-start | bytes 1572872 | tf_op jit(solution)/shard_map/ppermute | solution.py:435
  0.5 1.6 %copy-start.1 = (bf16[128,3,16,128]{3,2,1,0:T(8,128)(2,1)S(1)}, bf16[128,3,16,128]{3,2,1,0:T(8,128)(2,1)}, u32[]{:S(2)}) copy-start(bf16[128,3,16,128]{3,2,1,0:T(8,128)(2,1)} %src.1) | copy-start | bytes 4718596
  2.0 1.1 %copy-start.2 = (bf16[128,2048]{1,0:T(8,128)(2,1)S(1)}, bf16[128,2048]{1,0:T(8,128)(2,1)}, u32[]{:S(2)}) copy-start(bf16[128,2048]{1,0:T(8,128)(2,1)} %refs_0_) | copy-start | bytes 1572868
  2.0 5.2 %copy-start.4 = (f32[16,16]{1,0:T(8,128)S(1)}, f32[16,16]{1,0:T(8,128)}, u32[]{:S(2)}) copy-start(f32[16,16]{1,0:T(8,128)} %scales.1) | copy-start | bytes 3076
  3.1 4.2 %collective-permute-start.5 = (bf16[3,4,128,128]{3,2,1,0:T(8,128)(2,1)S(1)}, bf16[3,4,128,128]{3,2,1,0:T(8,128)(2,1)S(1)}, u32[]{:S(2)}, u32[]{:S(2)}) collective-permute-start(bf16[3,4,128,128]{3,2,1,0:T(8,128)(2,1)S(1)} %get-tuple-element.94), channel_id=1, source_target_pairs={{0,1},{1,0},{2,3},{3,2},{4,5},{5,4},{6,7},{7,6},{8,9},{9,8},{10,11... | collective-permute-start | bytes 1179656 | tf_op jit(solution)/shard_map/ppermute | solution.py:435
  3.1 23.0 %collective-permute-start.4 = (bf16[128,2048]{1,0:T(8,128)(2,1)S(1)}, bf16[128,2048]{1,0:T(8,128)(2,1)S(1)}, u32[]{:S(2)}, u32[]{:S(2)}) collective-permute-start(bf16[128,2048]{1,0:T(8,128)(2,1)S(1)} %copy-done.2), channel_id=1, source_target_pairs={{0,2},{1,3},{2,0},{3,1},{4,6},{5,7},{6,4},{7,5},{8,10},{9,11},{10,... | collective-permute-start | bytes 1572872 | tf_op jit(solution)/shard_map/ppermute | solution.py:435
  6.0 16.9 %collective-permute-start.2 = (bf16[3,2,128,128]{3,2,1,0:T(8,128)(2,1)S(1)}, bf16[3,2,128,128]{3,2,1,0:T(8,128)(2,1)S(1)}, u32[]{:S(2)}, u32[]{:S(2)}) collective-permute-start(bf16[3,2,128,128]{3,2,1,0:T(8,128)(2,1)S(1)} %get-tuple-element.91), channel_id=1, source_target_pairs={{0,2},{1,3},{2,0},{3,1},{4,6},{5,7},{6,4},{7,5},{8,10},{9,11},{10,... | collective-permute-start | bytes 589832 | tf_op jit(solution)/shard_map/ppermute | solution.py:435
  6.0 20.1 %collective-permute-start.3 = (bf16[3,2,128,128]{3,2,1,0:T(8,128)(2,1)S(1)}, bf16[3,2,128,128]{3,2,1,0:T(8,128)(2,1)S(1)}, u32[]{:S(2)}, u32[]{:S(2)}) collective-permute-start(bf16[3,2,128,128]{3,2,1,0:T(8,128)(2,1)S(1)} %get-tuple-element.92), channel_id=1, source_target_pairs={{0,3},{1,2},{2,1},{3,0},{4,7},{5,6},{6,5},{7,4},{8,11},{9,10},{10,... | collective-permute-start | bytes 589832 | tf_op jit(solution)/shard_map/ppermute | solution.py:435
  9.0 0.9 %copy-start.3 = (f32[31,3,4,128]{3,2,1,0:T(4,128)S(1)}, f32[31,3,4,128]{3,2,1,0:T(4,128)}, u32[]{:S(2)}) copy-start(f32[31,3,4,128]{3,2,1,0:T(4,128)} %taps.13) | copy-start | bytes 571396
  26.2 6.1 %collective-permute-start.7 = (bf16[128,2048]{1,0:T(8,128)(2,1)S(1)}, bf16[128,2048]{1,0:T(8,128)(2,1)S(1)}, u32[]{:S(2)}, u32[]{:S(2)}) collective-permute-start(bf16[128,2048]{1,0:T(8,128)(2,1)S(1)} %collective-permute-done.4.refs_0_), channel_id=1, source_target_pairs={{0,1},{1,0},{2,3},{3,2},{4,5},{5,4},{6,7},{7,6},{8,9},{9,8},{10,11... | collective-permute-start | bytes 1572872 | tf_op jit(solution)/shard_map/ppermute | solution.py:435
  26.5 11.9 %collective-permute-start = (bf16[3,2,128,128]{3,2,1,0:T(8,128)(2,1)S(1)}, bf16[3,2,128,128]{3,2,1,0:T(8,128)(2,1)S(1)}, u32[]{:S(2)}, u32[]{:S(2)}) collective-permute-start(bf16[3,2,128,128]{3,2,1,0:T(8,128)(2,1)S(1)} %get-tuple-element.89), channel_id=1, source_target_pairs={{0,2},{1,3},{2,0},{3,1},{4,6},{5,7},{6,4},{7,5},{8,10},{9,11},{10,... | collective-permute-start | bytes 589832 | tf_op jit(solution)/shard_map/ppermute | solution.py:435
  28.2 10.1 %collective-permute-start.1 = (bf16[3,2,128,128]{3,2,1,0:T(8,128)(2,1)S(1)}, bf16[3,2,128,128]{3,2,1,0:T(8,128)(2,1)S(1)}, u32[]{:S(2)}, u32[]{:S(2)}) collective-permute-start(bf16[3,2,128,128]{3,2,1,0:T(8,128)(2,1)S(1)} %get-tuple-element.90), channel_id=1, source_target_pairs={{0,3},{1,2},{2,1},{3,0},{4,7},{5,6},{6,5},{7,4},{8,11},{9,10},{10,... | collective-permute-start | bytes 589832 | tf_op jit(solution)/shard_map/ppermute | solution.py:435
  28.4 9.9 %collective-permute-start.8 = (bf16[2,352,128]{2,1,0:T(8,128)(2,1)S(1)}, bf16[2,352,128]{2,1,0:T(8,128)(2,1)S(1)}, u32[]{:S(2)}, u32[]{:S(2)}) collective-permute-start(bf16[2,352,128]{2,1,0:T(8,128)(2,1)S(1)} %tail.2), channel_id=1, source_target_pairs={{0,4},{4,8},{8,12},{12,16},{16,20},{20,24},{24,28},{28,0},{1,5},{5... | collective-permute-start | bytes 540680 | tf_op jit(solution)/shard_map/ppermute | solution.py:441
  32.3 6.4 %copy-start.5 = (s32[16]{0:T(128)S(1)}, s32[16]{0:T(128)}, u32[]{:S(2)}) copy-start(s32[16]{0:T(128)} %window.3) | copy-start | bytes 196
  32.3 6.4 %copy-start.6 = (s32[8]{0:T(128)S(1)}, s32[8]{0:T(128)}, u32[]{:S(2)}) copy-start(s32[8]{0:T(128)} %offsets.3) | copy-start | bytes 100
  38.6 9.0 %collective-permute-start.9 = (bf16[2,352,128]{2,1,0:T(8,128)(2,1)S(1)}, bf16[2,352,128]{2,1,0:T(8,128)(2,1)S(1)}, u32[]{:S(2)}, u32[]{:S(2)}) collective-permute-start(bf16[2,352,128]{2,1,0:T(8,128)(2,1)S(1)} %tail.3), channel_id=1, source_target_pairs={{0,4},{4,8},{8,12},{12,16},{16,20},{20,24},{24,28},{28,0},{1,5},{5... | collective-permute-start | bytes 540680 | tf_op jit(solution)/shard_map/ppermute | solution.py:441
  47.6 10.5 %collective-permute-start.10 = (bf16[2,352,128]{2,1,0:T(8,128)(2,1)S(1)}, bf16[2,352,128]{2,1,0:T(8,128)(2,1)S(1)}, u32[]{:S(2)}, u32[]{:S(2)}) collective-permute-start(bf16[2,352,128]{2,1,0:T(8,128)(2,1)S(1)} %get-tuple-element.140), channel_id=1, source_target_pairs={{0,28},{4,0},{8,4},{12,8},{16,12},{20,16},{24,20},{28,24},{1,29},{... | collective-permute-start | bytes 540680 | tf_op jit(solution)/shard_map/ppermute | solution.py:441
  56.7 7.4 %collective-permute-start.13 = (bf16[2,352,128]{2,1,0:T(8,128)(2,1)S(1)}, bf16[2,352,128]{2,1,0:T(8,128)(2,1)S(1)}, u32[]{:S(2)}, u32[]{:S(2)}) collective-permute-start(bf16[2,352,128]{2,1,0:T(8,128)(2,1)S(1)} %get-tuple-element.160), channel_id=1, source_target_pairs={{0,28},{4,0},{8,4},{12,8},{16,12},{20,16},{24,20},{28,24},{1,29},{... | collective-permute-start | bytes 540680 | tf_op jit(solution)/shard_map/ppermute | solution.py:441
  62.1 6.0 %collective-permute-start.11 = (bf16[3,2,128,128]{3,2,1,0:T(8,128)(2,1)S(1)}, bf16[3,2,128,128]{3,2,1,0:T(8,128)(2,1)S(1)}, u32[]{:S(2)}, u32[]{:S(2)}) collective-permute-start(bf16[3,2,128,128]{3,2,1,0:T(8,128)(2,1)S(1)} %get-tuple-element.157), channel_id=1, source_target_pairs={{0,1},{1,0},{2,3},{3,2},{4,5},{5,4},{6,7},{7,6},{8,9},{9,8},{10,11... | collective-permute-start | bytes 589832 | tf_op jit(solution)/shard_map/ppermute | solution.py:435
  62.2 7.8 %collective-permute-start.12 = (bf16[3,2,128,128]{3,2,1,0:T(8,128)(2,1)S(1)}, bf16[3,2,128,128]{3,2,1,0:T(8,128)(2,1)S(1)}, u32[]{:S(2)}, u32[]{:S(2)}) collective-permute-start(bf16[3,2,128,128]{3,2,1,0:T(8,128)(2,1)S(1)} %get-tuple-element.158), channel_id=1, source_target_pairs={{0,2},{1,3},{2,0},{3,1},{4,6},{5,7},{6,4},{7,5},{8,10},{9,11},{10,... | collective-permute-start | bytes 589832 | tf_op jit(solution)/shard_map/ppermute | solution.py:435
  63.8 9.5 %collective-permute-start.14 = (bf16[3,2,128,128]{3,2,1,0:T(8,128)(2,1)S(1)}, bf16[3,2,128,128]{3,2,1,0:T(8,128)(2,1)S(1)}, u32[]{:S(2)}, u32[]{:S(2)}) collective-permute-start(bf16[3,2,128,128]{3,2,1,0:T(8,128)(2,1)S(1)} %get-tuple-element.168), channel_id=1, source_target_pairs={{0,3},{1,2},{2,1},{3,0},{4,7},{5,6},{6,5},{7,4},{8,11},{9,10},{10,... | collective-permute-start | bytes 589832 | tf_op jit(solution)/shard_map/ppermute | solution.py:435
  69.9 3.3 %collective-permute-start.15 = (bf16[3,2,128,128]{3,2,1,0:T(8,128)(2,1)S(1)}, bf16[3,2,128,128]{3,2,1,0:T(8,128)(2,1)S(1)}, u32[]{:S(2)}, u32[]{:S(2)}) collective-permute-start(bf16[3,2,128,128]{3,2,1,0:T(8,128)(2,1)S(1)} %get-tuple-element.170), channel_id=1, source_target_pairs={{0,1},{1,0},{2,3},{3,2},{4,5},{5,4},{6,7},{7,6},{8,9},{9,8},{10,11... | collective-permute-start | bytes 589832 | tf_op jit(solution)/shard_map/ppermute | solution.py:435
  70.0 8.4 %collective-permute-start.16 = (bf16[3,2,128,128]{3,2,1,0:T(8,128)(2,1)S(1)}, bf16[3,2,128,128]{3,2,1,0:T(8,128)(2,1)S(1)}, u32[]{:S(2)}, u32[]{:S(2)}) collective-permute-start(bf16[3,2,128,128]{3,2,1,0:T(8,128)(2,1)S(1)} %get-tuple-element.171), channel_id=1, source_target_pairs={{0,2},{1,3},{2,0},{3,1},{4,6},{5,7},{6,4},{7,5},{8,10},{9,11},{10,... | collective-permute-start | bytes 589832 | tf_op jit(solution)/shard_map/ppermute | solution.py:435
  71.5 10.2 %collective-permute-start.17 = (bf16[3,2,128,128]{3,2,1,0:T(8,128)(2,1)S(1)}, bf16[3,2,128,128]{3,2,1,0:T(8,128)(2,1)S(1)}, u32[]{:S(2)}, u32[]{:S(2)}) collective-permute-start(bf16[3,2,128,128]{3,2,1,0:T(8,128)(2,1)S(1)} %get-tuple-element.172), channel_id=1, source_target_pairs={{0,3},{1,2},{2,1},{3,0},{4,7},{5,6},{6,5},{7,4},{8,11},{9,10},{10,... | collective-permute-start | bytes 589832 | tf_op jit(solution)/shard_map/ppermute | solution.py:435

commit v4 on v3

--- a/solution.py
+++ b/solution.py
@@ -124,7 +124,7 @@
     return call(
         functools.partial(dequant_kernel, side),
         8,
-        2,
+        0.01,
         grid=(width // step,),
         in_specs=[
             pl.BlockSpec((rows, step), lambda i: (0, i)),
@@ -147,7 +147,7 @@
     return call(
         functools.partial(dattn_kernel, len(pieces)),
         12,
-        1.5,
+        0.01,
         out_shape=[out] * len(pieces),
         name="dattn",
     )(*pieces, weight)
@@ -208,7 +208,7 @@
     return call(
         functools.partial(near_kernel, 2 * len(pieces)),
         16,
-        heads,
+        0.01,
         grid=(heads,),
         in_specs=[pl.BlockSpec(taps.shape, lambda h: (0, 0, 0, 0))]
         + [pl.BlockSpec((parts, 1, tokens, dim), lambda h: (0, h, 0, 0))] * len(pieces),
@@ -254,7 +254,7 @@
     return call(
         functools.partial(far_kernel, n_head, head0),
         16,
-        heads,
+        0.01,
         grid=(heads,),
         in_specs=[pl.BlockSpec(taps.shape, lambda h: (0, 0, 0, 0))]
         + [pl.BlockSpec((parts, 1, tokens, dim), lambda h: (0, head0 + h, 0, 0))] * len(near)
@@ -308,30 +308,36 @@
     base = window[me * local + head]
     blocks = seq_rows // MASKB
 
-    def attend(t):
-        first = t * TILE
-        reach = base + offsets[seq_index * blocks + first // MASKB]
-        limit = jnp.minimum(reach, seq_index * seq_rows + first + row)
-        allowed = (distance >= 0) & (distance <= limit)
-        q = mixed[0, pl.ds(span + first, TILE), :]
-        k = mixed[1, pl.ds(first, keys), :]
-        v = mixed[2, pl.ds(first, keys), :]
-        o = d_out[pl.ds(first, TILE), :]
-        scores = lax.dot_general(q, k, NT, preferred_element_type=F32)
-        d_prob = lax.dot_general(o, v, NT, preferred_element_type=F32)
-        scores = jnp.where(allowed, scores, NEG)
-        top = jnp.max(scores, axis=1, keepdims=True)
-        exps = jnp.exp((scores - top) * scale)
-        probs = exps * (1.0 / jnp.sum(exps, axis=1, keepdims=True))
-        delta = jnp.sum(probs * d_prob, axis=1, keepdims=True)
-        d_score = (probs * ((d_prob - delta) * scale)).astype(BF16)
-        probs_b = probs.astype(BF16)
-        totals[0, pl.ds(span + first, TILE), :] = jnp.dot(d_score, k, preferred_element_type=F32)
-        at = pl.ds(first, keys)
-        totals[1, at, :] += lax.dot_general(d_score, q, TN, preferred_element_type=F32)
-        totals[2, at, :] += lax.dot_general(probs_b, o, TN, preferred_element_type=F32)
-
-    loop(seq_rows // TILE, attend)
+    def attend(tiles):
+        firsts = [t * TILE for t in tiles]
+        q = [mixed[0, pl.ds(span + first, TILE), :] for first in firsts]
+        k = [mixed[1, pl.ds(first, keys), :] for first in firsts]
+        v = [mixed[2, pl.ds(first, keys), :] for first in firsts]
+        o = [d_out[pl.ds(first, TILE), :] for first in firsts]
+        every = range(len(firsts))
+        scores = [lax.dot_general(q[i], k[i], NT, preferred_element_type=F32) for i in every]
+        d_prob = [lax.dot_general(o[i], v[i], NT, preferred_element_type=F32) for i in every]
+        for i, first in enumerate(firsts):
+            reach = base + offsets[seq_index * blocks + first // MASKB]
+            limit = jnp.minimum(reach, seq_index * seq_rows + first + row)
+            scores[i] = jnp.where((distance >= 0) & (distance <= limit), scores[i], NEG)
+        top = [jnp.max(scores[i], axis=1, keepdims=True) for i in every]
+        exps = [jnp.exp((scores[i] - top[i]) * scale) for i in every]
+        part = [1.0 / jnp.sum(exps[i], axis=1, keepdims=True) for i in every]
+        probs = [exps[i] * part[i] for i in every]
+        delta = [jnp.sum(probs[i] * d_prob[i], axis=1, keepdims=True) for i in every]
+        d_score = [(probs[i] * ((d_prob[i] - delta[i]) * scale)).astype(BF16) for i in every]
+        for i, first in enumerate(firsts):
+            at = pl.ds(first, keys)
+            totals[0, pl.ds(span + first, TILE), :] = jnp.dot(d_score[i], k[i], preferred_element_type=F32)
+            totals[1, at, :] += lax.dot_general(d_score[i], q[i], TN, preferred_element_type=F32)
+            totals[2, at, :] += lax.dot_general(
+                probs[i].astype(BF16), o[i], TN, preferred_element_type=F32
+            )
+
+    count = seq_rows // TILE
+    group = 4 if count % 4 == 0 else 1
+    loop(count // group, lambda i: attend([i * group + n for n in range(group)]))
 
     carry_out[0, :span] = totals[1, :span].astype(BF16)
     carry_out[0, span : 2 * span] = totals[2, :span].astype(BF16)
@@ -351,7 +357,7 @@
     return call(
         functools.partial(attn_kernel, n_head, head0, span),
         16,
-        2.5 * heads,
+        0.01,
         grid=(heads,),
         in_specs=[pl.BlockSpec(memory_space=pltpu.SMEM)] * 2
         + [
@@ -512,30 +518,30 @@
     grads = list(d_attn(g_near, weight))
     near, grads = tied(near, grads)
     mixed_near = conv_near(near, conv_kernel)
+    g_far, mixed_near = tied(g_far, mixed_near)
     far[0], g_far, mixed_near = tied(far[0], g_far, mixed_near)
-
-    def halo_of(c):
+    g_rest = [partner(g_far, j) for j in range(1, half)]
+
+    halos, parts = [], []
+    for c in range(n_chunks):
+        if c > 0:
+            far[c], parts, grads = tied(far[c], parts, grads)
         tail = tail_of(near, far[c], c * per_chunk, span)
         far[c], tail = tied(far[c], tail)
-        return shifted(tail, 1)
-
-    halo = halo_of(0)
-    g_rest = [partner(g_far, j) for j in range(1, half)]
-    parts = conv_far(near, far[0], conv_kernel, 0)
-    g_rest, parts = tied(g_rest, parts)
-    grads += list(d_attn([g_far] + g_rest, weight))
-    parts, grads, halo = tied(parts, grads, halo)
+        halos.append(shifted(tail, 1))
+        parts.append(conv_far(near, far[c], conv_kernel, c * per_chunk))
+        if c == 0:
+            g_rest, parts[0] = tied(g_rest, parts[0])
+            grads += list(d_attn([g_far] + g_rest, weight))
+
     held = []
+    parts, grads, halos[0] = tied(parts, grads, halos[0])
     for c in range(n_chunks):
-        if c + 1 < n_chunks:
-            far[c + 1], halo, parts = tied(far[c + 1], halo, parts)
-            later = halo_of(c + 1)
         totals, carry = attention(
-            mixed_near, parts, halo, grads, conv_kernel, window, offsets, c * per_chunk, span
+            mixed_near, parts[c], halos[c], grads, conv_kernel, window, offsets, c * per_chunk, span
         )
         if c + 1 < n_chunks:
-            halo, totals, carry, near = tied(later, totals, carry, near)
-            parts = conv_far(near, far[c + 1], conv_kernel, (c + 1) * per_chunk)
+            halos[c + 1], totals, carry = tied(halos[c + 1], totals, carry)
         held.append((totals, shifted(carry, -1)))
     results = []
     held[0], last = tied(held[0], held[-1][0])

time: 83.9 us -> 76.5 us (0.912)
  waiting for transfers between devices: 32.9 us -> 26.9 us
  Pallas kernels: 34.2 us -> 30.3 us
  starting transfers between devices: 14.7 us -> 17.4 us
    ppermute x4, waiting for transfers between devices: 8.72 us -> 2.66 us  [shifted(): return lax.ppermute(value, 'seq', pairs)]
    pallas_call x8, Pallas kernels: 22.6 us -> 18.8 us  [the longest x2 7.1 us: attention(): call(functools.partial(attn_kernel, n_head, head0, span), 16, 0.01, grid=...]
    ppermute x4, starting transfers between devices: 4.28 us -> 6.32 us  [shifted(): return lax.ppermute(value, 'seq', pairs)]
  transfers between devices with their start and end apart: 18 -> 18, of which waited for: 8 -> 10; matrix products, arithmetic and copies ran while one was open for 0% -> 0% of each run, Pallas kernels for 38% -> 37%
where the time goes in v4:
time: 76.5 us; the launch traced here: 76.4 us
  Pallas kernels  30.3 us (40%)
  waiting for transfers between devices  26.9 us (35%)
  starting transfers between devices  17.4 us (23%)
  local copies, waits for them, and re-layouts  1.58 us (2%)
    ppermute x14, waiting for transfers between devices, partner(): return lax.ppermute(value, 'head', [(i, i ^ j) for i in range(size)])  24.2 us
    ppermute x14, starting transfers between devices, partner(): return lax.ppermute(value, 'head', [(i, i ^ j) for i in range(size)])  11.1 us
    pallas_call x2, Pallas kernels, finish(): call(functools.partial(finish_kernel, n_head, head0, span), 16, 2 * heads...  8.07 us
    pallas_call x2, Pallas kernels, attention(): call(functools.partial(attn_kernel, n_head, head0, span), 16, 0.01, grid=...  7.1 us
    ppermute x4, starting transfers between devices, shifted(): return lax.ppermute(value, 'seq', pairs)  6.32 us
    pallas_call x2, Pallas kernels, conv_far(): call(functools.partial(far_kernel, n_head, head0), 16, 0.01, grid=(heads,...  4.57 us
    pallas_call x1, Pallas kernels, conv_near(): call(functools.partial(near_kernel, 2 * len(pieces)), 16, 0.01, grid=(hea...  3.82 us
    ppermute x4, waiting for transfers between devices, shifted(): return lax.ppermute(value, 'seq', pairs)  2.66 us
  transfers between devices with their start and end apart: 18, of which 10 were waited for; matrix products, arithmetic and copies ran while one was open for 0% of the time, Pallas kernels for 37%

profile of v4, /device:TPU:0, one launch (start us, length us, event | category | flops | bytes accessed | tf_op | source)
XLA Modules:
  0.0 76.4 jit_solution(14724473576707903114)
XLA Ops:
  0.0 3.0 %collective-permute-start.4 = (bf16[128,2048]{1,0:T(8,128)(2,1)}, bf16[128,2048]{1,0:T(8,128)(2,1)S(1)}, u32[]{:S(2)}, u32[]{:S(2)}) collective-permute-start(bf16[128,2048]{1,0:T(8,128)(2,1)} %refs_0_), channel_id=1, source_target_pairs={{0,2},{1,3},{2,0},{3,1},{4,6},{5,7},{6,4},{7,5},{8,10},{9,11},{10,... | collective-permute-start | bytes 1572872 | tf_op jit(solution)/shard_map/ppermute | solution.py:441
  3.0 1.4 %copy-done.6 = bf16[128,3,16,128]{3,2,1,0:T(8,128)(2,1)S(1)} copy-done((bf16[128,3,16,128]{3,2,1,0:T(8,128)(2,1)S(1)}, bf16[128,3,16,128]{3,2,1,0:T(8,128)(2,1)}, u32[]{:S(2)}) %copy-start.6) | copy-done | bytes 1572888
  4.4 1.0 %pack.1 = (bf16[3,4,128,128]{3,2,1,0:T(8,128)(2,1)S(1)}, bf16[3,4,128,128]{3,2,1,0:T(8,128)(2,1)S(1)}, bf16[3,2,128,128]{3,2,1,0:T(8,128)(2,1)S(1)}, bf16[3,2,12...) custom-call(bf16[128,3,16,128]{3,2,1,0:T(8,128)(2,1)S(1)} %copy-done.6), custom_call_target="tpu_custom_call" | custom-call | flops 2000000000 | bytes 6000000 | tf_op jit(solution)/shard_map/pack/pallas_call | solution.py:64
  6.1 1.3 %collective-permute-start.3 = (bf16[3,2,128,128]{3,2,1,0:T(8,128)(2,1)S(1)}, bf16[3,2,128,128]{3,2,1,0:T(8,128)(2,1)S(1)}, u32[]{:S(2)}, u32[]{:S(2)}) collective-permute-start(bf16[3,2,128,128]{3,2,1,0:T(8,128)(2,1)S(1)} %get-tuple-element.98), channel_id=1, source_target_pairs={{0,3},{1,2},{2,1},{3,0},{4,7},{5,6},{6,5},{7,4},{8,11},{9,10},{10,... | collective-permute-start | bytes 589832 | tf_op jit(solution)/shard_map/ppermute | solution.py:441
  7.4 1.8 %dequant.1.refs_2_ = bf16[2048,512]{1,0:T(8,128)(2,1)S(1)} custom-call(bf16[512,2048]{1,0:T(8,128)(2,1)S(1)} %copy-done.1, f32[16,16]{1,0:T(8,128)S(1)} %copy-done.3), custom_call_target="tpu_custom_call" | custom-call | flops 10000000 | bytes 30000 | tf_op jit(solution)/shard_map/dequant/pallas_call | solution.py:124
  9.2 0.8 %dattn.2 = (bf16[128,512]{1,0:T(8,128)(2,1)S(1)}, bf16[128,512]{1,0:T(8,128)(2,1)S(1)}) custom-call(bf16[128,2048]{1,0:T(8,128)(2,1)S(1)} %copy-done.2, bf16[128,2048]{1,0:T(8,128)(2,1)S(1)} %collective-permute-done.6.refs_1_, bf16[2048,512]{1,0:T(8,128)(2,1)S(1)} %dequant.1.refs_2_), custom_call_target="tpu_custom_call" | custom-call | flops 10000000 | bytes 30000 | tf_op jit(solution)/shard_map/dattn/pallas_call | solution.py:147
  10.1 3.8 %conv_near.1.near = bf16[3,4,224,128]{3,2,1,0:T(8,128)(2,1)S(1)} custom-call(f32[31,3,4,128]{3,2,1,0:T(4,128)S(1)} %copy-done, bf16[3,4,128,128]{3,2,1,0:T(8,128)(2,1)S(1)} %get-tuple-element.108.refs_0_, bf16[3,4,128,128]{3,2,1,0:T(8,128)(2,1)S(1)} %collective-permute-done.5.refs_1_), custom_call_target="tpu_custom_call" | custom-call | flops 10000000 | bytes 30000 | tf_op jit(solution)/shard_map/conv_near/pallas_call | solution.py:208
  14.0 2.0 %collective-permute-done.4.refs_0_ = bf16[128,2048]{1,0:T(8,128)(2,1)S(1)} collective-permute-done((bf16[128,2048]{1,0:T(8,128)(2,1)}, bf16[128,2048]{1,0:T(8,128)(2,1)S(1)}, u32[]{:S(2)}, u32[]{:S(2)}) %collective-permute-start.4) | collective-permute-done | bytes 524320 | tf_op jit(solution)/shard_map/ppermute | solution.py:441
  15.9 4.2 %collective-permute-done.2.refs_2_ = bf16[3,2,128,128]{3,2,1,0:T(8,128)(2,1)S(1)} collective-permute-done((bf16[3,2,128,128]{3,2,1,0:T(8,128)(2,1)S(1)}, bf16[3,2,128,128]{3,2,1,0:T(8,128)(2,1)S(1)}, u32[]{:S(2)}, u32[]{:S(2)}) %collective-permute-start.2) | collective-permute-done | bytes 196640 | tf_op jit(solution)/shard_map/ppermute | solution.py:441
  20.1 2.6 %collective-permute-done.3.refs_3_ = bf16[3,2,128,128]{3,2,1,0:T(8,128)(2,1)S(1)} collective-permute-done((bf16[3,2,128,128]{3,2,1,0:T(8,128)(2,1)S(1)}, bf16[3,2,128,128]{3,2,1,0:T(8,128)(2,1)S(1)}, u32[]{:S(2)}, u32[]{:S(2)}) %collective-permute-start.3) | collective-permute-done | bytes 196640 | tf_op jit(solution)/shard_map/ppermute | solution.py:441
  23.4 1.7 %collective-permute-start = (bf16[3,2,128,128]{3,2,1,0:T(8,128)(2,1)S(1)}, bf16[3,2,128,128]{3,2,1,0:T(8,128)(2,1)S(1)}, u32[]{:S(2)}, u32[]{:S(2)}) collective-permute-start(bf16[3,2,128,128]{3,2,1,0:T(8,128)(2,1)S(1)} %get-tuple-element.95), channel_id=1, source_target_pairs={{0,2},{1,3},{2,0},{3,1},{4,6},{5,7},{6,4},{7,5},{8,10},{9,11},{10,... | collective-permute-start | bytes 589832 | tf_op jit(solution)/shard_map/ppermute | solution.py:441
  25.3 1.5 %collective-permute-start.9 = (bf16[2,352,128]{2,1,0:T(8,128)(2,1)S(1)}, bf16[2,352,128]{2,1,0:T(8,128)(2,1)S(1)}, u32[]{:S(2)}, u32[]{:S(2)}) collective-permute-start(bf16[2,352,128]{2,1,0:T(8,128)(2,1)S(1)} %tail.2), channel_id=1, source_target_pairs={{0,4},{4,8},{8,12},{12,16},{16,20},{20,24},{24,28},{28,0},{1,5},{5... | collective-permute-start | bytes 540680 | tf_op jit(solution)/shard_map/ppermute | solution.py:447
  26.9 2.3 %conv_far.2 = (bf16[3,2,224,128]{3,2,1,0:T(8,128)(2,1)S(1)}, bf16[3,2,32,128]{3,2,1,0:T(8,128)(2,1)S(1)}, bf16[3,2,32,128]{3,2,1,0:T(8,128)(2,1)S(1)}) custom-call(f32[31,3,4,128]{3,2,1,0:T(4,128)S(1)} %copy-done, bf16[3,4,128,128]{3,2,1,0:T(8,128)(2,1)S(1)} %get-tuple-element.108.refs_0_, bf16[3,4,128,128]{3,2,1,0:T(8,128)(2,1)S(1)} %collective-permute-done.5.refs_1_, ...), custom_call_target="tpu_custom_call" | custom-call | flops 10000000 | bytes 30000 | tf_op jit(solution)/shard_map/conv_far/pallas_call | solution.py:254
  29.2 0.8 %dattn.3 = (bf16[128,512]{1,0:T(8,128)(2,1)S(1)}, bf16[128,512]{1,0:T(8,128)(2,1)S(1)}) custom-call(bf16[128,2048]{1,0:T(8,128)(2,1)S(1)} %collective-permute-done.4.refs_0_, bf16[128,2048]{1,0:T(8,128)(2,1)S(1)} %collective-permute-done.7.refs_1_, bf16[2048,512]{1,0:T(8,128)(2,1)S(1)} %dequant.1.refs_2_), custom_call_target="tpu_custom_call" | custom-call | flops 10000000 | bytes 30000 | tf_op jit(solution)/shard_map/dattn/pallas_call | solution.py:147
  30.0 1.2 %collective-permute-done.refs_2_ = bf16[3,2,128,128]{3,2,1,0:T(8,128)(2,1)S(1)} collective-permute-done((bf16[3,2,128,128]{3,2,1,0:T(8,128)(2,1)S(1)}, bf16[3,2,128,128]{3,2,1,0:T(8,128)(2,1)S(1)}, u32[]{:S(2)}, u32[]{:S(2)}) %collective-permute-start) | collective-permute-done | bytes 196640 | tf_op jit(solution)/shard_map/ppermute | solution.py:441
  31.1 2.5 %collective-permute-done.1.refs_3_ = bf16[3,2,128,128]{3,2,1,0:T(8,128)(2,1)S(1)} collective-permute-done((bf16[3,2,128,128]{3,2,1,0:T(8,128)(2,1)S(1)}, bf16[3,2,128,128]{3,2,1,0:T(8,128)(2,1)S(1)}, u32[]{:S(2)}, u32[]{:S(2)}) %collective-permute-start.1) | collective-permute-done | bytes 196640 | tf_op jit(solution)/shard_map/ppermute | solution.py:441
  33.8 1.5 %collective-permute-start.8 = (bf16[2,352,128]{2,1,0:T(8,128)(2,1)S(1)}, bf16[2,352,128]{2,1,0:T(8,128)(2,1)S(1)}, u32[]{:S(2)}, u32[]{:S(2)}) collective-permute-start(bf16[2,352,128]{2,1,0:T(8,128)(2,1)S(1)} %tail.3), channel_id=1, source_target_pairs={{0,4},{4,8},{8,12},{12,16},{16,20},{20,24},{24,28},{28,0},{1,5},{5... | collective-permute-start | bytes 540680 | tf_op jit(solution)/shard_map/ppermute | solution.py:447
  35.4 2.3 %conv_far.3 = (bf16[3,2,224,128]{3,2,1,0:T(8,128)(2,1)S(1)}, bf16[3,2,32,128]{3,2,1,0:T(8,128)(2,1)S(1)}, bf16[3,2,32,128]{3,2,1,0:T(8,128)(2,1)S(1)}) custom-call(f32[31,3,4,128]{3,2,1,0:T(4,128)S(1)} %copy-done, bf16[3,4,128,128]{3,2,1,0:T(8,128)(2,1)S(1)} %get-tuple-element.108.refs_0_, bf16[3,4,128,128]{3,2,1,0:T(8,128)(2,1)S(1)} %collective-permute-done.5.refs_1_, ...), custom_call_target="tpu_custom_call" | custom-call | flops 10000000 | bytes 30000 | tf_op jit(solution)/shard_map/conv_far/pallas_call | solution.py:254
  37.7 3.6 %attention.2 = (f32[3,2,640,128]{3,2,1,0:T(8,128)S(1)}, bf16[2,352,128]{2,1,0:T(8,128)(2,1)S(1)}) custom-call(s32[16]{0:T(128)S(1)} %copy-done.4, s32[8]{0:T(128)S(1)} %copy-done.5, bf16[3,4,224,128]{3,2,1,0:T(8,128)(2,1)S(1)} %conv_near.1.near, bf16[3,2,224,128]{3,2,1,0:T(8,128)(2,1)S(1)} %get-tuple-element.145.far, ...), custom_call_target="tpu_custom_call" | custom-call | flops 10000000 | bytes 30000 | tf_op jit(solution)/shard_map/attention/pallas_call | solution.py:357
  41.3 2.6 %collective-permute-done.8.halo = bf16[2,352,128]{2,1,0:T(8,128)(2,1)S(1)} collective-permute-done((bf16[2,352,128]{2,1,0:T(8,128)(2,1)S(1)}, bf16[2,352,128]{2,1,0:T(8,128)(2,1)S(1)}, u32[]{:S(2)}, u32[]{:S(2)}) %collective-permute-start.8) | collective-permute-done | bytes 180256 | tf_op jit(solution)/shard_map/ppermute | solution.py:447
  43.9 1.7 %collective-permute-start.10 = (bf16[2,352,128]{2,1,0:T(8,128)(2,1)S(1)}, bf16[2,352,128]{2,1,0:T(8,128)(2,1)S(1)}, u32[]{:S(2)}, u32[]{:S(2)}) collective-permute-start(bf16[2,352,128]{2,1,0:T(8,128)(2,1)S(1)} %get-tuple-element.156), channel_id=1, source_target_pairs={{0,28},{4,0},{8,4},{12,8},{16,12},{20,16},{24,20},{28,24},{1,29},{... | collective-permute-start | bytes 540680 | tf_op jit(solution)/shard_map/ppermute | solution.py:447
  45.7 3.5 %attention.3 = (f32[3,2,640,128]{3,2,1,0:T(8,128)S(1)}, bf16[2,352,128]{2,1,0:T(8,128)(2,1)S(1)}) custom-call(s32[16]{0:T(128)S(1)} %copy-done.4, s32[8]{0:T(128)S(1)} %copy-done.5, bf16[3,4,224,128]{3,2,1,0:T(8,128)(2,1)S(1)} %conv_near.1.near, bf16[3,2,224,128]{3,2,1,0:T(8,128)(2,1)S(1)} %get-tuple-element.157.far, ...), custom_call_target="tpu_custom_call" | custom-call | flops 10000000 | bytes 30000 | tf_op jit(solution)/shard_map/attention/pallas_call | solution.py:357
  49.2 1.5 %collective-permute-start.13 = (bf16[2,352,128]{2,1,0:T(8,128)(2,1)S(1)}, bf16[2,352,128]{2,1,0:T(8,128)(2,1)S(1)}, u32[]{:S(2)}, u32[]{:S(2)}) collective-permute-start(bf16[2,352,128]{2,1,0:T(8,128)(2,1)S(1)} %get-tuple-element.172), channel_id=1, source_target_pairs={{0,28},{4,0},{8,4},{12,8},{16,12},{20,16},{24,20},{28,24},{1,29},{... | collective-permute-start | bytes 540680 | tf_op jit(solution)/shard_map/ppermute | solution.py:447
  50.7 4.0 %finish.2 = (bf16[3,2,128,128]{3,2,1,0:T(8,128)(2,1)S(1)}, bf16[3,2,128,128]{3,2,1,0:T(8,128)(2,1)S(1)}, bf16[3,2,128,128]{3,2,1,0:T(8,128)(2,1)S(1)}, bf16[3,2,128,128]{3,2,1,0:T(8,128)(2,1)S(1)}) custom-call(f32[3,2,640,128]{3,2,1,0:T(8,128)S(1)} %get-tuple-element.162.totals, bf16[2,352,128]{2,1,0:T(8,128)(2,1)S(1)} %collective-permute-done.10.carry, ...), custom_call_target="tpu_custom_call" | custom-call | flops 4000000000 | bytes 12000000 | tf_op jit(solution)/shard_map/finish/pallas_call | solution.py:420
  54.8 1.6 %collective-permute-start.12 = (bf16[3,2,128,128]{3,2,1,0:T(8,128)(2,1)S(1)}, bf16[3,2,128,128]{3,2,1,0:T(8,128)(2,1)S(1)}, u32[]{:S(2)}, u32[]{:S(2)}) collective-permute-start(bf16[3,2,128,128]{3,2,1,0:T(8,128)(2,1)S(1)} %get-tuple-element.170), channel_id=1, source_target_pairs={{0,2},{1,3},{2,0},{3,1},{4,6},{5,7},{6,4},{7,5},{8,10},{9,11},{10,... | collective-permute-start | bytes 589832 | tf_op jit(solution)/shard_map/ppermute | solution.py:441
  56.7 4.0 %finish.3 = (bf16[3,2,128,128]{3,2,1,0:T(8,128)(2,1)S(1)}, bf16[3,2,128,128]{3,2,1,0:T(8,128)(2,1)S(1)}, bf16[3,2,128,128]{3,2,1,0:T(8,128)(2,1)S(1)}, bf16[3,2,128,128]{3,2,1,0:T(8,128)(2,1)S(1)}) custom-call(f32[3,2,640,128]{3,2,1,0:T(8,128)S(1)} %get-tuple-element.171.totals, bf16[2,352,128]{2,1,0:T(8,128)(2,1)S(1)} %collective-permute-done.13.carry, ...), custom_call_target="tpu_custom_call" | custom-call | flops 4000000000 | bytes 12000000 | tf_op jit(solution)/shard_map/finish/pallas_call | solution.py:420
  60.8 1.8 %collective-permute-done.12.refs_2_ = bf16[3,2,128,128]{3,2,1,0:T(8,128)(2,1)S(1)} collective-permute-done((bf16[3,2,128,128]{3,2,1,0:T(8,128)(2,1)S(1)}, bf16[3,2,128,128]{3,2,1,0:T(8,128)(2,1)S(1)}, u32[]{:S(2)}, u32[]{:S(2)}) %collective-permute-start.12) | collective-permute-done | bytes 196640 | tf_op jit(solution)/shard_map/ppermute | solution.py:441
  62.6 1.5 %collective-permute-start.16 = (bf16[3,2,128,128]{3,2,1,0:T(8,128)(2,1)S(1)}, bf16[3,2,128,128]{3,2,1,0:T(8,128)(2,1)S(1)}, u32[]{:S(2)}, u32[]{:S(2)}) collective-permute-start(bf16[3,2,128,128]{3,2,1,0:T(8,128)(2,1)S(1)} %get-tuple-element.183), channel_id=1, source_target_pairs={{0,2},{1,3},{2,0},{3,1},{4,6},{5,7},{6,4},{7,5},{8,10},{9,11},{10,... | collective-permute-start | bytes 589832 | tf_op jit(solution)/shard_map/ppermute | solution.py:441
  64.5 1.4 %collective-permute-done.14.refs_3_ = bf16[3,2,128,128]{3,2,1,0:T(8,128)(2,1)S(1)} collective-permute-done((bf16[3,2,128,128]{3,2,1,0:T(8,128)(2,1)S(1)}, bf16[3,2,128,128]{3,2,1,0:T(8,128)(2,1)S(1)}, u32[]{:S(2)}, u32[]{:S(2)}) %collective-permute-start.14) | collective-permute-done | bytes 196640 | tf_op jit(solution)/shard_map/ppermute | solution.py:441
  65.9 5.1 %collective-permute-done.16.refs_6_ = bf16[3,2,128,128]{3,2,1,0:T(8,128)(2,1)S(1)} collective-permute-done((bf16[3,2,128,128]{3,2,1,0:T(8,128)(2,1)S(1)}, bf16[3,2,128,128]{3,2,1,0:T(8,128)(2,1)S(1)}, u32[]{:S(2)}, u32[]{:S(2)}) %collective-permute-start.16) | collective-permute-done | bytes 196640 | tf_op jit(solution)/shard_map/ppermute | solution.py:441
  71.0 3.3 %collective-permute-done.17.refs_7_ = bf16[3,2,128,128]{3,2,1,0:T(8,128)(2,1)S(1)} collective-permute-done((bf16[3,2,128,128]{3,2,1,0:T(8,128)(2,1)S(1)}, bf16[3,2,128,128]{3,2,1,0:T(8,128)(2,1)S(1)}, u32[]{:S(2)}, u32[]{:S(2)}) %collective-permute-start.17) | collective-permute-done | bytes 196640 | tf_op jit(solution)/shard_map/ppermute | solution.py:441
  74.3 2.0 %unpack.1 = bf16[128,3,16,128]{3,2,1,0:T(8,128)(2,1)} custom-call(bf16[3,2,128,128]{3,2,1,0:T(8,128)(2,1)S(1)} %get-tuple-element.177.refs_0_, bf16[3,2,128,128]{3,2,1,0:T(8,128)(2,1)S(1)} %collective-permute-done.11.refs_1_, bf16[3,2,128,128]{3,2,1,0:T(8,128)(2,1)S(1)} %collective-permute-done.12.refs_2_, ...), custom_call_target="tpu_custom_call" | custom-call | flops 2000000000 | bytes 6000000 | tf_op jit(solution)/shard_map/unpack/pallas_call | solution.py:97
  (32 shorter events, 2.5 us)
Async XLA Ops:
  0.0 7.4 %copy-start.1 = (bf16[512,2048]{1,0:T(8,128)(2,1)S(1)}, bf16[512,2048]{1,0:T(8,128)(2,1)}, u32[]{:S(2)}) copy-start(bf16[512,2048]{1,0:T(8,128)(2,1)} %values) | copy-start | bytes 6291460
  0.0 7.4 %copy-start.3 = (f32[16,16]{1,0:T(8,128)S(1)}, f32[16,16]{1,0:T(8,128)}, u32[]{:S(2)}) copy-start(f32[16,16]{1,0:T(8,128)} %scales.1) | copy-start | bytes 3076
  0.0 15.9 %collective-permute-start.4 = (bf16[128,2048]{1,0:T(8,128)(2,1)}, bf16[128,2048]{1,0:T(8,128)(2,1)S(1)}, u32[]{:S(2)}, u32[]{:S(2)}) collective-permute-start(bf16[128,2048]{1,0:T(8,128)(2,1)} %refs_0_), channel_id=1, source_target_pairs={{0,2},{1,3},{2,0},{3,1},{4,6},{5,7},{6,4},{7,5},{8,10},{9,11},{10,... | collective-permute-start | bytes 1572872 | tf_op jit(solution)/shard_map/ppermute | solution.py:441
  3.0 4.4 %collective-permute-start.6 = (bf16[128,2048]{1,0:T(8,128)(2,1)}, bf16[128,2048]{1,0:T(8,128)(2,1)S(1)}, u32[]{:S(2)}, u32[]{:S(2)}) collective-permute-start(bf16[128,2048]{1,0:T(8,128)(2,1)} %refs_0_), channel_id=1, source_target_pairs={{0,1},{1,0},{2,3},{3,2},{4,5},{5,4},{6,7},{7,6},{8,9},{9,8},{10,11... | collective-permute-start | bytes 1572872 | tf_op jit(solution)/shard_map/ppermute | solution.py:441
  3.0 1.4 %copy-start.6 = (bf16[128,3,16,128]{3,2,1,0:T(8,128)(2,1)S(1)}, bf16[128,3,16,128]{3,2,1,0:T(8,128)(2,1)}, u32[]{:S(2)}) copy-start(bf16[128,3,16,128]{3,2,1,0:T(8,128)(2,1)} %src.1) | copy-start | bytes 4718596
  5.4 2.0 %collective-permute-start.5 = (bf16[3,4,128,128]{3,2,1,0:T(8,128)(2,1)S(1)}, bf16[3,4,128,128]{3,2,1,0:T(8,128)(2,1)S(1)}, u32[]{:S(2)}, u32[]{:S(2)}) collective-permute-start(bf16[3,4,128,128]{3,2,1,0:T(8,128)(2,1)S(1)} %get-tuple-element.100), channel_id=1, source_target_pairs={{0,1},{1,0},{2,3},{3,2},{4,5},{5,4},{6,7},{7,6},{8,9},{9,8},{10,11... | collective-permute-start | bytes 1179656 | tf_op jit(solution)/shard_map/ppermute | solution.py:441
  6.0 14.2 %collective-permute-start.2 = (bf16[3,2,128,128]{3,2,1,0:T(8,128)(2,1)S(1)}, bf16[3,2,128,128]{3,2,1,0:T(8,128)(2,1)S(1)}, u32[]{:S(2)}, u32[]{:S(2)}) collective-permute-start(bf16[3,2,128,128]{3,2,1,0:T(8,128)(2,1)S(1)} %get-tuple-element.97), channel_id=1, source_target_pairs={{0,2},{1,3},{2,0},{3,1},{4,6},{5,7},{6,4},{7,5},{8,10},{9,11},{10,... | collective-permute-start | bytes 589832 | tf_op jit(solution)/shard_map/ppermute | solution.py:441
  6.1 16.7 %collective-permute-start.3 = (bf16[3,2,128,128]{3,2,1,0:T(8,128)(2,1)S(1)}, bf16[3,2,128,128]{3,2,1,0:T(8,128)(2,1)S(1)}, u32[]{:S(2)}, u32[]{:S(2)}) collective-permute-start(bf16[3,2,128,128]{3,2,1,0:T(8,128)(2,1)S(1)} %get-tuple-element.98), channel_id=1, source_target_pairs={{0,3},{1,2},{2,1},{3,0},{4,7},{5,6},{6,5},{7,4},{8,11},{9,10},{10,... | collective-permute-start | bytes 589832 | tf_op jit(solution)/shard_map/ppermute | solution.py:441
  7.4 1.8 %copy-start.2 = (bf16[128,2048]{1,0:T(8,128)(2,1)S(1)}, bf16[128,2048]{1,0:T(8,128)(2,1)}, u32[]{:S(2)}) copy-start(bf16[128,2048]{1,0:T(8,128)(2,1)} %refs_0_) | copy-start | bytes 1572868
  9.2 0.9 %copy-start = (f32[31,3,4,128]{3,2,1,0:T(4,128)S(1)}, f32[31,3,4,128]{3,2,1,0:T(4,128)}, u32[]{:S(2)}) copy-start(f32[31,3,4,128]{3,2,1,0:T(4,128)} %taps.13) | copy-start | bytes 571396
  22.8 6.4 %collective-permute-start.7 = (bf16[128,2048]{1,0:T(8,128)(2,1)S(1)}, bf16[128,2048]{1,0:T(8,128)(2,1)S(1)}, u32[]{:S(2)}, u32[]{:S(2)}) collective-permute-start(bf16[128,2048]{1,0:T(8,128)(2,1)S(1)} %collective-permute-done.4.refs_0_), channel_id=1, source_target_pairs={{0,1},{1,0},{2,3},{3,2},{4,5},{5,4},{6,7},{7,6},{8,9},{9,8},{10,11... | collective-permute-start | bytes 1572872 | tf_op jit(solution)/shard_map/ppermute | solution.py:441
  23.4 7.8 %collective-permute-start = (bf16[3,2,128,128]{3,2,1,0:T(8,128)(2,1)S(1)}, bf16[3,2,128,128]{3,2,1,0:T(8,128)(2,1)S(1)}, u32[]{:S(2)}, u32[]{:S(2)}) collective-permute-start(bf16[3,2,128,128]{3,2,1,0:T(8,128)(2,1)S(1)} %get-tuple-element.95), channel_id=1, source_target_pairs={{0,2},{1,3},{2,0},{3,1},{4,6},{5,7},{6,4},{7,5},{8,10},{9,11},{10,... | collective-permute-start | bytes 589832 | tf_op jit(solution)/shard_map/ppermute | solution.py:441
  25.1 8.5 %collective-permute-start.1 = (bf16[3,2,128,128]{3,2,1,0:T(8,128)(2,1)S(1)}, bf16[3,2,128,128]{3,2,1,0:T(8,128)(2,1)S(1)}, u32[]{:S(2)}, u32[]{:S(2)}) collective-permute-start(bf16[3,2,128,128]{3,2,1,0:T(8,128)(2,1)S(1)} %get-tuple-element.96), channel_id=1, source_target_pairs={{0,3},{1,2},{2,1},{3,0},{4,7},{5,6},{6,5},{7,4},{8,11},{9,10},{10,... | collective-permute-start | bytes 589832 | tf_op jit(solution)/shard_map/ppermute | solution.py:441
  25.3 12.4 %collective-permute-start.9 = (bf16[2,352,128]{2,1,0:T(8,128)(2,1)S(1)}, bf16[2,352,128]{2,1,0:T(8,128)(2,1)S(1)}, u32[]{:S(2)}, u32[]{:S(2)}) collective-permute-start(bf16[2,352,128]{2,1,0:T(8,128)(2,1)S(1)} %tail.2), channel_id=1, source_target_pairs={{0,4},{4,8},{8,12},{12,16},{16,20},{20,24},{24,28},{28,0},{1,5},{5... | collective-permute-start | bytes 540680 | tf_op jit(solution)/shard_map/ppermute | solution.py:447
  29.9 7.8 %copy-start.4 = (s32[16]{0:T(128)S(1)}, s32[16]{0:T(128)}, u32[]{:S(2)}) copy-start(s32[16]{0:T(128)} %window.3) | copy-start | bytes 196
  29.9 7.8 %copy-start.5 = (s32[8]{0:T(128)S(1)}, s32[8]{0:T(128)}, u32[]{:S(2)}) copy-start(s32[8]{0:T(128)} %offsets.3) | copy-start | bytes 100
  33.8 10.1 %collective-permute-start.8 = (bf16[2,352,128]{2,1,0:T(8,128)(2,1)S(1)}, bf16[2,352,128]{2,1,0:T(8,128)(2,1)S(1)}, u32[]{:S(2)}, u32[]{:S(2)}) collective-permute-start(bf16[2,352,128]{2,1,0:T(8,128)(2,1)S(1)} %tail.3), channel_id=1, source_target_pairs={{0,4},{4,8},{8,12},{12,16},{16,20},{20,24},{24,28},{28,0},{1,5},{5... | collective-permute-start | bytes 540680 | tf_op jit(solution)/shard_map/ppermute | solution.py:447
  43.9 6.8 %collective-permute-start.10 = (bf16[2,352,128]{2,1,0:T(8,128)(2,1)S(1)}, bf16[2,352,128]{2,1,0:T(8,128)(2,1)S(1)}, u32[]{:S(2)}, u32[]{:S(2)}) collective-permute-start(bf16[2,352,128]{2,1,0:T(8,128)(2,1)S(1)} %get-tuple-element.156), channel_id=1, source_target_pairs={{0,28},{4,0},{8,4},{12,8},{16,12},{20,16},{24,20},{28,24},{1,29},{... | collective-permute-start | bytes 540680 | tf_op jit(solution)/shard_map/ppermute | solution.py:447
  49.2 7.5 %collective-permute-start.13 = (bf16[2,352,128]{2,1,0:T(8,128)(2,1)S(1)}, bf16[2,352,128]{2,1,0:T(8,128)(2,1)S(1)}, u32[]{:S(2)}, u32[]{:S(2)}) collective-permute-start(bf16[2,352,128]{2,1,0:T(8,128)(2,1)S(1)} %get-tuple-element.172), channel_id=1, source_target_pairs={{0,28},{4,0},{8,4},{12,8},{16,12},{20,16},{24,20},{28,24},{1,29},{... | collective-permute-start | bytes 540680 | tf_op jit(solution)/shard_map/ppermute | solution.py:447
  54.8 6.0 %collective-permute-start.11 = (bf16[3,2,128,128]{3,2,1,0:T(8,128)(2,1)S(1)}, bf16[3,2,128,128]{3,2,1,0:T(8,128)(2,1)S(1)}, u32[]{:S(2)}, u32[]{:S(2)}) collective-permute-start(bf16[3,2,128,128]{3,2,1,0:T(8,128)(2,1)S(1)} %get-tuple-element.169), channel_id=1, source_target_pairs={{0,1},{1,0},{2,3},{3,2},{4,5},{5,4},{6,7},{7,6},{8,9},{9,8},{10,11... | collective-permute-start | bytes 589832 | tf_op jit(solution)/shard_map/ppermute | solution.py:441
  54.8 7.8 %collective-permute-start.12 = (bf16[3,2,128,128]{3,2,1,0:T(8,128)(2,1)S(1)}, bf16[3,2,128,128]{3,2,1,0:T(8,128)(2,1)S(1)}, u32[]{:S(2)}, u32[]{:S(2)}) collective-permute-start(bf16[3,2,128,128]{3,2,1,0:T(8,128)(2,1)S(1)} %get-tuple-element.170), channel_id=1, source_target_pairs={{0,2},{1,3},{2,0},{3,1},{4,6},{5,7},{6,4},{7,5},{8,10},{9,11},{10,... | collective-permute-start | bytes 589832 | tf_op jit(solution)/shard_map/ppermute | solution.py:441
  56.4 9.5 %collective-permute-start.14 = (bf16[3,2,128,128]{3,2,1,0:T(8,128)(2,1)S(1)}, bf16[3,2,128,128]{3,2,1,0:T(8,128)(2,1)S(1)}, u32[]{:S(2)}, u32[]{:S(2)}) collective-permute-start(bf16[3,2,128,128]{3,2,1,0:T(8,128)(2,1)S(1)} %get-tuple-element.180), channel_id=1, source_target_pairs={{0,3},{1,2},{2,1},{3,0},{4,7},{5,6},{6,5},{7,4},{8,11},{9,10},{10,... | collective-permute-start | bytes 589832 | tf_op jit(solution)/shard_map/ppermute | solution.py:441
  62.6 3.3 %collective-permute-start.15 = (bf16[3,2,128,128]{3,2,1,0:T(8,128)(2,1)S(1)}, bf16[3,2,128,128]{3,2,1,0:T(8,128)(2,1)S(1)}, u32[]{:S(2)}, u32[]{:S(2)}) collective-permute-start(bf16[3,2,128,128]{3,2,1,0:T(8,128)(2,1)S(1)} %get-tuple-element.182), channel_id=1, source_target_pairs={{0,1},{1,0},{2,3},{3,2},{4,5},{5,4},{6,7},{7,6},{8,9},{9,8},{10,11... | collective-permute-start | bytes 589832 | tf_op jit(solution)/shard_map/ppermute | solution.py:441
  62.6 8.4 %collective-permute-start.16 = (bf16[3,2,128,128]{3,2,1,0:T(8,128)(2,1)S(1)}, bf16[3,2,128,128]{3,2,1,0:T(8,128)(2,1)S(1)}, u32[]{:S(2)}, u32[]{:S(2)}) collective-permute-start(bf16[3,2,128,128]{3,2,1,0:T(8,128)(2,1)S(1)} %get-tuple-element.183), channel_id=1, source_target_pairs={{0,2},{1,3},{2,0},{3,1},{4,6},{5,7},{6,4},{7,5},{8,10},{9,11},{10,... | collective-permute-start | bytes 589832 | tf_op jit(solution)/shard_map/ppermute | solution.py:441
  64.1 10.2 %collective-permute-start.17 = (bf16[3,2,128,128]{3,2,1,0:T(8,128)(2,1)S(1)}, bf16[3,2,128,128]{3,2,1,0:T(8,128)(2,1)S(1)}, u32[]{:S(2)}, u32[]{:S(2)}) collective-permute-start(bf16[3,2,128,128]{3,2,1,0:T(8,128)(2,1)S(1)} %get-tuple-element.184), channel_id=1, source_target_pairs={{0,3},{1,2},{2,1},{3,0},{4,7},{5,6},{6,5},{7,4},{8,11},{9,10},{10,... | collective-permute-start | bytes 589832 | tf_op jit(solution)/shard_map/ppermute | solution.py:441

commit v5 on v4

--- a/solution.py
+++ b/solution.py
@@ -153,27 +153,28 @@
     )(*pieces, weight)
 
 
+def weighted(ref, taps, head, p, start, rows, place):
+    acc = None
+    for b in range(8):
+        window_rows = ref[p, pl.ds(start(b), rows + 24), :]
+        terms = [
+            taps[8 * a + b, p, pl.ds(head, 1), :] * window_rows[place(a) : place(a) + rows]
+            for a in range(4)
+            if 8 * a + b < KW
+        ]
+        while len(terms) > 1:
+            terms = [sum(terms[i + 1 : i + 2], terms[i]) for i in range(0, len(terms), 2)]
+        acc = terms[0] if acc is None else acc + terms[0]
+    return acc
+
+
 def spread(totals, taps, head, p, first, rows):
-    acc = jnp.zeros((rows, totals.shape[-1]), F32)
-    for b in range(8):
-        window_rows = totals[p, pl.ds(first + b, rows + 24), :]
-        for a in range(4):
-            tau = 8 * a + b
-            if tau < KW:
-                acc = acc + taps[tau, p, pl.ds(head, 1), :] * window_rows[8 * a : 8 * a + rows]
-    return acc
+    return weighted(totals, taps, head, p, lambda b: first + b, rows, lambda a: 8 * a)
 
 
 def convolve(ext, taps, head, p, first, rows):
-    acc = jnp.zeros((rows, ext.shape[-1]), F32)
-    for b in range(8):
-        window_rows = ext[p, pl.ds(first + 8 - b, rows + 24), :]
-        for a in range(4):
-            tau = 8 * a + b
-            if tau < KW:
-                at = 24 - 8 * a
-                acc = acc + taps[tau, p, pl.ds(head, 1), :] * window_rows[at : at + rows]
-    return acc.astype(BF16)
+    start = lambda b: first + 8 - b
+    return weighted(ext, taps, head, p, start, rows, lambda a: 24 - 8 * a).astype(BF16)
 
 
 def steps(rows):

time: 76.5 us -> 76.2 us (level)
  Pallas kernels: 30.3 us -> 28.9 us
  waiting for transfers between devices: 26.9 us -> 27.9 us
    ppermute x14, waiting for transfers between devices: 24.2 us -> 25 us  [partner(): return lax.ppermute(value, 'head', [(i, i ^ j) for i in range(size)])]
  transfers between devices with their start and end apart: 18 -> 18, of which waited for: 10 -> 10; matrix products, arithmetic and copies ran while one was open for 0% -> 0% of each run, Pallas kernels for 37% -> 35%
where the time goes in v5:
time: 76.2 us; the launch traced here: 76.1 us
  Pallas kernels  28.9 us (38%)
  waiting for transfers between devices  27.9 us (37%)
  starting transfers between devices  17.4 us (23%)
  local copies, waits for them, and re-layouts  1.58 us (2%)
    ppermute x14, waiting for transfers between devices, partner(): return lax.ppermute(value, 'head', [(i, i ^ j) for i in range(size)])  25 us
    ppermute x14, starting transfers between devices, partner(): return lax.ppermute(value, 'head', [(i, i ^ j) for i in range(size)])  11.1 us
    pallas_call x2, Pallas kernels, finish(): call(functools.partial(finish_kernel, n_head, head0, span), 16, 2 * heads...  7.5 us
    pallas_call x2, Pallas kernels, attention(): call(functools.partial(attn_kernel, n_head, head0, span), 16, 0.01, grid=...  7.04 us
    ppermute x4, starting transfers between devices, shifted(): return lax.ppermute(value, 'seq', pairs)  6.31 us
    pallas_call x2, Pallas kernels, conv_far(): call(functools.partial(far_kernel, n_head, head0), 16, 0.01, grid=(heads,...  4.16 us
    pallas_call x1, Pallas kernels, conv_near(): call(functools.partial(near_kernel, 2 * len(pieces)), 16, 0.01, grid=(hea...  3.49 us
    ppermute x4, waiting for transfers between devices, shifted(): return lax.ppermute(value, 'seq', pairs)  2.91 us
  transfers between devices with their start and end apart: 18, of which 10 were waited for; matrix products, arithmetic and copies ran while one was open for 0% of the time, Pallas kernels for 35%

profile of v5, /device:TPU:0, one launch (start us, length us, event | category | flops | bytes accessed | tf_op | source)
XLA Modules:
  0.0 76.1 jit_solution(5949484538182016229)
XLA Ops:
  0.0 3.0 %collective-permute-start.4 = (bf16[128,2048]{1,0:T(8,128)(2,1)}, bf16[128,2048]{1,0:T(8,128)(2,1)S(1)}, u32[]{:S(2)}, u32[]{:S(2)}) collective-permute-start(bf16[128,2048]{1,0:T(8,128)(2,1)} %refs_0_), channel_id=1, source_target_pairs={{0,2},{1,3},{2,0},{3,1},{4,6},{5,7},{6,4},{7,5},{8,10},{9,11},{10,... | collective-permute-start | bytes 1572872 | tf_op jit(solution)/shard_map/ppermute | solution.py:442
  3.0 1.4 %copy-done.6 = bf16[128,3,16,128]{3,2,1,0:T(8,128)(2,1)S(1)} copy-done((bf16[128,3,16,128]{3,2,1,0:T(8,128)(2,1)S(1)}, bf16[128,3,16,128]{3,2,1,0:T(8,128)(2,1)}, u32[]{:S(2)}) %copy-start.6) | copy-done | bytes 1572888
  4.4 1.0 %pack.1 = (bf16[3,4,128,128]{3,2,1,0:T(8,128)(2,1)S(1)}, bf16[3,4,128,128]{3,2,1,0:T(8,128)(2,1)S(1)}, bf16[3,2,128,128]{3,2,1,0:T(8,128)(2,1)S(1)}, bf16[3,2,12...) custom-call(bf16[128,3,16,128]{3,2,1,0:T(8,128)(2,1)S(1)} %copy-done.6), custom_call_target="tpu_custom_call" | custom-call | flops 2000000000 | bytes 6000000 | tf_op jit(solution)/shard_map/pack/pallas_call | solution.py:64
  6.1 1.3 %collective-permute-start.3 = (bf16[3,2,128,128]{3,2,1,0:T(8,128)(2,1)S(1)}, bf16[3,2,128,128]{3,2,1,0:T(8,128)(2,1)S(1)}, u32[]{:S(2)}, u32[]{:S(2)}) collective-permute-start(bf16[3,2,128,128]{3,2,1,0:T(8,128)(2,1)S(1)} %get-tuple-element.98), channel_id=1, source_target_pairs={{0,3},{1,2},{2,1},{3,0},{4,7},{5,6},{6,5},{7,4},{8,11},{9,10},{10,... | collective-permute-start | bytes 589832 | tf_op jit(solution)/shard_map/ppermute | solution.py:442
  7.4 1.8 %dequant.1.refs_2_ = bf16[2048,512]{1,0:T(8,128)(2,1)S(1)} custom-call(bf16[512,2048]{1,0:T(8,128)(2,1)S(1)} %copy-done.1, f32[16,16]{1,0:T(8,128)S(1)} %copy-done.3), custom_call_target="tpu_custom_call" | custom-call | flops 10000000 | bytes 30000 | tf_op jit(solution)/shard_map/dequant/pallas_call | solution.py:124
  9.2 0.8 %dattn.2 = (bf16[128,512]{1,0:T(8,128)(2,1)S(1)}, bf16[128,512]{1,0:T(8,128)(2,1)S(1)}) custom-call(bf16[128,2048]{1,0:T(8,128)(2,1)S(1)} %copy-done.2, bf16[128,2048]{1,0:T(8,128)(2,1)S(1)} %collective-permute-done.6.refs_1_, bf16[2048,512]{1,0:T(8,128)(2,1)S(1)} %dequant.1.refs_2_), custom_call_target="tpu_custom_call" | custom-call | flops 10000000 | bytes 30000 | tf_op jit(solution)/shard_map/dattn/pallas_call | solution.py:147
  10.1 3.5 %conv_near.1.near = bf16[3,4,224,128]{3,2,1,0:T(8,128)(2,1)S(1)} custom-call(f32[31,3,4,128]{3,2,1,0:T(4,128)S(1)} %copy-done, bf16[3,4,128,128]{3,2,1,0:T(8,128)(2,1)S(1)} %get-tuple-element.108.refs_0_, bf16[3,4,128,128]{3,2,1,0:T(8,128)(2,1)S(1)} %collective-permute-done.5.refs_1_), custom_call_target="tpu_custom_call" | custom-call | flops 10000000 | bytes 30000 | tf_op jit(solution)/shard_map/conv_near/pallas_call | solution.py:209
  13.6 2.3 %collective-permute-done.4.refs_0_ = bf16[128,2048]{1,0:T(8,128)(2,1)S(1)} collective-permute-done((bf16[128,2048]{1,0:T(8,128)(2,1)}, bf16[128,2048]{1,0:T(8,128)(2,1)S(1)}, u32[]{:S(2)}, u32[]{:S(2)}) %collective-permute-start.4) | collective-permute-done | bytes 524320 | tf_op jit(solution)/shard_map/ppermute | solution.py:442
  15.9 4.2 %collective-permute-done.2.refs_2_ = bf16[3,2,128,128]{3,2,1,0:T(8,128)(2,1)S(1)} collective-permute-done((bf16[3,2,128,128]{3,2,1,0:T(8,128)(2,1)S(1)}, bf16[3,2,128,128]{3,2,1,0:T(8,128)(2,1)S(1)}, u32[]{:S(2)}, u32[]{:S(2)}) %collective-permute-start.2) | collective-permute-done | bytes 196640 | tf_op jit(solution)/shard_map/ppermute | solution.py:442
  20.1 2.6 %collective-permute-done.3.refs_3_ = bf16[3,2,128,128]{3,2,1,0:T(8,128)(2,1)S(1)} collective-permute-done((bf16[3,2,128,128]{3,2,1,0:T(8,128)(2,1)S(1)}, bf16[3,2,128,128]{3,2,1,0:T(8,128)(2,1)S(1)}, u32[]{:S(2)}, u32[]{:S(2)}) %collective-permute-start.3) | collective-permute-done | bytes 196640 | tf_op jit(solution)/shard_map/ppermute | solution.py:442
  23.4 1.7 %collective-permute-start = (bf16[3,2,128,128]{3,2,1,0:T(8,128)(2,1)S(1)}, bf16[3,2,128,128]{3,2,1,0:T(8,128)(2,1)S(1)}, u32[]{:S(2)}, u32[]{:S(2)}) collective-permute-start(bf16[3,2,128,128]{3,2,1,0:T(8,128)(2,1)S(1)} %get-tuple-element.95), channel_id=1, source_target_pairs={{0,2},{1,3},{2,0},{3,1},{4,6},{5,7},{6,4},{7,5},{8,10},{9,11},{10,... | collective-permute-start | bytes 589832 | tf_op jit(solution)/shard_map/ppermute | solution.py:442
  25.3 1.5 %collective-permute-start.9 = (bf16[2,352,128]{2,1,0:T(8,128)(2,1)S(1)}, bf16[2,352,128]{2,1,0:T(8,128)(2,1)S(1)}, u32[]{:S(2)}, u32[]{:S(2)}) collective-permute-start(bf16[2,352,128]{2,1,0:T(8,128)(2,1)S(1)} %tail.2), channel_id=1, source_target_pairs={{0,4},{4,8},{8,12},{12,16},{16,20},{20,24},{24,28},{28,0},{1,5},{5... | collective-permute-start | bytes 540680 | tf_op jit(solution)/shard_map/ppermute | solution.py:448
  26.9 2.1 %conv_far.2 = (bf16[3,2,224,128]{3,2,1,0:T(8,128)(2,1)S(1)}, bf16[3,2,32,128]{3,2,1,0:T(8,128)(2,1)S(1)}, bf16[3,2,32,128]{3,2,1,0:T(8,128)(2,1)S(1)}) custom-call(f32[31,3,4,128]{3,2,1,0:T(4,128)S(1)} %copy-done, bf16[3,4,128,128]{3,2,1,0:T(8,128)(2,1)S(1)} %get-tuple-element.108.refs_0_, bf16[3,4,128,128]{3,2,1,0:T(8,128)(2,1)S(1)} %collective-permute-done.5.refs_1_, ...), custom_call_target="tpu_custom_call" | custom-call | flops 10000000 | bytes 30000 | tf_op jit(solution)/shard_map/conv_far/pallas_call | solution.py:255
  29.0 0.8 %dattn.3 = (bf16[128,512]{1,0:T(8,128)(2,1)S(1)}, bf16[128,512]{1,0:T(8,128)(2,1)S(1)}) custom-call(bf16[128,2048]{1,0:T(8,128)(2,1)S(1)} %collective-permute-done.4.refs_0_, bf16[128,2048]{1,0:T(8,128)(2,1)S(1)} %collective-permute-done.7.refs_1_, bf16[2048,512]{1,0:T(8,128)(2,1)S(1)} %dequant.1.refs_2_), custom_call_target="tpu_custom_call" | custom-call | flops 10000000 | bytes 30000 | tf_op jit(solution)/shard_map/dattn/pallas_call | solution.py:147
  29.8 1.4 %collective-permute-done.refs_2_ = bf16[3,2,128,128]{3,2,1,0:T(8,128)(2,1)S(1)} collective-permute-done((bf16[3,2,128,128]{3,2,1,0:T(8,128)(2,1)S(1)}, bf16[3,2,128,128]{3,2,1,0:T(8,128)(2,1)S(1)}, u32[]{:S(2)}, u32[]{:S(2)}) %collective-permute-start) | collective-permute-done | bytes 196640 | tf_op jit(solution)/shard_map/ppermute | solution.py:442
  31.1 2.5 %collective-permute-done.1.refs_3_ = bf16[3,2,128,128]{3,2,1,0:T(8,128)(2,1)S(1)} collective-permute-done((bf16[3,2,128,128]{3,2,1,0:T(8,128)(2,1)S(1)}, bf16[3,2,128,128]{3,2,1,0:T(8,128)(2,1)S(1)}, u32[]{:S(2)}, u32[]{:S(2)}) %collective-permute-start.1) | collective-permute-done | bytes 196640 | tf_op jit(solution)/shard_map/ppermute | solution.py:442
  33.8 1.5 %collective-permute-start.8 = (bf16[2,352,128]{2,1,0:T(8,128)(2,1)S(1)}, bf16[2,352,128]{2,1,0:T(8,128)(2,1)S(1)}, u32[]{:S(2)}, u32[]{:S(2)}) collective-permute-start(bf16[2,352,128]{2,1,0:T(8,128)(2,1)S(1)} %tail.3), channel_id=1, source_target_pairs={{0,4},{4,8},{8,12},{12,16},{16,20},{20,24},{24,28},{28,0},{1,5},{5... | collective-permute-start | bytes 540680 | tf_op jit(solution)/shard_map/ppermute | solution.py:448
  35.4 2.1 %conv_far.3 = (bf16[3,2,224,128]{3,2,1,0:T(8,128)(2,1)S(1)}, bf16[3,2,32,128]{3,2,1,0:T(8,128)(2,1)S(1)}, bf16[3,2,32,128]{3,2,1,0:T(8,128)(2,1)S(1)}) custom-call(f32[31,3,4,128]{3,2,1,0:T(4,128)S(1)} %copy-done, bf16[3,4,128,128]{3,2,1,0:T(8,128)(2,1)S(1)} %get-tuple-element.108.refs_0_, bf16[3,4,128,128]{3,2,1,0:T(8,128)(2,1)S(1)} %collective-permute-done.5.refs_1_, ...), custom_call_target="tpu_custom_call" | custom-call | flops 10000000 | bytes 30000 | tf_op jit(solution)/shard_map/conv_far/pallas_call | solution.py:255
  37.5 3.5 %attention.2 = (f32[3,2,640,128]{3,2,1,0:T(8,128)S(1)}, bf16[2,352,128]{2,1,0:T(8,128)(2,1)S(1)}) custom-call(s32[16]{0:T(128)S(1)} %copy-done.4, s32[8]{0:T(128)S(1)} %copy-done.5, bf16[3,4,224,128]{3,2,1,0:T(8,128)(2,1)S(1)} %conv_near.1.near, bf16[3,2,224,128]{3,2,1,0:T(8,128)(2,1)S(1)} %get-tuple-element.145.far, ...), custom_call_target="tpu_custom_call" | custom-call | flops 10000000 | bytes 30000 | tf_op jit(solution)/shard_map/attention/pallas_call | solution.py:358
  41.0 2.9 %collective-permute-done.8.halo = bf16[2,352,128]{2,1,0:T(8,128)(2,1)S(1)} collective-permute-done((bf16[2,352,128]{2,1,0:T(8,128)(2,1)S(1)}, bf16[2,352,128]{2,1,0:T(8,128)(2,1)S(1)}, u32[]{:S(2)}, u32[]{:S(2)}) %collective-permute-start.8) | collective-permute-done | bytes 180256 | tf_op jit(solution)/shard_map/ppermute | solution.py:448
  43.9 1.7 %collective-permute-start.10 = (bf16[2,352,128]{2,1,0:T(8,128)(2,1)S(1)}, bf16[2,352,128]{2,1,0:T(8,128)(2,1)S(1)}, u32[]{:S(2)}, u32[]{:S(2)}) collective-permute-start(bf16[2,352,128]{2,1,0:T(8,128)(2,1)S(1)} %get-tuple-element.156), channel_id=1, source_target_pairs={{0,28},{4,0},{8,4},{12,8},{16,12},{20,16},{24,20},{28,24},{1,29},{... | collective-permute-start | bytes 540680 | tf_op jit(solution)/shard_map/ppermute | solution.py:448
  45.7 3.5 %attention.3 = (f32[3,2,640,128]{3,2,1,0:T(8,128)S(1)}, bf16[2,352,128]{2,1,0:T(8,128)(2,1)S(1)}) custom-call(s32[16]{0:T(128)S(1)} %copy-done.4, s32[8]{0:T(128)S(1)} %copy-done.5, bf16[3,4,224,128]{3,2,1,0:T(8,128)(2,1)S(1)} %conv_near.1.near, bf16[3,2,224,128]{3,2,1,0:T(8,128)(2,1)S(1)} %get-tuple-element.157.far, ...), custom_call_target="tpu_custom_call" | custom-call | flops 10000000 | bytes 30000 | tf_op jit(solution)/shard_map/attention/pallas_call | solution.py:358
  49.2 1.5 %collective-permute-start.13 = (bf16[2,352,128]{2,1,0:T(8,128)(2,1)S(1)}, bf16[2,352,128]{2,1,0:T(8,128)(2,1)S(1)}, u32[]{:S(2)}, u32[]{:S(2)}) collective-permute-start(bf16[2,352,128]{2,1,0:T(8,128)(2,1)S(1)} %get-tuple-element.172), channel_id=1, source_target_pairs={{0,28},{4,0},{8,4},{12,8},{16,12},{20,16},{24,20},{28,24},{1,29},{... | collective-permute-start | bytes 540680 | tf_op jit(solution)/shard_map/ppermute | solution.py:448
  50.7 3.7 %finish.2 = (bf16[3,2,128,128]{3,2,1,0:T(8,128)(2,1)S(1)}, bf16[3,2,128,128]{3,2,1,0:T(8,128)(2,1)S(1)}, bf16[3,2,128,128]{3,2,1,0:T(8,128)(2,1)S(1)}, bf16[3,2,128,128]{3,2,1,0:T(8,128)(2,1)S(1)}) custom-call(f32[3,2,640,128]{3,2,1,0:T(8,128)S(1)} %get-tuple-element.162.totals, bf16[2,352,128]{2,1,0:T(8,128)(2,1)S(1)} %collective-permute-done.10.carry, ...), custom_call_target="tpu_custom_call" | custom-call | flops 4000000000 | bytes 12000000 | tf_op jit(solution)/shard_map/finish/pallas_call | solution.py:421
  54.5 1.6 %collective-permute-start.12 = (bf16[3,2,128,128]{3,2,1,0:T(8,128)(2,1)S(1)}, bf16[3,2,128,128]{3,2,1,0:T(8,128)(2,1)S(1)}, u32[]{:S(2)}, u32[]{:S(2)}) collective-permute-start(bf16[3,2,128,128]{3,2,1,0:T(8,128)(2,1)S(1)} %get-tuple-element.170), channel_id=1, source_target_pairs={{0,2},{1,3},{2,0},{3,1},{4,6},{5,7},{6,4},{7,5},{8,10},{9,11},{10,... | collective-permute-start | bytes 589832 | tf_op jit(solution)/shard_map/ppermute | solution.py:442
  56.4 3.8 %finish.3 = (bf16[3,2,128,128]{3,2,1,0:T(8,128)(2,1)S(1)}, bf16[3,2,128,128]{3,2,1,0:T(8,128)(2,1)S(1)}, bf16[3,2,128,128]{3,2,1,0:T(8,128)(2,1)S(1)}, bf16[3,2,128,128]{3,2,1,0:T(8,128)(2,1)S(1)}) custom-call(f32[3,2,640,128]{3,2,1,0:T(8,128)S(1)} %get-tuple-element.171.totals, bf16[2,352,128]{2,1,0:T(8,128)(2,1)S(1)} %collective-permute-done.13.carry, ...), custom_call_target="tpu_custom_call" | custom-call | flops 4000000000 | bytes 12000000 | tf_op jit(solution)/shard_map/finish/pallas_call | solution.py:421
  60.2 2.1 %collective-permute-done.12.refs_2_ = bf16[3,2,128,128]{3,2,1,0:T(8,128)(2,1)S(1)} collective-permute-done((bf16[3,2,128,128]{3,2,1,0:T(8,128)(2,1)S(1)}, bf16[3,2,128,128]{3,2,1,0:T(8,128)(2,1)S(1)}, u32[]{:S(2)}, u32[]{:S(2)}) %collective-permute-start.12) | collective-permute-done | bytes 196640 | tf_op jit(solution)/shard_map/ppermute | solution.py:442
  62.3 1.5 %collective-permute-start.16 = (bf16[3,2,128,128]{3,2,1,0:T(8,128)(2,1)S(1)}, bf16[3,2,128,128]{3,2,1,0:T(8,128)(2,1)S(1)}, u32[]{:S(2)}, u32[]{:S(2)}) collective-permute-start(bf16[3,2,128,128]{3,2,1,0:T(8,128)(2,1)S(1)} %get-tuple-element.183), channel_id=1, source_target_pairs={{0,2},{1,3},{2,0},{3,1},{4,6},{5,7},{6,4},{7,5},{8,10},{9,11},{10,... | collective-permute-start | bytes 589832 | tf_op jit(solution)/shard_map/ppermute | solution.py:442
  64.1 1.4 %collective-permute-done.14.refs_3_ = bf16[3,2,128,128]{3,2,1,0:T(8,128)(2,1)S(1)} collective-permute-done((bf16[3,2,128,128]{3,2,1,0:T(8,128)(2,1)S(1)}, bf16[3,2,128,128]{3,2,1,0:T(8,128)(2,1)S(1)}, u32[]{:S(2)}, u32[]{:S(2)}) %collective-permute-start.14) | collective-permute-done | bytes 196640 | tf_op jit(solution)/shard_map/ppermute | solution.py:442
  65.6 5.1 %collective-permute-done.16.refs_6_ = bf16[3,2,128,128]{3,2,1,0:T(8,128)(2,1)S(1)} collective-permute-done((bf16[3,2,128,128]{3,2,1,0:T(8,128)(2,1)S(1)}, bf16[3,2,128,128]{3,2,1,0:T(8,128)(2,1)S(1)}, u32[]{:S(2)}, u32[]{:S(2)}) %collective-permute-start.16) | collective-permute-done | bytes 196640 | tf_op jit(solution)/shard_map/ppermute | solution.py:442
  70.7 3.3 %collective-permute-done.17.refs_7_ = bf16[3,2,128,128]{3,2,1,0:T(8,128)(2,1)S(1)} collective-permute-done((bf16[3,2,128,128]{3,2,1,0:T(8,128)(2,1)S(1)}, bf16[3,2,128,128]{3,2,1,0:T(8,128)(2,1)S(1)}, u32[]{:S(2)}, u32[]{:S(2)}) %collective-permute-start.17) | collective-permute-done | bytes 196640 | tf_op jit(solution)/shard_map/ppermute | solution.py:442
  74.0 2.0 %unpack.1 = bf16[128,3,16,128]{3,2,1,0:T(8,128)(2,1)} custom-call(bf16[3,2,128,128]{3,2,1,0:T(8,128)(2,1)S(1)} %get-tuple-element.177.refs_0_, bf16[3,2,128,128]{3,2,1,0:T(8,128)(2,1)S(1)} %collective-permute-done.11.refs_1_, bf16[3,2,128,128]{3,2,1,0:T(8,128)(2,1)S(1)} %collective-permute-done.12.refs_2_, ...), custom_call_target="tpu_custom_call" | custom-call | flops 2000000000 | bytes 6000000 | tf_op jit(solution)/shard_map/unpack/pallas_call | solution.py:97
  (32 shorter events, 2.5 us)
Async XLA Ops:
  0.0 7.4 %copy-start.1 = (bf16[512,2048]{1,0:T(8,128)(2,1)S(1)}, bf16[512,2048]{1,0:T(8,128)(2,1)}, u32[]{:S(2)}) copy-start(bf16[512,2048]{1,0:T(8,128)(2,1)} %values) | copy-start | bytes 6291460
  0.0 7.4 %copy-start.3 = (f32[16,16]{1,0:T(8,128)S(1)}, f32[16,16]{1,0:T(8,128)}, u32[]{:S(2)}) copy-start(f32[16,16]{1,0:T(8,128)} %scales.1) | copy-start | bytes 3076
  0.0 15.9 %collective-permute-start.4 = (bf16[128,2048]{1,0:T(8,128)(2,1)}, bf16[128,2048]{1,0:T(8,128)(2,1)S(1)}, u32[]{:S(2)}, u32[]{:S(2)}) collective-permute-start(bf16[128,2048]{1,0:T(8,128)(2,1)} %refs_0_), channel_id=1, source_target_pairs={{0,2},{1,3},{2,0},{3,1},{4,6},{5,7},{6,4},{7,5},{8,10},{9,11},{10,... | collective-permute-start | bytes 1572872 | tf_op jit(solution)/shard_map/ppermute | solution.py:442
  3.0 4.4 %collective-permute-start.6 = (bf16[128,2048]{1,0:T(8,128)(2,1)}, bf16[128,2048]{1,0:T(8,128)(2,1)S(1)}, u32[]{:S(2)}, u32[]{:S(2)}) collective-permute-start(bf16[128,2048]{1,0:T(8,128)(2,1)} %refs_0_), channel_id=1, source_target_pairs={{0,1},{1,0},{2,3},{3,2},{4,5},{5,4},{6,7},{7,6},{8,9},{9,8},{10,11... | collective-permute-start | bytes 1572872 | tf_op jit(solution)/shard_map/ppermute | solution.py:442
  3.0 1.4 %copy-start.6 = (bf16[128,3,16,128]{3,2,1,0:T(8,128)(2,1)S(1)}, bf16[128,3,16,128]{3,2,1,0:T(8,128)(2,1)}, u32[]{:S(2)}) copy-start(bf16[128,3,16,128]{3,2,1,0:T(8,128)(2,1)} %src.1) | copy-start | bytes 4718596
  5.4 2.0 %collective-permute-start.5 = (bf16[3,4,128,128]{3,2,1,0:T(8,128)(2,1)S(1)}, bf16[3,4,128,128]{3,2,1,0:T(8,128)(2,1)S(1)}, u32[]{:S(2)}, u32[]{:S(2)}) collective-permute-start(bf16[3,4,128,128]{3,2,1,0:T(8,128)(2,1)S(1)} %get-tuple-element.100), channel_id=1, source_target_pairs={{0,1},{1,0},{2,3},{3,2},{4,5},{5,4},{6,7},{7,6},{8,9},{9,8},{10,11... | collective-permute-start | bytes 1179656 | tf_op jit(solution)/shard_map/ppermute | solution.py:442
  6.0 14.2 %collective-permute-start.2 = (bf16[3,2,128,128]{3,2,1,0:T(8,128)(2,1)S(1)}, bf16[3,2,128,128]{3,2,1,0:T(8,128)(2,1)S(1)}, u32[]{:S(2)}, u32[]{:S(2)}) collective-permute-start(bf16[3,2,128,128]{3,2,1,0:T(8,128)(2,1)S(1)} %get-tuple-element.97), channel_id=1, source_target_pairs={{0,2},{1,3},{2,0},{3,1},{4,6},{5,7},{6,4},{7,5},{8,10},{9,11},{10,... | collective-permute-start | bytes 589832 | tf_op jit(solution)/shard_map/ppermute | solution.py:442
  6.1 16.7 %collective-permute-start.3 = (bf16[3,2,128,128]{3,2,1,0:T(8,128)(2,1)S(1)}, bf16[3,2,128,128]{3,2,1,0:T(8,128)(2,1)S(1)}, u32[]{:S(2)}, u32[]{:S(2)}) collective-permute-start(bf16[3,2,128,128]{3,2,1,0:T(8,128)(2,1)S(1)} %get-tuple-element.98), channel_id=1, source_target_pairs={{0,3},{1,2},{2,1},{3,0},{4,7},{5,6},{6,5},{7,4},{8,11},{9,10},{10,... | collective-permute-start | bytes 589832 | tf_op jit(solution)/shard_map/ppermute | solution.py:442
  7.4 1.8 %copy-start.2 = (bf16[128,2048]{1,0:T(8,128)(2,1)S(1)}, bf16[128,2048]{1,0:T(8,128)(2,1)}, u32[]{:S(2)}) copy-start(bf16[128,2048]{1,0:T(8,128)(2,1)} %refs_0_) | copy-start | bytes 1572868
  9.2 0.9 %copy-start = (f32[31,3,4,128]{3,2,1,0:T(4,128)S(1)}, f32[31,3,4,128]{3,2,1,0:T(4,128)}, u32[]{:S(2)}) copy-start(f32[31,3,4,128]{3,2,1,0:T(4,128)} %taps.13) | copy-start | bytes 571396
  22.8 6.2 %collective-permute-start.7 = (bf16[128,2048]{1,0:T(8,128)(2,1)S(1)}, bf16[128,2048]{1,0:T(8,128)(2,1)S(1)}, u32[]{:S(2)}, u32[]{:S(2)}) collective-permute-start(bf16[128,2048]{1,0:T(8,128)(2,1)S(1)} %collective-permute-done.4.refs_0_), channel_id=1, source_target_pairs={{0,1},{1,0},{2,3},{3,2},{4,5},{5,4},{6,7},{7,6},{8,9},{9,8},{10,11... | collective-permute-start | bytes 1572872 | tf_op jit(solution)/shard_map/ppermute | solution.py:442
  23.4 7.8 %collective-permute-start = (bf16[3,2,128,128]{3,2,1,0:T(8,128)(2,1)S(1)}, bf16[3,2,128,128]{3,2,1,0:T(8,128)(2,1)S(1)}, u32[]{:S(2)}, u32[]{:S(2)}) collective-permute-start(bf16[3,2,128,128]{3,2,1,0:T(8,128)(2,1)S(1)} %get-tuple-element.95), channel_id=1, source_target_pairs={{0,2},{1,3},{2,0},{3,1},{4,6},{5,7},{6,4},{7,5},{8,10},{9,11},{10,... | collective-permute-start | bytes 589832 | tf_op jit(solution)/shard_map/ppermute | solution.py:442
  25.1 8.5 %collective-permute-start.1 = (bf16[3,2,128,128]{3,2,1,0:T(8,128)(2,1)S(1)}, bf16[3,2,128,128]{3,2,1,0:T(8,128)(2,1)S(1)}, u32[]{:S(2)}, u32[]{:S(2)}) collective-permute-start(bf16[3,2,128,128]{3,2,1,0:T(8,128)(2,1)S(1)} %get-tuple-element.96), channel_id=1, source_target_pairs={{0,3},{1,2},{2,1},{3,0},{4,7},{5,6},{6,5},{7,4},{8,11},{9,10},{10,... | collective-permute-start | bytes 589832 | tf_op jit(solution)/shard_map/ppermute | solution.py:442
  25.3 12.2 %collective-permute-start.9 = (bf16[2,352,128]{2,1,0:T(8,128)(2,1)S(1)}, bf16[2,352,128]{2,1,0:T(8,128)(2,1)S(1)}, u32[]{:S(2)}, u32[]{:S(2)}) collective-permute-start(bf16[2,352,128]{2,1,0:T(8,128)(2,1)S(1)} %tail.2), channel_id=1, source_target_pairs={{0,4},{4,8},{8,12},{12,16},{16,20},{20,24},{24,28},{28,0},{1,5},{5... | collective-permute-start | bytes 540680 | tf_op jit(solution)/shard_map/ppermute | solution.py:448
  29.7 7.8 %copy-start.4 = (s32[16]{0:T(128)S(1)}, s32[16]{0:T(128)}, u32[]{:S(2)}) copy-start(s32[16]{0:T(128)} %window.3) | copy-start | bytes 196
  29.7 7.7 %copy-start.5 = (s32[8]{0:T(128)S(1)}, s32[8]{0:T(128)}, u32[]{:S(2)}) copy-start(s32[8]{0:T(128)} %offsets.3) | copy-start | bytes 100
  33.8 10.1 %collective-permute-start.8 = (bf16[2,352,128]{2,1,0:T(8,128)(2,1)S(1)}, bf16[2,352,128]{2,1,0:T(8,128)(2,1)S(1)}, u32[]{:S(2)}, u32[]{:S(2)}) collective-permute-start(bf16[2,352,128]{2,1,0:T(8,128)(2,1)S(1)} %tail.3), channel_id=1, source_target_pairs={{0,4},{4,8},{8,12},{12,16},{16,20},{20,24},{24,28},{28,0},{1,5},{5... | collective-permute-start | bytes 540680 | tf_op jit(solution)/shard_map/ppermute | solution.py:448
  43.9 6.8 %collective-permute-start.10 = (bf16[2,352,128]{2,1,0:T(8,128)(2,1)S(1)}, bf16[2,352,128]{2,1,0:T(8,128)(2,1)S(1)}, u32[]{:S(2)}, u32[]{:S(2)}) collective-permute-start(bf16[2,352,128]{2,1,0:T(8,128)(2,1)S(1)} %get-tuple-element.156), channel_id=1, source_target_pairs={{0,28},{4,0},{8,4},{12,8},{16,12},{20,16},{24,20},{28,24},{1,29},{... | collective-permute-start | bytes 540680 | tf_op jit(solution)/shard_map/ppermute | solution.py:448
  49.2 7.2 %collective-permute-start.13 = (bf16[2,352,128]{2,1,0:T(8,128)(2,1)S(1)}, bf16[2,352,128]{2,1,0:T(8,128)(2,1)S(1)}, u32[]{:S(2)}, u32[]{:S(2)}) collective-permute-start(bf16[2,352,128]{2,1,0:T(8,128)(2,1)S(1)} %get-tuple-element.172), channel_id=1, source_target_pairs={{0,28},{4,0},{8,4},{12,8},{16,12},{20,16},{24,20},{28,24},{1,29},{... | collective-permute-start | bytes 540680 | tf_op jit(solution)/shard_map/ppermute | solution.py:448
  54.4 5.7 %collective-permute-start.11 = (bf16[3,2,128,128]{3,2,1,0:T(8,128)(2,1)S(1)}, bf16[3,2,128,128]{3,2,1,0:T(8,128)(2,1)S(1)}, u32[]{:S(2)}, u32[]{:S(2)}) collective-permute-start(bf16[3,2,128,128]{3,2,1,0:T(8,128)(2,1)S(1)} %get-tuple-element.169), channel_id=1, source_target_pairs={{0,1},{1,0},{2,3},{3,2},{4,5},{5,4},{6,7},{7,6},{8,9},{9,8},{10,11... | collective-permute-start | bytes 589832 | tf_op jit(solution)/shard_map/ppermute | solution.py:442
  54.5 7.8 %collective-permute-start.12 = (bf16[3,2,128,128]{3,2,1,0:T(8,128)(2,1)S(1)}, bf16[3,2,128,128]{3,2,1,0:T(8,128)(2,1)S(1)}, u32[]{:S(2)}, u32[]{:S(2)}) collective-permute-start(bf16[3,2,128,128]{3,2,1,0:T(8,128)(2,1)S(1)} %get-tuple-element.170), channel_id=1, source_target_pairs={{0,2},{1,3},{2,0},{3,1},{4,6},{5,7},{6,4},{7,5},{8,10},{9,11},{10,... | collective-permute-start | bytes 589832 | tf_op jit(solution)/shard_map/ppermute | solution.py:442
  56.1 9.5 %collective-permute-start.14 = (bf16[3,2,128,128]{3,2,1,0:T(8,128)(2,1)S(1)}, bf16[3,2,128,128]{3,2,1,0:T(8,128)(2,1)S(1)}, u32[]{:S(2)}, u32[]{:S(2)}) collective-permute-start(bf16[3,2,128,128]{3,2,1,0:T(8,128)(2,1)S(1)} %get-tuple-element.180), channel_id=1, source_target_pairs={{0,3},{1,2},{2,1},{3,0},{4,7},{5,6},{6,5},{7,4},{8,11},{9,10},{10,... | collective-permute-start | bytes 589832 | tf_op jit(solution)/shard_map/ppermute | solution.py:442
  62.3 3.3 %collective-permute-start.15 = (bf16[3,2,128,128]{3,2,1,0:T(8,128)(2,1)S(1)}, bf16[3,2,128,128]{3,2,1,0:T(8,128)(2,1)S(1)}, u32[]{:S(2)}, u32[]{:S(2)}) collective-permute-start(bf16[3,2,128,128]{3,2,1,0:T(8,128)(2,1)S(1)} %get-tuple-element.182), channel_id=1, source_target_pairs={{0,1},{1,0},{2,3},{3,2},{4,5},{5,4},{6,7},{7,6},{8,9},{9,8},{10,11... | collective-permute-start | bytes 589832 | tf_op jit(solution)/shard_map/ppermute | solution.py:442
  62.3 8.4 %collective-permute-start.16 = (bf16[3,2,128,128]{3,2,1,0:T(8,128)(2,1)S(1)}, bf16[3,2,128,128]{3,2,1,0:T(8,128)(2,1)S(1)}, u32[]{:S(2)}, u32[]{:S(2)}) collective-permute-start(bf16[3,2,128,128]{3,2,1,0:T(8,128)(2,1)S(1)} %get-tuple-element.183), channel_id=1, source_target_pairs={{0,2},{1,3},{2,0},{3,1},{4,6},{5,7},{6,4},{7,5},{8,10},{9,11},{10,... | collective-permute-start | bytes 589832 | tf_op jit(solution)/shard_map/ppermute | solution.py:442
  63.8 10.2 %collective-permute-start.17 = (bf16[3,2,128,128]{3,2,1,0:T(8,128)(2,1)S(1)}, bf16[3,2,128,128]{3,2,1,0:T(8,128)(2,1)S(1)}, u32[]{:S(2)}, u32[]{:S(2)}) collective-permute-start(bf16[3,2,128,128]{3,2,1,0:T(8,128)(2,1)S(1)} %get-tuple-element.184), channel_id=1, source_target_pairs={{0,3},{1,2},{2,1},{3,0},{4,7},{5,6},{6,5},{7,4},{8,11},{9,10},{10,... | collective-permute-start | bytes 589832 | tf_op jit(solution)/shard_map/ppermute | solution.py:442
